TPU v7x, 32 devices: a whole 2x2x4 slice. The times are simulated.
32 devices in a mesh: img: 8 (over z, y), cap: 4 (over x, core).
Axes of the slice: x: 2, y: 2, z: 4, core: 2. Of those that a mesh axis runs over, the one named last changes fastest.
Arguments:
- pair_list: int32 [512, 2], replicated, may hold values from 0 to 127, as said below
- verify_order: int32 [512], P(('img', 'cap')), may hold values from 0 to 511, as said below
- image_slot: int32 [64], replicated, may hold values from 0 to 63, as said below
- caption_slot: int32 [128], replicated, may hold values from 0 to 127, as said below
- images: bfloat16 [64, 197, 768], P('img'), may hold values from -6 to 6
- captions: bfloat16 [128, 32, 768], P('cap'), may hold values from -6 to 6
- query_weight: bfloat16 [768, 768], replicated, may hold values from -1 to 1
- key_weight: bfloat16 [768, 768], replicated, may hold values from -1 to 1
- value_weight: bfloat16 [768, 768], replicated, may hold values from -0.21875 to 0.21875
- out_weight: bfloat16 [768, 768], replicated, may hold values from -0.4375 to 0.4375
- gain_attn: float32 [768], replicated, may hold values from 0.5 to 1.5
- in_weight: bfloat16 [768, 3072], replicated, may hold values from -0.21875 to 0.21875
- back_weight: bfloat16 [3072, 768], replicated, may hold values from -0.109375 to 0.109375
- gain_ffn: float32 [768], replicated, may hold values from 0.5 to 1.5
- match_weight: bfloat16 [768, 2], replicated, may hold values from -0.21875 to 0.21875
Outputs:
- merged: bfloat16 [512, 32, 768], P(('img', 'cap'))
- match_logits: float32 [512, 2], P(('img', 'cap'))
Inputs may be any that keep to these rules, and one draw needn't show every extreme that they name: Each image id and caption id of pair_list lies in range; image_slot is a permutation. caption_slot is a permutation. verify_order is a permutation. Of the 16 rows verified by one device, at most 2 have images stored on one index of img and at most 4 have captions stored on one index of cap; every device has some index reaching each bound. `pair_list`: column 0 holds image ids, column 1 caption ids.
All inputs are finite; a program needn't handle non-finite values.
Results may differ from a plain program's by a relative error of at most 0.018.
Values may be sent and summed in bfloat16 or wider, within the bound.
No kernel may reach another device: no remote copies, remote signals or barrier semaphores. Data moves between devices by JAX's collectives and lax.ppermute only.
A program may use at most 192 MiB of HBM per device.

v0:
```python
import functools

import jax
import jax.numpy as jnp
from jax import lax
from jax.experimental import pallas as pl
from jax.experimental.pallas import tpu as pltpu
from jax.sharding import PartitionSpec as P

HEADS = 12
IMG_MOST = 2
CORES = 2
PACK = 65536
KEY_PAD = 256
LANES = 128
GROUP = 256
F32 = jnp.float32
BF16 = jnp.bfloat16

SMEM = pl.BlockSpec(memory_space=pltpu.SMEM)
VMEM = pl.BlockSpec(memory_space=pltpu.VMEM)


def params(mib):
    return pltpu.CompilerParams(vmem_limit_bytes=mib * 1024 * 1024)


def norm_rows(hidden, gain):
    row_mean = jnp.mean(hidden, axis=-1, keepdims=True)
    centred = hidden - row_mean
    row_var = jnp.mean(centred * centred, axis=-1, keepdims=True)
    return centred * lax.rsqrt(row_var + 1e-06) * gain


def table_kernel(image_local, caption_count, pairs, order, image_slot, caption_slot, table, place, count):
    img_count = count.shape[0]
    me = lax.axis_index("img")
    for owner in range(img_count):
        count[owner] = 0
        for rank in range(IMG_MOST):
            for column in range(caption_count):
                table[owner * caption_count + column, rank] = 0
    for row in range(order.shape[0]):
        pair = order[row]
        image = image_slot[pairs[0, pair]]
        caption = caption_slot[pairs[1, pair]]
        owner = image // image_local
        rank = count[owner]
        count[owner] = rank + 1
        entry = (image - owner * image_local) * PACK + caption
        for column in range(caption_count):
            table[owner * caption_count + column, rank] = entry
        place[row] = jnp.bitwise_xor(owner, me) * IMG_MOST + rank


def make_table(pairs, order, image_slot, caption_slot, image_local, img_count, caption_count):
    return pl.pallas_call(
        functools.partial(table_kernel, image_local, caption_count),
        out_shape=(
            jax.ShapeDtypeStruct((img_count * caption_count, LANES), jnp.int32),
            jax.ShapeDtypeStruct(order.shape, jnp.int32),
        ),
        in_specs=[SMEM] * 4,
        out_specs=(SMEM, SMEM),
        scratch_shapes=[pltpu.SMEM((img_count,), jnp.int32)],
        name="slot_table",
    )(pairs, order, image_slot, caption_slot)


def read_slot(table, cap_count, column, distance, rank, caption_local):
    verifier = jnp.bitwise_xor(lax.axis_index("img"), distance)
    entry = table[verifier * cap_count + column, rank]
    caption = jnp.bitwise_and(entry, PACK - 1)
    owner = caption // caption_local
    return lax.shift_right_logical(entry, 16), owner, caption - owner * caption_local


def pick_kernel(step, cap_count, chunks, table, own, sibling, *outs):
    mine = lax.axis_index("cap")
    asker = jnp.bitwise_xor(mine, step * CORES)
    for chunk, out in zip(chunks, outs):
        for index, distance in enumerate(chunk):
            for rank in range(IMG_MOST):
                _, owner, local = read_slot(table, cap_count, asker, distance, rank, own.shape[0])
                near = owner == jnp.bitwise_xor(mine, 1)

                @pl.when(near)
                def _():
                    out[index * IMG_MOST + rank] = sibling[local]

                @pl.when(jnp.logical_not(near))
                def _():
                    out[index * IMG_MOST + rank] = own[local]


def pick_blocks(step, cap_count, chunks, table, own, sibling):
    outs = tuple(
        jax.ShapeDtypeStruct((len(chunk) * IMG_MOST,) + own.shape[1:], own.dtype) for chunk in chunks
    )
    return pl.pallas_call(
        functools.partial(pick_kernel, step, cap_count, chunks),
        out_shape=outs,
        in_specs=[SMEM, VMEM, VMEM],
        out_specs=(VMEM,) * len(outs),
        compiler_params=params(8),
        cost_estimate=pl.CostEstimate(flops=0, bytes_accessed=1 << 20, transcendentals=0),
        name="pick_captions",
    )(table, own, sibling)


def project_kernel(images, key_weight, value_weight, keys, values):
    rows = images.shape[1]
    patches = images[0]
    for weight, out in ((key_weight, keys), (value_weight, values)):
        out[0, rows // 16 * 16 :, :] = jnp.zeros((KEY_PAD - rows // 16 * 16, out.shape[2]), BF16)
        out[0, :rows, :] = jnp.dot(patches, weight[...], preferred_element_type=F32).astype(BF16)


def project_images(images, key_weight, value_weight):
    count, rows, width = images.shape
    whole = pl.BlockSpec((width, width), lambda i: (0, 0))
    out = jax.ShapeDtypeStruct((count, KEY_PAD, width), BF16)
    return pl.pallas_call(
        project_kernel,
        out_shape=(out, out),
        grid=(count,),
        in_specs=[pl.BlockSpec((1, rows, width), lambda i: (i, 0, 0)), whole, whole],
        out_specs=(pl.BlockSpec((1, KEY_PAD, width), lambda i: (i, 0, 0)),) * 2,
        compiler_params=params(16),
        cost_estimate=pl.CostEstimate(
            flops=4 * count * KEY_PAD * width * width,
            bytes_accessed=2 * (2 * width * width + count * (rows + 2 * KEY_PAD) * width),
            transcendentals=0,
        ),
        name="project_images",
    )(images, key_weight, value_weight)


def attend_kernel(key_rows, cap_count, far_count, chunk, table, own, sibling, *rest):
    far = rest[:far_count]
    keys, values, query_weight, out_weight, gain = rest[far_count : far_count + 5]
    outs = rest[far_count + 5 : far_count + 5 + len(chunk)]
    rows, query, context = rest[far_count + 5 + len(chunk) :]
    column = lax.axis_index("cap")
    tokens, width = own.shape[1], own.shape[2]
    head_size = width // HEADS
    heads = GROUP // head_size
    pair_count = len(chunk) * IMG_MOST
    images = []
    for pair in range(pair_count):
        image, owner, local = read_slot(
            table, cap_count, column, chunk[pair // IMG_MOST], pair % IMG_MOST, own.shape[0]
        )
        images.append(image)
        apart = jnp.bitwise_xor(owner, column)

        @pl.when(apart == 0)
        def _():
            rows[pair] = own[local]

        @pl.when(apart == 1)
        def _():
            rows[pair] = sibling[local]

        for step in range(far_count):

            @pl.when(apart // CORES == step + 1)
            def _():
                rows[pair] = far[step][pair]

    flat = rows[...].reshape(pair_count * tokens, width)
    query[...] = jnp.dot(flat, query_weight[...], preferred_element_type=F32).astype(BF16)
    lane_head = lax.broadcasted_iota(jnp.int32, (tokens, GROUP), 1) // head_size
    visible = lax.broadcasted_iota(jnp.int32, (heads * tokens, KEY_PAD), 1) < key_rows
    scale = 1.0 / float(head_size) ** 0.5
    spans = [slice(group * GROUP, (group + 1) * GROUP) for group in range(width // GROUP)]

    def score(pair):
        found = []
        for span in spans:
            part = query[pair * tokens : (pair + 1) * tokens, span]
            stacked = jnp.concatenate(
                [jnp.where(lane_head == head, part, jnp.zeros_like(part)) for head in range(heads)],
                axis=0,
            )
            found.append(
                lax.dot_general(
                    stacked,
                    keys[images[pair], :, span],
                    (((1,), (1,)), ((), ())),
                    preferred_element_type=F32,
                )
            )
        return found

    def mix(pair, found):
        for span, scores in zip(spans, found):
            scores = jnp.where(visible, scores * scale, -jnp.inf)
            top = jnp.max(scores, axis=-1, keepdims=True)
            weights = jnp.exp(scores - top)
            share = 1.0 / jnp.sum(weights, axis=-1, keepdims=True)
            probs = (weights * share).astype(BF16)
            mixed = jnp.dot(probs, values[images[pair], :, span], preferred_element_type=F32)
            joined = mixed[:tokens]
            for head in range(1, heads):
                joined = jnp.where(lane_head == head, mixed[head * tokens : (head + 1) * tokens], joined)
            context[pair * tokens : (pair + 1) * tokens, span] = joined.astype(BF16)

    found = score(0)
    for pair in range(pair_count):
        later = score(pair + 1) if pair + 1 < pair_count else None
        mix(pair, found)
        found = later
    hidden = flat.astype(F32) + jnp.dot(context[...], out_weight[...], preferred_element_type=F32)
    hidden = norm_rows(hidden, gain[...]).astype(BF16).reshape(pair_count, tokens, width)
    for index, out in enumerate(outs):
        out[...] = hidden[index * IMG_MOST : (index + 1) * IMG_MOST]


def attend(key_rows, cap_count, chunk, table, own, sibling, far, keys, values, query_weight, out_weight, gain):
    tokens, width = own.shape[1:]
    pair_count = len(chunk) * IMG_MOST
    rows = pair_count * tokens
    return pl.pallas_call(
        functools.partial(attend_kernel, key_rows, cap_count, len(far), chunk),
        out_shape=(jax.ShapeDtypeStruct((IMG_MOST, tokens, width), BF16),) * len(chunk),
        in_specs=[SMEM] + [VMEM] * (7 + len(far)),
        out_specs=(VMEM,) * len(chunk),
        scratch_shapes=[
            pltpu.VMEM((pair_count, tokens, width), BF16),
            pltpu.VMEM((rows, width), BF16),
            pltpu.VMEM((rows, width), BF16),
        ],
        compiler_params=params(16),
        cost_estimate=pl.CostEstimate(
            flops=4 * rows * width * width + 4 * rows * GROUP * KEY_PAD * HEADS,
            bytes_accessed=8 * width * width,
            transcendentals=rows * HEADS * KEY_PAD,
        ),
        name="attend",
    )(table, own, sibling, *far, keys, values, query_weight, out_weight, gain)


TILES = 3


def feed_rows(parts, gain, in_weight, back_weight):
    count, tokens, width = parts[0].shape
    step = in_weight.shape[1] // TILES
    flat = jnp.concatenate([part[...] for part in parts], axis=0).reshape(-1, width)
    total = flat.astype(F32)
    for tile in range(TILES):
        span = slice(tile * step, (tile + 1) * step)
        inner = jnp.dot(flat, in_weight[:, span], preferred_element_type=F32)
        inner = (0.5 * inner * (1.0 + lax.erf(inner * (0.5**0.5)))).astype(BF16)
        total = total + jnp.dot(inner, back_weight[span, :], preferred_element_type=F32)
    return norm_rows(total, gain[...]).astype(BF16).reshape(-1, tokens, width)


def feed_first_kernel(gain, in_weight, back_weight, *rest):
    parts, out = rest[:-1], rest[-1]
    out[...] = feed_rows(parts, gain, in_weight, back_weight)


def feed_last_kernel(first_parts, last_parts, place, gain, match_weight, in_weight, back_weight, earlier, *rest):
    parts = rest[: len(last_parts)]
    merged, logits, done, first = rest[len(last_parts) :]
    slots = len(first_parts) * IMG_MOST
    done[:slots] = earlier[...]
    done[slots:] = feed_rows(parts, gain, in_weight, back_weight)
    for row in range(merged.shape[0]):
        slot = place[row]
        distance = slot // IMG_MOST
        spot = jnp.int32(0)
        for index, listed in enumerate(first_parts + last_parts):
            spot = jnp.where(distance == listed, index, spot)
        block = done[spot * IMG_MOST + slot % IMG_MOST]
        merged[row] = block
        first[row : row + 1, :] = block[0:1, :].astype(F32)
    logits[...] = lax.dot_general(
        match_weight[...], first[...].astype(BF16), (((1,), (1,)), ((), ())), preferred_element_type=F32
    )


def feed_cost(rows, width, inner_width):
    return pl.CostEstimate(
        flops=4 * rows * width * inner_width,
        bytes_accessed=4 * width * inner_width,
        transcendentals=rows * inner_width,
    )


def feed_first(parts, gain, in_weight, back_weight):
    count, tokens, width = parts[0].shape
    slots = len(parts) * count
    return pl.pallas_call(
        feed_first_kernel,
        out_shape=jax.ShapeDtypeStruct((slots, tokens, width), BF16),
        in_specs=[VMEM] * (3 + len(parts)),
        out_specs=VMEM,
        compiler_params=params(16),
        cost_estimate=feed_cost(slots * tokens, width, in_weight.shape[1]),
        name="feed_first",
    )(gain, in_weight, back_weight, *parts)


def feed_last(first_parts, last_parts, place, gain, match_weight, in_weight, back_weight, earlier, parts):
    count, tokens, width = parts[0].shape
    rows = place.shape[0]
    slots = (len(first_parts) + len(last_parts)) * count
    return pl.pallas_call(
        functools.partial(feed_last_kernel, first_parts, last_parts),
        out_shape=(
            jax.ShapeDtypeStruct((rows, tokens, width), BF16),
            jax.ShapeDtypeStruct((match_weight.shape[0], rows), F32),
        ),
        in_specs=[SMEM] + [VMEM] * (5 + len(parts)),
        out_specs=(VMEM, VMEM),
        scratch_shapes=[pltpu.VMEM((slots, tokens, width), BF16), pltpu.VMEM((rows, width), F32)],
        compiler_params=params(16),
        cost_estimate=feed_cost(len(parts) * count * tokens, width, in_weight.shape[1]),
        name="feed_last",
    )(place, gain, match_weight, in_weight, back_weight, earlier, *parts)


def body(
    pair_list,
    verify_order,
    image_slot,
    caption_slot,
    images,
    captions,
    query_weight,
    key_weight,
    value_weight,
    out_weight,
    gain_attn,
    in_weight,
    back_weight,
    gain_ffn,
    match_weight,
):
    img_count = lax.axis_size("img")
    cap_count = lax.axis_size("cap")
    far_steps = range(1, cap_count // CORES)
    half, quarter = img_count // 2, img_count // 4
    chunks = (tuple(range(img_count - 1, half - 1, -1)), tuple(range(half - 1, -1, -1)))
    first_parts = chunks[0][:quarter] + chunks[1][half - quarter :]
    last_parts = chunks[0][quarter:] + chunks[1][: half - quarter]

    def swap(array, axis, distance):
        size = lax.axis_size(axis)
        return lax.ppermute(array, axis, [(peer, peer ^ distance) for peer in range(size)])

    sibling = swap(captions, "cap", 1)
    table, place = make_table(
        pair_list.T, verify_order, image_slot, caption_slot, images.shape[0], img_count, cap_count
    )
    table = lax.all_to_all(table, ("img", "cap"), split_axis=0, concat_axis=0, tiled=True)
    keys, values = project_images(images, key_weight, value_weight)
    far = [[] for _ in chunks]
    for step in far_steps:
        picked = pick_blocks(step, cap_count, chunks, table, captions, sibling)
        for blocks, block in zip(far, picked):
            blocks.append(swap(block, "cap", step * CORES))
    gain_attn = gain_attn.reshape(1, -1)
    gain_ffn = gain_ffn.reshape(1, -1)
    hidden = {}
    for index, chunk in enumerate(chunks):
        blocks = attend(
            images.shape[1],
            cap_count,
            chunk,
            table,
            captions,
            sibling,
            far[index],
            keys,
            values,
            query_weight,
            out_weight,
            gain_attn,
        )
        if index == 0:
            blocks, far = lax.optimization_barrier((blocks, far))
        for distance, block in zip(chunk, blocks):
            hidden[distance] = swap(block, "img", distance) if distance else block
    earlier = feed_first([hidden[part] for part in first_parts], gain_ffn, in_weight, back_weight)
    merged, logits = feed_last(
        first_parts,
        last_parts,
        place,
        gain_ffn,
        match_weight.T,
        in_weight,
        back_weight,
        earlier,
        [hidden[part] for part in last_parts],
    )
    return merged, logits.T


def solution(mesh):
    placed = (
        P(),
        P(("img", "cap")),
        P(),
        P(),
        P("img", None, None),
        P("cap", None, None),
        P(),
        P(),
        P(),
        P(),
        P(),
        P(),
        P(),
        P(),
        P(),
    )
    return jax.shard_map(
        body,
        mesh=mesh,
        in_specs=placed,
        out_specs=(P(("img", "cap"), None, None), P(("img", "cap"), None)),
        check_vma=False,
    )
```

profile of v0, /device:TPU:0, one launch (start us, length us, event | category | flops | bytes accessed | tf_op | source)
XLA Modules:
  0.0 66.4 jit_solution(17992784434946845200)
XLA Ops:
  0.6 0.5 collective-permute-start
  1.1 1.8 %slot_table.1 = (s32[32,128]{1,0:T(8,128)}, s32[16]{0:T(128)}) custom-call(s32[2,512]{1,0:T(2,128)} %bitcast.16, s32[16]{0:T(128)} %order.1, s32[64]{0:T(128)} %image_slot.1, s32[128]{0:T(128)} %caption_slot.1), custom_call_target="tpu_custom_call" | custom-call | tf_op jit(solution)/shard_map/slot_table/pallas_call | solution.py:57
  2.9 7.0 %all-to-all-start = ((s32[32,1,128]{2,1,0:T(1,128)}), s32[32,1,128]{2,1,0:T(1,128)S(1)}, u32[]{:S(2)}, u32[]{:S(2)}) async-start(s32[32,1,128]{2,1,0:T(1,128)} %bitcast.15), calls=%async_computation | async-start | bytes 32768 | tf_op jit(solution)/shard_map/all_to_all | solution.py:359
  9.9 0.0 copy-start.8
  9.9 0.0 copy-start
  9.9 3.7 %copy.19.images = bf16[8,197,768]{2,1,0:T(8,128)(2,1)} copy(bf16[8,197,768]{2,0,1:T(8,128)(2,1)} %param.19) | data formatting | bytes 4841472 | tf_op args[4]
  13.7 0.0 copy-done.8
  13.7 3.3 %all-to-all-done = s32[32,1,128]{2,1,0:T(1,128)S(1)} async-done(((s32[32,1,128]{2,1,0:T(1,128)}), s32[32,1,128]{2,1,0:T(1,128)S(1)}, u32[]{:S(2)}, u32[]{:S(2)}) %all-to-all-start) | async-done | bytes 16416 | tf_op jit(solution)/shard_map/all_to_all | solution.py:359
  17.0 0.0 copy-start.3
  17.0 0.0 collective-permute-done.sibling
  17.0 0.0 copy-done
  17.0 1.1 %pick_captions.1 = (bf16[8,32,768]{2,1,0:T(8,128)(2,1)S(1)}, bf16[8,32,768]{2,1,0:T(8,128)(2,1)S(1)}) custom-call(s32[32,128]{1,0:T(8,128)S(1)} %bitcast.11, bf16[32,32,768]{2,1,0:T(8,128)(2,1)S(1)} %copy-done, bf16[32,32,768]{2,1,0:T(8,128)(2,1)S(1)} %collective-permute-done.sibling), custom_call_target="tpu_custom_call" | custom-call | bytes 1048576 | tf_op jit(solution)/shard_map/pick_captions/pallas_call | solution.py:100
  18.1 0.6 collective-permute-start.1
  18.7 0.0 copy-start.1
  18.7 0.0 copy-start.2
  18.7 1.5 %collective-permute-start.2 = (bf16[8,32,768]{2,1,0:T(8,128)(2,1)S(1)}, bf16[8,32,768]{2,1,0:T(8,128)(2,1)S(1)}, u32[]{:S(2)}, u32[]{:S(2)}) collective-permute-start(bf16[8,32,768]{2,1,0:T(8,128)(2,1)S(1)} %get-tuple-element.32), channel_id=1, source_target_pairs={{0,2},{1,3},{2,0},{3,1},{4,6},{5,7},{6,4},{7,5},{8,10},{9,11},{10,... | collective-permute-start | bytes 1179656 | tf_op jit(solution)/shard_map/ppermute | solution.py:353
  20.2 0.0 copy-done.3
  20.2 0.0 copy-start.6
  20.2 1.3 %copy-done.6 = bf16[768,768]{1,0:T(8,128)(2,1)S(1)} copy-done((bf16[768,768]{1,0:T(8,128)(2,1)S(1)}, bf16[768,768]{1,0:T(8,128)(2,1)}, u32[]{:S(2)}) %copy-start.6) | copy-done | bytes 1179672
  21.5 0.0 copy-start.7
  21.5 1.3 %copy-done.7 = bf16[768,768]{1,0:T(8,128)(2,1)S(1)} copy-done((bf16[768,768]{1,0:T(8,128)(2,1)S(1)}, bf16[768,768]{1,0:T(8,128)(2,1)}, u32[]{:S(2)}) %copy-start.7) | copy-done | bytes 1179672
  22.8 5.4 %project_images.1 = (bf16[8,256,768]{2,1,0:T(8,128)(2,1)S(1)}, bf16[8,256,768]{2,1,0:T(8,128)(2,1)S(1)}) custom-call(bf16[8,197,768]{2,1,0:T(8,128)(2,1)S(1)} %copy-done.3, bf16[768,768]{1,0:T(8,128)(2,1)S(1)} %copy-done.6, bf16[768,768]{1,0:T(8,128)(2,1)S(1)} %copy-done.7), custom_call_target="tpu_custom_call" | custom-call | flops 4831838208 | bytes 11071488 | tf_op jit(solution)/shard_map/project_images/pallas_call | solution.py:123
  28.2 2.0 %collective-permute-done.1.rest_0_ = bf16[8,32,768]{2,1,0:T(8,128)(2,1)S(1)} collective-permute-done((bf16[8,32,768]{2,1,0:T(8,128)(2,1)S(1)}, bf16[8,32,768]{2,1,0:T(8,128)(2,1)S(1)}, u32[]{:S(2)}, u32[]{:S(2)}) %collective-permute-start.1) | collective-permute-done | bytes 393248 | tf_op jit(solution)/shard_map/ppermute | solution.py:353
  30.2 0.0 copy-done.1
  30.2 0.0 copy-done.2
  30.2 0.0 slice-start
  30.2 0.0 slice-start.2
  30.2 4.6 %attend.2 = (bf16[2,32,768]{2,1,0:T(8,128)(2,1)S(1)}, bf16[2,32,768]{2,1,0:T(8,128)(2,1)S(1)}, bf16[2,32,768]{2,1,0:T(8,128)(2,1)S(1)}, bf16[2,32,768]{2,1,0:T(8,128)(2,1)S(1)}) custom-call(s32[32,128]{1,0:T(8,128)S(1)} %bitcast.12, bf16[32,32,768]{2,1,0:T(8,128)(2,1)S(1)} %copy-done, bf16[32,32,768]{2,1,0:T(8,128)(2,1)S(1)} %collective-permute-done.sibling, ...), custom_call_target="tpu_custom_call" | custom-call | flops 1409286144 | bytes 4718592 | tf_op jit(solution)/shard_map/attend/pallas_call | solution.py:224
  34.8 2.7 %collective-permute-done.2.rest_0_ = bf16[8,32,768]{2,1,0:T(8,128)(2,1)S(1)} collective-permute-done((bf16[8,32,768]{2,1,0:T(8,128)(2,1)S(1)}, bf16[8,32,768]{2,1,0:T(8,128)(2,1)S(1)}, u32[]{:S(2)}, u32[]{:S(2)}) %collective-permute-start.2) | collective-permute-done | bytes 393248 | tf_op jit(solution)/shard_map/ppermute | solution.py:353
  37.5 0.0 copy-start.9
  37.5 0.0 slice-start.1
  37.5 0.0 slice-start.3
  37.5 4.7 %attend.3 = (bf16[2,32,768]{2,1,0:T(8,128)(2,1)S(1)}, bf16[2,32,768]{2,1,0:T(8,128)(2,1)S(1)}, bf16[2,32,768]{2,1,0:T(8,128)(2,1)S(1)}, bf16[2,32,768]{2,1,0:T(8,128)(2,1)S(1)}) custom-call(s32[32,128]{1,0:T(8,128)S(1)} %bitcast.13, bf16[32,32,768]{2,1,0:T(8,128)(2,1)S(1)} %copy-done, bf16[32,32,768]{2,1,0:T(8,128)(2,1)S(1)} %collective-permute-done.sibling, ...), custom_call_target="tpu_custom_call" | custom-call | flops 1409286144 | bytes 4718592 | tf_op jit(solution)/shard_map/attend/pallas_call | solution.py:224
  42.3 0.6 collective-permute-start.5
  42.8 1.6 %collective-permute-start.3 = (bf16[2,32,768]{2,1,0:T(8,128)(2,1)S(1)}, bf16[2,32,768]{2,1,0:T(8,128)(2,1)S(1)}, u32[]{:S(2)}, u32[]{:S(2)}) collective-permute-start(bf16[2,32,768]{2,1,0:T(8,128)(2,1)S(1)} %get-tuple-element.33), channel_id=1, source_target_pairs={{0,28},{4,24},{8,20},{12,16},{16,12},{20,8},{24,4},{28,0},{1,29},{... | collective-permute-start | bytes 294920 | tf_op jit(solution)/shard_map/ppermute | solution.py:353
  44.4 3.2 %collective-permute-start.4 = (bf16[2,32,768]{2,1,0:T(8,128)(2,1)S(1)}, bf16[2,32,768]{2,1,0:T(8,128)(2,1)S(1)}, u32[]{:S(2)}, u32[]{:S(2)}) collective-permute-start(bf16[2,32,768]{2,1,0:T(8,128)(2,1)S(1)} %get-tuple-element.34), channel_id=1, source_target_pairs={{0,24},{4,28},{8,16},{12,20},{16,8},{20,12},{24,0},{28,4},{1,25},{... | collective-permute-start | bytes 294920 | tf_op jit(solution)/shard_map/ppermute | solution.py:353
  47.6 0.0 copy-done.9
  47.6 0.0 collective-permute-start.8
  47.6 2.0 %collective-permute-start.9 = (bf16[2,32,768]{2,1,0:T(8,128)(2,1)S(1)}, bf16[2,32,768]{2,1,0:T(8,128)(2,1)S(1)}, u32[]{:S(2)}, u32[]{:S(2)}) collective-permute-start(bf16[2,32,768]{2,1,0:T(8,128)(2,1)S(1)} %get-tuple-element.41), channel_id=1, source_target_pairs={{0,8},{4,12},{8,0},{12,4},{16,24},{20,28},{24,16},{28,20},{1,9},{5... | collective-permute-start | bytes 294920 | tf_op jit(solution)/shard_map/ppermute | solution.py:353
  49.6 0.0 collective-permute-done.5.rest_2_
  49.6 0.2 collective-permute-start.6
  49.8 1.4 %collective-permute-done.3.rest_0_ = bf16[2,32,768]{2,1,0:T(8,128)(2,1)S(1)} collective-permute-done((bf16[2,32,768]{2,1,0:T(8,128)(2,1)S(1)}, bf16[2,32,768]{2,1,0:T(8,128)(2,1)S(1)}, u32[]{:S(2)}, u32[]{:S(2)}) %collective-permute-start.3) | collective-permute-done | bytes 98336 | tf_op jit(solution)/shard_map/ppermute | solution.py:353
  51.2 2.3 %collective-permute-start.7 = (bf16[2,32,768]{2,1,0:T(8,128)(2,1)S(1)}, bf16[2,32,768]{2,1,0:T(8,128)(2,1)S(1)}, u32[]{:S(2)}, u32[]{:S(2)}) collective-permute-start(bf16[2,32,768]{2,1,0:T(8,128)(2,1)S(1)} %get-tuple-element.39), channel_id=1, source_target_pairs={{0,16},{4,20},{8,24},{12,28},{16,0},{20,4},{24,8},{28,12},{1,17},{... | collective-permute-start | bytes 294920 | tf_op jit(solution)/shard_map/ppermute | solution.py:353
  53.5 0.0 collective-permute-done.4.rest_1_
  53.5 0.0 slice-done
  53.5 0.0 slice-done.2
  53.5 0.0 slice-done.1
  53.5 0.0 slice-done.3
  53.5 0.0 copy-start.4
  53.5 0.0 copy-start.5
  53.6 3.2 %feed_first.1.earlier = bf16[8,32,768]{2,1,0:T(8,128)(2,1)S(1)} custom-call(f32[1,768]{1,0:T(1,128)S(1)} %reshape.12.gain, bf16[768,3072]{1,0:T(8,128)(2,1)S(1)} %bitcast.8, bf16[3072,768]{1,0:T(8,128)(2,1)S(1)} %bitcast.10, bf16[2,32,768]{2,1,0:T(8,128)(2,1)S(1)} %collective-permute-done.3.rest_0_, bf16[2,32,768]{2,1,0:T(8,128)(2,1)S(1)} %collective-permute-done.4.rest_1_, ...), custom_call_target="tpu_custom_call" | custom-call | flops 2415919104 | bytes 9437184 | tf_op jit(solution)/shard_map/feed_first/pallas_call | solution.py:296
  56.8 0.1 collective-permute-done.8.rest_2_
  56.9 0.6 collective-permute-done.9.rest_3_
  57.6 3.3 %collective-permute-done.6.rest_0_ = bf16[2,32,768]{2,1,0:T(8,128)(2,1)S(1)} collective-permute-done((bf16[2,32,768]{2,1,0:T(8,128)(2,1)S(1)}, bf16[2,32,768]{2,1,0:T(8,128)(2,1)S(1)}, u32[]{:S(2)}, u32[]{:S(2)}) %collective-permute-start.6) | collective-permute-done | bytes 98336 | tf_op jit(solution)/shard_map/ppermute | solution.py:353
  60.8 0.9 %collective-permute-done.7.rest_1_ = bf16[2,32,768]{2,1,0:T(8,128)(2,1)S(1)} collective-permute-done((bf16[2,32,768]{2,1,0:T(8,128)(2,1)S(1)}, bf16[2,32,768]{2,1,0:T(8,128)(2,1)S(1)}, u32[]{:S(2)}, u32[]{:S(2)}) %collective-permute-start.7) | collective-permute-done | bytes 98336 | tf_op jit(solution)/shard_map/ppermute | solution.py:353
  61.7 0.0 copy-done.4
  61.7 0.0 copy-done.5
  61.7 4.6 %feed_last.1 = (bf16[16,32,768]{2,1,0:T(8,128)(2,1)}, f32[2,16]{1,0:T(2,128)}) custom-call(s32[16]{0:T(128)S(1)} %copy-done.5, f32[1,768]{1,0:T(1,128)S(1)} %reshape.12.gain, bf16[2,768]{1,0:T(2,128)(2,1)S(1)} %bitcast.14, bf16[768,3072]{1,0:T(8,128)(2,1)S(1)} %bitcast.8, bf16[3072,768]{1,0:T(8,128)(2,1)S(1)} %bitcast.10, ...), custom_call_target="tpu_custom_call" | custom-call | flops 2415919104 | bytes 9437184 | tf_op jit(solution)/shard_map/feed_last/pallas_call | solution.py:311
  (4 shorter events, 0.0 us)
Async XLA Ops:
  0.6 16.4 %collective-permute-start = (bf16[32,32,768]{2,1,0:T(8,128)(2,1)}, bf16[32,32,768]{2,1,0:T(8,128)(2,1)S(1)}, u32[]{:S(2)}, u32[]{:S(2)}) collective-permute-start(bf16[32,32,768]{2,1,0:T(8,128)(2,1)} %own.5), channel_id=1, source_target_pairs={{0,1},{1,0},{2,3},{3,2},{4,5},{5,4},{6,7},{7,6},{8,9},{9,8},{10,11... | collective-permute-start | bytes 4718600 | tf_op jit(solution)/shard_map/ppermute | solution.py:353
  2.9 14.0 %all-to-all-start = ((s32[32,1,128]{2,1,0:T(1,128)}), s32[32,1,128]{2,1,0:T(1,128)S(1)}, u32[]{:S(2)}, u32[]{:S(2)}) async-start(s32[32,1,128]{2,1,0:T(1,128)} %bitcast.15), calls=%async_computation | async-start | bytes 32768 | tf_op jit(solution)/shard_map/all_to_all | solution.py:359
  9.9 3.8 %copy-start.8 = (f32[768]{0:T(1024)S(1)}, f32[768]{0:T(1024)}, u32[]{:S(2)}) copy-start(f32[768]{0:T(1024)} %param.25) | copy-start | bytes 9220
  9.9 7.1 %copy-start = (bf16[32,32,768]{2,1,0:T(8,128)(2,1)S(1)}, bf16[32,32,768]{2,1,0:T(8,128)(2,1)}, u32[]{:S(2)}) copy-start(bf16[32,32,768]{2,1,0:T(8,128)(2,1)} %own.5) | copy-start | bytes 4718596
  17.0 3.2 %copy-start.3 = (bf16[8,197,768]{2,1,0:T(8,128)(2,1)S(1)}, bf16[8,197,768]{2,1,0:T(8,128)(2,1)}, u32[]{:S(2)}) copy-start(bf16[8,197,768]{2,1,0:T(8,128)(2,1)} %copy.19.images) | copy-start | bytes 7262212
  18.1 12.1 %collective-permute-start.1 = (bf16[8,32,768]{2,1,0:T(8,128)(2,1)S(1)}, bf16[8,32,768]{2,1,0:T(8,128)(2,1)S(1)}, u32[]{:S(2)}, u32[]{:S(2)}) collective-permute-start(bf16[8,32,768]{2,1,0:T(8,128)(2,1)S(1)} %get-tuple-element.25), channel_id=1, source_target_pairs={{0,2},{1,3},{2,0},{3,1},{4,6},{5,7},{6,4},{7,5},{8,10},{9,11},{10,... | collective-permute-start | bytes 1179656 | tf_op jit(solution)/shard_map/ppermute | solution.py:353
  18.7 11.5 %copy-start.1 = (bf16[768,768]{1,0:T(8,128)(2,1)S(1)}, bf16[768,768]{1,0:T(8,128)(2,1)}, u32[]{:S(2)}) copy-start(bf16[768,768]{1,0:T(8,128)(2,1)} %rest_3_.3) | copy-start | bytes 3538948
  18.7 11.5 %copy-start.2 = (bf16[768,768]{1,0:T(8,128)(2,1)S(1)}, bf16[768,768]{1,0:T(8,128)(2,1)}, u32[]{:S(2)}) copy-start(bf16[768,768]{1,0:T(8,128)(2,1)} %rest_4_.3) | copy-start | bytes 3538948
  18.7 18.8 %collective-permute-start.2 = (bf16[8,32,768]{2,1,0:T(8,128)(2,1)S(1)}, bf16[8,32,768]{2,1,0:T(8,128)(2,1)S(1)}, u32[]{:S(2)}, u32[]{:S(2)}) collective-permute-start(bf16[8,32,768]{2,1,0:T(8,128)(2,1)S(1)} %get-tuple-element.32), channel_id=1, source_target_pairs={{0,2},{1,3},{2,0},{3,1},{4,6},{5,7},{6,4},{7,5},{8,10},{9,11},{10,... | collective-permute-start | bytes 1179656 | tf_op jit(solution)/shard_map/ppermute | solution.py:353
  20.2 1.3 %copy-start.6 = (bf16[768,768]{1,0:T(8,128)(2,1)S(1)}, bf16[768,768]{1,0:T(8,128)(2,1)}, u32[]{:S(2)}) copy-start(bf16[768,768]{1,0:T(8,128)(2,1)} %key_weight.1) | copy-start | bytes 3538948
  21.5 1.3 %copy-start.7 = (bf16[768,768]{1,0:T(8,128)(2,1)S(1)}, bf16[768,768]{1,0:T(8,128)(2,1)}, u32[]{:S(2)}) copy-start(bf16[768,768]{1,0:T(8,128)(2,1)} %value_weight.1) | copy-start | bytes 3538948
  30.2 23.3 %slice-start = ((s8[4718592]{0:T(1024)(128)(4,1)}), s8[4194304]{0:T(1024)(128)(4,1)S(1)}, s32[]{:S(2)}) async-start(s8[4718592]{0:T(1024)(128)(4,1)} %bitcast.7), calls=%async_computation.1 | async-start | bytes 8388608
  30.2 23.3 %slice-start.2 = ((s8[4718592]{0:T(1024)(128)(4,1)}), s8[4194304]{0:T(1024)(128)(4,1)S(1)}, s32[]{:S(2)}) async-start(s8[4718592]{0:T(1024)(128)(4,1)} %bitcast.9), calls=%async_computation.3 | async-start | bytes 8388608
  37.5 10.1 %copy-start.9 = (f32[768]{0:T(1024)S(1)}, f32[768]{0:T(1024)}, u32[]{:S(2)}) copy-start(f32[768]{0:T(1024)} %param.28) | copy-start | bytes 9220
  37.5 16.0 %slice-start.1 = ((s8[4718592]{0:T(1024)(128)(4,1)}), s8[524288]{0:T(1024)(128)(4,1)S(1)}, s32[]{:S(2)}) async-start(s8[4718592]{0:T(1024)(128)(4,1)} %bitcast.7), calls=%async_computation.2 | async-start | bytes 1048576
  37.5 16.0 %slice-start.3 = ((s8[4718592]{0:T(1024)(128)(4,1)}), s8[524288]{0:T(1024)(128)(4,1)S(1)}, s32[]{:S(2)}) async-start(s8[4718592]{0:T(1024)(128)(4,1)} %bitcast.9), calls=%async_computation.4 | async-start | bytes 1048576
  42.3 7.3 %collective-permute-start.5 = (bf16[2,32,768]{2,1,0:T(8,128)(2,1)S(1)}, bf16[2,32,768]{2,1,0:T(8,128)(2,1)S(1)}, u32[]{:S(2)}, u32[]{:S(2)}) collective-permute-start(bf16[2,32,768]{2,1,0:T(8,128)(2,1)S(1)} %get-tuple-element.36), channel_id=1, source_target_pairs={{0,4},{4,0},{8,12},{12,8},{16,20},{20,16},{24,28},{28,24},{1,5},{5... | collective-permute-start | bytes 294920 | tf_op jit(solution)/shard_map/ppermute | solution.py:353
  42.8 8.4 %collective-permute-start.3 = (bf16[2,32,768]{2,1,0:T(8,128)(2,1)S(1)}, bf16[2,32,768]{2,1,0:T(8,128)(2,1)S(1)}, u32[]{:S(2)}, u32[]{:S(2)}) collective-permute-start(bf16[2,32,768]{2,1,0:T(8,128)(2,1)S(1)} %get-tuple-element.33), channel_id=1, source_target_pairs={{0,28},{4,24},{8,20},{12,16},{16,12},{20,8},{24,4},{28,0},{1,29},{... | collective-permute-start | bytes 294920 | tf_op jit(solution)/shard_map/ppermute | solution.py:353
  44.4 9.1 %collective-permute-start.4 = (bf16[2,32,768]{2,1,0:T(8,128)(2,1)S(1)}, bf16[2,32,768]{2,1,0:T(8,128)(2,1)S(1)}, u32[]{:S(2)}, u32[]{:S(2)}) collective-permute-start(bf16[2,32,768]{2,1,0:T(8,128)(2,1)S(1)} %get-tuple-element.34), channel_id=1, source_target_pairs={{0,24},{4,28},{8,16},{12,20},{16,8},{20,12},{24,0},{28,4},{1,25},{... | collective-permute-start | bytes 294920 | tf_op jit(solution)/shard_map/ppermute | solution.py:353
  47.6 9.3 %collective-permute-start.8 = (bf16[2,32,768]{2,1,0:T(8,128)(2,1)S(1)}, bf16[2,32,768]{2,1,0:T(8,128)(2,1)S(1)}, u32[]{:S(2)}, u32[]{:S(2)}) collective-permute-start(bf16[2,32,768]{2,1,0:T(8,128)(2,1)S(1)} %get-tuple-element.40), channel_id=1, source_target_pairs={{0,12},{4,8},{8,4},{12,0},{16,28},{20,24},{24,20},{28,16},{1,13},{... | collective-permute-start | bytes 294920 | tf_op jit(solution)/shard_map/ppermute | solution.py:353
  47.6 9.9 %collective-permute-start.9 = (bf16[2,32,768]{2,1,0:T(8,128)(2,1)S(1)}, bf16[2,32,768]{2,1,0:T(8,128)(2,1)S(1)}, u32[]{:S(2)}, u32[]{:S(2)}) collective-permute-start(bf16[2,32,768]{2,1,0:T(8,128)(2,1)S(1)} %get-tuple-element.41), channel_id=1, source_target_pairs={{0,8},{4,12},{8,0},{12,4},{16,24},{20,28},{24,16},{28,20},{1,9},{5... | collective-permute-start | bytes 294920 | tf_op jit(solution)/shard_map/ppermute | solution.py:353
  49.6 11.2 %collective-permute-start.6 = (bf16[2,32,768]{2,1,0:T(8,128)(2,1)S(1)}, bf16[2,32,768]{2,1,0:T(8,128)(2,1)S(1)}, u32[]{:S(2)}, u32[]{:S(2)}) collective-permute-start(bf16[2,32,768]{2,1,0:T(8,128)(2,1)S(1)} %get-tuple-element.38), channel_id=1, source_target_pairs={{0,20},{4,16},{8,28},{12,24},{16,4},{20,0},{24,12},{28,8},{1,21},{... | collective-permute-start | bytes 294920 | tf_op jit(solution)/shard_map/ppermute | solution.py:353
  51.2 10.5 %collective-permute-start.7 = (bf16[2,32,768]{2,1,0:T(8,128)(2,1)S(1)}, bf16[2,32,768]{2,1,0:T(8,128)(2,1)S(1)}, u32[]{:S(2)}, u32[]{:S(2)}) collective-permute-start(bf16[2,32,768]{2,1,0:T(8,128)(2,1)S(1)} %get-tuple-element.39), channel_id=1, source_target_pairs={{0,16},{4,20},{8,24},{12,28},{16,0},{20,4},{24,8},{28,12},{1,17},{... | collective-permute-start | bytes 294920 | tf_op jit(solution)/shard_map/ppermute | solution.py:353
  53.5 8.2 %copy-start.4 = (bf16[768,2]{0,1:T(2,128)(2,1)S(1)}, bf16[768,2]{0,1:T(2,128)(2,1)}, u32[]{:S(2)}) copy-start(bf16[768,2]{0,1:T(2,128)(2,1)} %param.29) | copy-start | bytes 9220
  53.5 8.2 %copy-start.5 = (s32[16]{0:T(128)S(1)}, s32[16]{0:T(128)}, u32[]{:S(2)}) copy-start(s32[16]{0:T(128)} %get-tuple-element.23.place) | copy-start | bytes 196
where the time goes:
time: 66.6 us; the launch traced here: 66.4 us
  Pallas kernels  25.5 us (38%)
  starting transfers between devices  19.4 us (29%)
  waiting for transfers between devices  14.3 us (21%)
  local copies, waits for them, and re-layouts  6.32 us (9%)
  between operations  0.79 us (1%)
    ppermute x10, starting transfers between devices, swap(): lax.ppermute(array, axis, [(peer, peer ^ distance) for peer in range(size)])  12.4 us
    ppermute x10, waiting for transfers between devices, swap(): lax.ppermute(array, axis, [(peer, peer ^ distance) for peer in range(size)])  11 us
    pallas_call x2, Pallas kernels, attend(): pl.pallas_call(functools.partial(attend_kernel, key_rows, cap_count, len(...  9.3 us
    all_to_all x1, starting transfers between devices, body(): lax.all_to_all(table, ('img', 'cap'), split_axis=0, concat_axis=0, tiled=...  6.97 us
    unnamed x29, local copies, waits for them, and re-layouts  6.32 us
    pallas_call x1, Pallas kernels, project_images(): pl.pallas_call(project_kernel, out_shape=(out, out), grid=(count,), in_sp...  5.44 us
    pallas_call x1, Pallas kernels, feed_last(): pl.pallas_call(functools.partial(feed_last_kernel, first_parts, last_part...  4.64 us
    all_to_all x1, waiting for transfers between devices, body(): lax.all_to_all(table, ('img', 'cap'), split_axis=0, concat_axis=0, tiled=...  3.32 us
  transfers between devices with their start and end apart: 11, of which 8 were waited for; matrix products, arithmetic and copies ran while one was open for 6% of the time, Pallas kernels for 23%

commit v1 on v0

--- a/solution.py
+++ b/solution.py
@@ -16,6 +16,7 @@
 GROUP = 256
 F32 = jnp.float32
 BF16 = jnp.bfloat16
+SMALL = pl.CostEstimate(flops=1 << 16, bytes_accessed=1 << 10, transcendentals=0)
 
 SMEM = pl.BlockSpec(memory_space=pltpu.SMEM)
 VMEM = pl.BlockSpec(memory_space=pltpu.VMEM)
@@ -127,11 +128,7 @@
         in_specs=[pl.BlockSpec((1, rows, width), lambda i: (i, 0, 0)), whole, whole],
         out_specs=(pl.BlockSpec((1, KEY_PAD, width), lambda i: (i, 0, 0)),) * 2,
         compiler_params=params(16),
-        cost_estimate=pl.CostEstimate(
-            flops=4 * count * KEY_PAD * width * width,
-            bytes_accessed=2 * (2 * width * width + count * (rows + 2 * KEY_PAD) * width),
-            transcendentals=0,
-        ),
+        cost_estimate=SMALL,
         name="project_images",
     )(images, key_weight, value_weight)
 
@@ -232,11 +229,7 @@
             pltpu.VMEM((rows, width), BF16),
         ],
         compiler_params=params(16),
-        cost_estimate=pl.CostEstimate(
-            flops=4 * rows * width * width + 4 * rows * GROUP * KEY_PAD * HEADS,
-            bytes_accessed=8 * width * width,
-            transcendentals=rows * HEADS * KEY_PAD,
-        ),
+        cost_estimate=SMALL,
         name="attend",
     )(table, own, sibling, *far, keys, values, query_weight, out_weight, gain)
 
@@ -344,9 +337,9 @@
     cap_count = lax.axis_size("cap")
     far_steps = range(1, cap_count // CORES)
     half, quarter = img_count // 2, img_count // 4
-    chunks = (tuple(range(img_count - 1, half - 1, -1)), tuple(range(half - 1, -1, -1)))
-    first_parts = chunks[0][:quarter] + chunks[1][half - quarter :]
-    last_parts = chunks[0][quarter:] + chunks[1][: half - quarter]
+    distances = tuple(range(img_count - 1, -1, -1))
+    first_parts, last_parts = distances[:half], distances[half:]
+    chunks = (distances[:quarter], distances[quarter:half], distances[half:])
 
     def swap(array, axis, distance):
         size = lax.axis_size(axis)
@@ -367,6 +360,10 @@
     gain_ffn = gain_ffn.reshape(1, -1)
     hidden = {}
     for index, chunk in enumerate(chunks):
+        if index == 2:
+            sent = [hidden[distance] for distance in chunks[0]]
+            table, sent = lax.optimization_barrier((table, sent))
+            hidden.update(zip(chunks[0], sent))
         blocks = attend(
             images.shape[1],
             cap_count,
@@ -381,8 +378,6 @@
             out_weight,
             gain_attn,
         )
-        if index == 0:
-            blocks, far = lax.optimization_barrier((blocks, far))
         for distance, block in zip(chunk, blocks):
             hidden[distance] = swap(block, "img", distance) if distance else block
     earlier = feed_first([hidden[part] for part in first_parts], gain_ffn, in_weight, back_weight)

time: 66.6 us -> 69.5 us (1.044)
  blocking collectives: 0 us -> 14.1 us
  waiting for transfers between devices: 14.3 us -> 8.23 us
  local copies, waits for them, and re-layouts: 6.32 us -> 2.56 us
  starting transfers between devices: 19.4 us -> 16.3 us
  Pallas kernels: 25.5 us -> 27.2 us
    all_to_all x0 -> x1, blocking collectives: none -> 14.1 us  [body(): lax.all_to_all(table, ('img', 'cap'), split_axis=0, concat_axis=0, tiled=...]
    all_to_all x1 -> x0, starting transfers between devices: 6.97 us -> none  [body(): lax.all_to_all(table, ('img', 'cap'), split_axis=0, concat_axis=0, tiled=...]
    ppermute x10 -> x11, starting transfers between devices: 12.4 us -> 16.3 us  [swap(): lax.ppermute(array, axis, [(peer, peer ^ distance) for peer in range(size)])]
    unnamed x29 -> x31, local copies, waits for them, and re-layouts: 6.32 us -> 2.55 us
    all_to_all x1 -> x0, waiting for transfers between devices: 3.32 us -> none  [body(): lax.all_to_all(table, ('img', 'cap'), split_axis=0, concat_axis=0, tiled=...]
    ppermute x10 -> x11, waiting for transfers between devices: 11 us -> 8.23 us  [swap(): lax.ppermute(array, axis, [(peer, peer ^ distance) for peer in range(size)])]
    pallas_call x2 -> x3, Pallas kernels: 9.3 us -> 10.8 us  [attend(): pl.pallas_call(functools.partial(attend_kernel, key_rows, cap_count, len(...]
  transfers between devices with their start and end apart: 11 -> 11, of which waited for: 8 -> 2; matrix products, arithmetic and copies ran while one was open for 6% -> 1% of each run, Pallas kernels for 23% -> 31%
where the time goes in v1:
time: 69.5 us; the launch traced here: 69.3 us
  Pallas kernels  27.2 us (39%)
  starting transfers between devices  16.3 us (23%)
  blocking collectives  14.1 us (20%)
  waiting for transfers between devices  8.23 us (12%)
  local copies, waits for them, and re-layouts  2.56 us (4%)
  between operations  0.86 us (1%)
    ppermute x11, starting transfers between devices, swap(): lax.ppermute(array, axis, [(peer, peer ^ distance) for peer in range(size)])  16.3 us
    all_to_all x1, blocking collectives, body(): lax.all_to_all(table, ('img', 'cap'), split_axis=0, concat_axis=0, tiled=...  14.1 us
    pallas_call x3, Pallas kernels, attend(): pl.pallas_call(functools.partial(attend_kernel, key_rows, cap_count, len(...  10.8 us
    ppermute x11, waiting for transfers between devices, swap(): lax.ppermute(array, axis, [(peer, peer ^ distance) for peer in range(size)])  8.23 us
    pallas_call x1, Pallas kernels, project_images(): pl.pallas_call(project_kernel, out_shape=(out, out), grid=(count,), in_sp...  5.54 us
    pallas_call x1, Pallas kernels, feed_last(): pl.pallas_call(functools.partial(feed_last_kernel, first_parts, last_part...  4.68 us
    pallas_call x1, Pallas kernels, feed_first(): pl.pallas_call(feed_first_kernel, out_shape=jax.ShapeDtypeStruct((slots,...  3.28 us
    unnamed x31, local copies, waits for them, and re-layouts  2.55 us
  transfers between devices with their start and end apart: 11, of which 2 were waited for; matrix products, arithmetic and copies ran while one was open for 1% of the time, Pallas kernels for 31%

profile of v1, /device:TPU:0, one launch (start us, length us, event | category | flops | bytes accessed | tf_op | source)
XLA Modules:
  0.0 69.3 jit_solution(7019981946817856981)
XLA Ops:
  0.6 0.5 collective-permute-start
  1.1 1.8 %slot_table.1 = (s32[32,128]{1,0:T(8,128)}, s32[16]{0:T(128)}) custom-call(s32[2,512]{1,0:T(2,128)} %bitcast.17, s32[16]{0:T(128)} %order.1, s32[64]{0:T(128)} %image_slot.1, s32[128]{0:T(128)} %caption_slot.1), custom_call_target="tpu_custom_call" | custom-call | tf_op jit(solution)/shard_map/slot_table/pallas_call | solution.py:58
  2.9 14.1 %all_to_all.11 = s32[32,1,128]{2,1,0:T(1,128)S(1)} all-to-all(s32[32,1,128]{2,1,0:T(1,128)} %bitcast.16), channel_id=1, replica_groups=mesh['img'=8,'cap'=4] {'img','cap'}, dimensions={0} | all-to-all | bytes 32768 | tf_op jit(solution)/shard_map/all_to_all | solution.py:352
  17.0 0.0 collective-permute-done.sibling
  17.0 0.0 copy-start
  17.0 1.4 %copy-done = bf16[32,32,768]{2,1,0:T(8,128)(2,1)S(1)} copy-done((bf16[32,32,768]{2,1,0:T(8,128)(2,1)S(1)}, bf16[32,32,768]{2,1,0:T(8,128)(2,1)}, u32[]{:S(2)}) %copy-start) | copy-done | bytes 1572888
  18.4 0.0 copy-start.8
  18.4 1.1 %pick_captions.1 = (bf16[4,32,768]{2,1,0:T(8,128)(2,1)S(1)}, bf16[4,32,768]{2,1,0:T(8,128)(2,1)S(1)}, bf16[8,32,768]{2,1,0:T(8,128)(2,1)S(1)}) custom-call(s32[32,128]{1,0:T(8,128)S(1)} %bitcast.11, bf16[32,32,768]{2,1,0:T(8,128)(2,1)S(1)} %copy-done, bf16[32,32,768]{2,1,0:T(8,128)(2,1)S(1)} %collective-permute-done.sibling), custom_call_target="tpu_custom_call" | custom-call | bytes 1048576 | tf_op jit(solution)/shard_map/pick_captions/pallas_call | solution.py:101
  19.5 0.6 collective-permute-start.7
  20.1 1.5 %collective-permute-start.1 = (bf16[4,32,768]{2,1,0:T(8,128)(2,1)S(1)}, bf16[4,32,768]{2,1,0:T(8,128)(2,1)S(1)}, u32[]{:S(2)}, u32[]{:S(2)}) collective-permute-start(bf16[4,32,768]{2,1,0:T(8,128)(2,1)S(1)} %get-tuple-element.24), channel_id=1, source_target_pairs={{0,2},{1,3},{2,0},{3,1},{4,6},{5,7},{6,4},{7,5},{8,10},{9,11},{10,... | collective-permute-start | bytes 589832 | tf_op jit(solution)/shard_map/ppermute | solution.py:346
  21.6 0.0 copy-start.4
  21.6 0.0 copy-start.5
  21.6 0.5 collective-permute-start.4
  22.2 0.0 copy-done.8
  22.2 0.5 copy.19.images
  22.6 0.3 copy-done.4
  22.9 0.4 copy-done.5
  23.3 0.0 copy-start.9
  23.3 0.0 copy-start.1
  23.3 0.0 copy-start.2
  23.3 0.0 copy-start.3
  23.3 5.5 %project_images.1 = (bf16[8,256,768]{2,1,0:T(8,128)(2,1)S(1)}, bf16[8,256,768]{2,1,0:T(8,128)(2,1)S(1)}) custom-call(bf16[8,197,768]{2,1,0:T(8,128)(2,1)S(1)} %copy.19.images, bf16[768,768]{1,0:T(8,128)(2,1)S(1)} %copy-done.4, bf16[768,768]{1,0:T(8,128)(2,1)S(1)} %copy-done.5), custom_call_target="tpu_custom_call" | custom-call | flops 65536 | bytes 1024 | tf_op jit(solution)/shard_map/project_images/pallas_call | solution.py:124
  28.8 0.0 copy-done.9
  28.8 7.0 %collective-permute-done.1.rest_0_ = bf16[4,32,768]{2,1,0:T(8,128)(2,1)S(1)} collective-permute-done((bf16[4,32,768]{2,1,0:T(8,128)(2,1)S(1)}, bf16[4,32,768]{2,1,0:T(8,128)(2,1)S(1)}, u32[]{:S(2)}, u32[]{:S(2)}) %collective-permute-start.1) | collective-permute-done | bytes 196640 | tf_op jit(solution)/shard_map/ppermute | solution.py:346
  35.8 0.0 copy-done.1
  35.8 0.0 copy-done.2
  35.8 0.0 copy-done.3
  35.8 0.0 slice-start.2
  35.8 3.0 %attend.3 = (bf16[2,32,768]{2,1,0:T(8,128)(2,1)S(1)}, bf16[2,32,768]{2,1,0:T(8,128)(2,1)S(1)}) custom-call(s32[32,128]{1,0:T(8,128)S(1)} %bitcast.12, bf16[32,32,768]{2,1,0:T(8,128)(2,1)S(1)} %copy-done.1, bf16[32,32,768]{2,1,0:T(8,128)(2,1)S(1)} %collective-permute-done.sibling, bf16[4,32,768]{2,1,0:T(8,128)(2,1)S(1)} %collective-permute-done.1.rest_0_, ...), custom_call_target="tpu_custom_call" | custom-call | flops 65536 | bytes 1024 | tf_op jit(solution)/shard_map/attend/pallas_call | solution.py:221
  38.9 0.6 collective-permute-start.2
  39.5 0.0 copy-start.10
  39.5 0.0 slice-start.3
  39.5 3.3 %collective-permute-start.3 = (bf16[2,32,768]{2,1,0:T(8,128)(2,1)S(1)}, bf16[2,32,768]{2,1,0:T(8,128)(2,1)S(1)}, u32[]{:S(2)}, u32[]{:S(2)}) collective-permute-start(bf16[2,32,768]{2,1,0:T(8,128)(2,1)S(1)} %get-tuple-element.28), channel_id=1, source_target_pairs={{0,24},{4,28},{8,16},{12,20},{16,8},{20,12},{24,0},{28,4},{1,25},{... | collective-permute-start | bytes 294920 | tf_op jit(solution)/shard_map/ppermute | solution.py:346
  42.8 0.0 collective-permute-done.4.rest_0_
  42.8 3.0 %attend.4 = (bf16[2,32,768]{2,1,0:T(8,128)(2,1)S(1)}, bf16[2,32,768]{2,1,0:T(8,128)(2,1)S(1)}) custom-call(s32[32,128]{1,0:T(8,128)S(1)} %bitcast.13, bf16[32,32,768]{2,1,0:T(8,128)(2,1)S(1)} %copy-done.1, bf16[32,32,768]{2,1,0:T(8,128)(2,1)S(1)} %collective-permute-done.sibling, bf16[4,32,768]{2,1,0:T(8,128)(2,1)S(1)} %collective-permute-done.4.rest_0_, ...), custom_call_target="tpu_custom_call" | custom-call | flops 65536 | bytes 1024 | tf_op jit(solution)/shard_map/attend/pallas_call | solution.py:221
  45.8 0.1 collective-permute-start.5
  45.9 3.8 %collective-permute-start.6 = (bf16[2,32,768]{2,1,0:T(8,128)(2,1)S(1)}, bf16[2,32,768]{2,1,0:T(8,128)(2,1)S(1)}, u32[]{:S(2)}, u32[]{:S(2)}) collective-permute-start(bf16[2,32,768]{2,1,0:T(8,128)(2,1)S(1)} %get-tuple-element.33), channel_id=1, source_target_pairs={{0,16},{4,20},{8,24},{12,28},{16,0},{20,4},{24,8},{28,12},{1,17},{... | collective-permute-start | bytes 294920 | tf_op jit(solution)/shard_map/ppermute | solution.py:346
  49.7 0.0 copy-done.10
  49.7 0.0 slice-start
  49.7 0.0 slice-start.1
  49.8 0.0 collective-permute-done.2.rest_0_
  49.8 0.0 collective-permute-done.3.rest_1_
  49.8 0.0 collective-permute-done.7.rest_0_
  49.8 4.7 %attend.5 = (bf16[2,32,768]{2,1,0:T(8,128)(2,1)S(1)}, bf16[2,32,768]{2,1,0:T(8,128)(2,1)S(1)}, bf16[2,32,768]{2,1,0:T(8,128)(2,1)S(1)}, bf16[2,32,768]{2,1,0:T(8,128)(2,1)S(1)}) custom-call(s32[32,128]{1,0:T(8,128)S(1)} %bitcast.14, bf16[32,32,768]{2,1,0:T(8,128)(2,1)S(1)} %copy-done.1, bf16[32,32,768]{2,1,0:T(8,128)(2,1)S(1)} %collective-permute-done.sibling, ...), custom_call_target="tpu_custom_call" | custom-call | flops 65536 | bytes 1024 | tf_op jit(solution)/shard_map/attend/pallas_call | solution.py:221
  54.5 0.6 collective-permute-start.10
  55.2 4.8 %collective-permute-start.8 = (bf16[2,32,768]{2,1,0:T(8,128)(2,1)S(1)}, bf16[2,32,768]{2,1,0:T(8,128)(2,1)S(1)}, u32[]{:S(2)}, u32[]{:S(2)}) collective-permute-start(bf16[2,32,768]{2,1,0:T(8,128)(2,1)S(1)} %get-tuple-element.36), channel_id=1, source_target_pairs={{0,12},{4,8},{8,4},{12,0},{16,28},{20,24},{24,20},{28,16},{1,13},{... | collective-permute-start | bytes 294920 | tf_op jit(solution)/shard_map/ppermute | solution.py:346
  60.0 0.0 copy-start.6
  60.0 0.0 copy-start.7
  60.0 0.0 collective-permute-start.9
  60.0 0.0 collective-permute-done.5.rest_2_
  60.0 0.0 collective-permute-done.6.rest_3_
  60.0 0.0 slice-done.2
  60.0 0.0 slice-done.3
  60.0 0.0 slice-done
  60.0 0.0 slice-done.1
  60.1 3.3 %feed_first.1.earlier = bf16[8,32,768]{2,1,0:T(8,128)(2,1)S(1)} custom-call(f32[1,768]{1,0:T(1,128)S(1)} %reshape.12.gain, bf16[768,3072]{1,0:T(8,128)(2,1)S(1)} %bitcast.8, bf16[3072,768]{1,0:T(8,128)(2,1)S(1)} %bitcast.10, bf16[2,32,768]{2,1,0:T(8,128)(2,1)S(1)} %collective-permute-done.2.rest_0_, bf16[2,32,768]{2,1,0:T(8,128)(2,1)S(1)} %collective-permute-done.3.rest_1_, ...), custom_call_target="tpu_custom_call" | custom-call | flops 2415919104 | bytes 9437184 | tf_op jit(solution)/shard_map/feed_first/pallas_call | solution.py:289
  63.3 0.0 collective-permute-done.10.rest_2_
  63.4 0.0 collective-permute-done.8.rest_0_
  63.4 1.2 %collective-permute-done.9.rest_1_ = bf16[2,32,768]{2,1,0:T(8,128)(2,1)S(1)} collective-permute-done((bf16[2,32,768]{2,1,0:T(8,128)(2,1)S(1)}, bf16[2,32,768]{2,1,0:T(8,128)(2,1)S(1)}, u32[]{:S(2)}, u32[]{:S(2)}) %collective-permute-start.9) | collective-permute-done | bytes 98336 | tf_op jit(solution)/shard_map/ppermute | solution.py:346
  64.6 0.0 copy-done.6
  64.6 0.0 copy-done.7
  64.6 4.7 %feed_last.1 = (bf16[16,32,768]{2,1,0:T(8,128)(2,1)}, f32[2,16]{1,0:T(2,128)}) custom-call(s32[16]{0:T(128)S(1)} %copy-done.7, f32[1,768]{1,0:T(1,128)S(1)} %reshape.12.gain, bf16[2,768]{1,0:T(2,128)(2,1)S(1)} %bitcast.15, bf16[768,3072]{1,0:T(8,128)(2,1)S(1)} %bitcast.8, bf16[3072,768]{1,0:T(8,128)(2,1)S(1)} %bitcast.10, ...), custom_call_target="tpu_custom_call" | custom-call | flops 2415919104 | bytes 9437184 | tf_op jit(solution)/shard_map/feed_last/pallas_call | solution.py:304
  (4 shorter events, 0.0 us)
Async XLA Ops:
  0.6 16.4 %collective-permute-start = (bf16[32,32,768]{2,1,0:T(8,128)(2,1)}, bf16[32,32,768]{2,1,0:T(8,128)(2,1)S(1)}, u32[]{:S(2)}, u32[]{:S(2)}) collective-permute-start(bf16[32,32,768]{2,1,0:T(8,128)(2,1)} %own.7), channel_id=1, source_target_pairs={{0,1},{1,0},{2,3},{3,2},{4,5},{5,4},{6,7},{7,6},{8,9},{9,8},{10,11... | collective-permute-start | bytes 4718600 | tf_op jit(solution)/shard_map/ppermute | solution.py:346
  17.0 1.4 %copy-start = (bf16[32,32,768]{2,1,0:T(8,128)(2,1)S(1)}, bf16[32,32,768]{2,1,0:T(8,128)(2,1)}, u32[]{:S(2)}) copy-start(bf16[32,32,768]{2,1,0:T(8,128)(2,1)} %own.7) | copy-start | bytes 4718596
  18.4 3.8 %copy-start.8 = (bf16[8,197,768]{2,0,1:T(8,128)(2,1)S(1)}, bf16[8,197,768]{2,0,1:T(8,128)(2,1)}, u32[]{:S(2)}) copy-start(bf16[8,197,768]{2,0,1:T(8,128)(2,1)} %param.19) | copy-start | bytes 7262212
  19.5 30.2 %collective-permute-start.7 = (bf16[8,32,768]{2,1,0:T(8,128)(2,1)S(1)}, bf16[8,32,768]{2,1,0:T(8,128)(2,1)S(1)}, u32[]{:S(2)}, u32[]{:S(2)}) collective-permute-start(bf16[8,32,768]{2,1,0:T(8,128)(2,1)S(1)} %get-tuple-element.35), channel_id=1, source_target_pairs={{0,2},{1,3},{2,0},{3,1},{4,6},{5,7},{6,4},{7,5},{8,10},{9,11},{10,... | collective-permute-start | bytes 1179656 | tf_op jit(solution)/shard_map/ppermute | solution.py:346
  20.1 15.7 %collective-permute-start.1 = (bf16[4,32,768]{2,1,0:T(8,128)(2,1)S(1)}, bf16[4,32,768]{2,1,0:T(8,128)(2,1)S(1)}, u32[]{:S(2)}, u32[]{:S(2)}) collective-permute-start(bf16[4,32,768]{2,1,0:T(8,128)(2,1)S(1)} %get-tuple-element.24), channel_id=1, source_target_pairs={{0,2},{1,3},{2,0},{3,1},{4,6},{5,7},{6,4},{7,5},{8,10},{9,11},{10,... | collective-permute-start | bytes 589832 | tf_op jit(solution)/shard_map/ppermute | solution.py:346
  21.6 1.3 %copy-start.4 = (bf16[768,768]{1,0:T(8,128)(2,1)S(1)}, bf16[768,768]{1,0:T(8,128)(2,1)}, u32[]{:S(2)}) copy-start(bf16[768,768]{1,0:T(8,128)(2,1)} %key_weight.1) | copy-start | bytes 3538948
  21.6 1.6 %copy-start.5 = (bf16[768,768]{1,0:T(8,128)(2,1)S(1)}, bf16[768,768]{1,0:T(8,128)(2,1)}, u32[]{:S(2)}) copy-start(bf16[768,768]{1,0:T(8,128)(2,1)} %value_weight.1) | copy-start | bytes 3538948
  21.6 21.1 %collective-permute-start.4 = (bf16[4,32,768]{2,1,0:T(8,128)(2,1)S(1)}, bf16[4,32,768]{2,1,0:T(8,128)(2,1)S(1)}, u32[]{:S(2)}, u32[]{:S(2)}) collective-permute-start(bf16[4,32,768]{2,1,0:T(8,128)(2,1)S(1)} %get-tuple-element.31), channel_id=1, source_target_pairs={{0,2},{1,3},{2,0},{3,1},{4,6},{5,7},{6,4},{7,5},{8,10},{9,11},{10,... | collective-permute-start | bytes 589832 | tf_op jit(solution)/shard_map/ppermute | solution.py:346
  23.3 5.6 %copy-start.9 = (f32[768]{0:T(1024)S(1)}, f32[768]{0:T(1024)}, u32[]{:S(2)}) copy-start(f32[768]{0:T(1024)} %param.25) | copy-start | bytes 9220
  23.3 12.6 %copy-start.1 = (bf16[32,32,768]{2,1,0:T(8,128)(2,1)S(1)}, bf16[32,32,768]{2,1,0:T(8,128)(2,1)}, u32[]{:S(2)}) copy-start(bf16[32,32,768]{2,1,0:T(8,128)(2,1)} %own.7) | copy-start | bytes 4718596
  23.3 12.6 %copy-start.2 = (bf16[768,768]{1,0:T(8,128)(2,1)S(1)}, bf16[768,768]{1,0:T(8,128)(2,1)}, u32[]{:S(2)}) copy-start(bf16[768,768]{1,0:T(8,128)(2,1)} %rest_3_.5) | copy-start | bytes 3538948
  23.3 12.6 %copy-start.3 = (bf16[768,768]{1,0:T(8,128)(2,1)S(1)}, bf16[768,768]{1,0:T(8,128)(2,1)}, u32[]{:S(2)}) copy-start(bf16[768,768]{1,0:T(8,128)(2,1)} %rest_4_.5) | copy-start | bytes 3538948
  35.8 24.2 %slice-start.2 = ((s8[4718592]{0:T(1024)(128)(4,1)}), s8[4194304]{0:T(1024)(128)(4,1)S(1)}, s32[]{:S(2)}) async-start(s8[4718592]{0:T(1024)(128)(4,1)} %bitcast.9), calls=%async_computation.3 | async-start | bytes 8388608
  38.9 10.9 %collective-permute-start.2 = (bf16[2,32,768]{2,1,0:T(8,128)(2,1)S(1)}, bf16[2,32,768]{2,1,0:T(8,128)(2,1)S(1)}, u32[]{:S(2)}, u32[]{:S(2)}) collective-permute-start(bf16[2,32,768]{2,1,0:T(8,128)(2,1)S(1)} %get-tuple-element.27), channel_id=1, source_target_pairs={{0,28},{4,24},{8,20},{12,16},{16,12},{20,8},{24,4},{28,0},{1,29},{... | collective-permute-start | bytes 294920 | tf_op jit(solution)/shard_map/ppermute | solution.py:346
  39.5 10.2 %copy-start.10 = (f32[768]{0:T(1024)S(1)}, f32[768]{0:T(1024)}, u32[]{:S(2)}) copy-start(f32[768]{0:T(1024)} %param.28) | copy-start | bytes 9220
  39.5 20.5 %slice-start.3 = ((s8[4718592]{0:T(1024)(128)(4,1)}), s8[524288]{0:T(1024)(128)(4,1)S(1)}, s32[]{:S(2)}) async-start(s8[4718592]{0:T(1024)(128)(4,1)} %bitcast.9), calls=%async_computation.4 | async-start | bytes 1048576
  39.5 10.3 %collective-permute-start.3 = (bf16[2,32,768]{2,1,0:T(8,128)(2,1)S(1)}, bf16[2,32,768]{2,1,0:T(8,128)(2,1)S(1)}, u32[]{:S(2)}, u32[]{:S(2)}) collective-permute-start(bf16[2,32,768]{2,1,0:T(8,128)(2,1)S(1)} %get-tuple-element.28), channel_id=1, source_target_pairs={{0,24},{4,28},{8,16},{12,20},{16,8},{20,12},{24,0},{28,4},{1,25},{... | collective-permute-start | bytes 294920 | tf_op jit(solution)/shard_map/ppermute | solution.py:346
  45.8 14.1 %collective-permute-start.5 = (bf16[2,32,768]{2,1,0:T(8,128)(2,1)S(1)}, bf16[2,32,768]{2,1,0:T(8,128)(2,1)S(1)}, u32[]{:S(2)}, u32[]{:S(2)}) collective-permute-start(bf16[2,32,768]{2,1,0:T(8,128)(2,1)S(1)} %get-tuple-element.32), channel_id=1, source_target_pairs={{0,20},{4,16},{8,28},{12,24},{16,4},{20,0},{24,12},{28,8},{1,21},{... | collective-permute-start | bytes 294920 | tf_op jit(solution)/shard_map/ppermute | solution.py:346
  45.9 14.1 %collective-permute-start.6 = (bf16[2,32,768]{2,1,0:T(8,128)(2,1)S(1)}, bf16[2,32,768]{2,1,0:T(8,128)(2,1)S(1)}, u32[]{:S(2)}, u32[]{:S(2)}) collective-permute-start(bf16[2,32,768]{2,1,0:T(8,128)(2,1)S(1)} %get-tuple-element.33), channel_id=1, source_target_pairs={{0,16},{4,20},{8,24},{12,28},{16,0},{20,4},{24,8},{28,12},{1,17},{... | collective-permute-start | bytes 294920 | tf_op jit(solution)/shard_map/ppermute | solution.py:346
  49.7 10.3 %slice-start = ((s8[4718592]{0:T(1024)(128)(4,1)}), s8[4194304]{0:T(1024)(128)(4,1)S(1)}, s32[]{:S(2)}) async-start(s8[4718592]{0:T(1024)(128)(4,1)} %bitcast.7), calls=%async_computation.1 | async-start | bytes 8388608
  49.7 10.3 %slice-start.1 = ((s8[4718592]{0:T(1024)(128)(4,1)}), s8[524288]{0:T(1024)(128)(4,1)S(1)}, s32[]{:S(2)}) async-start(s8[4718592]{0:T(1024)(128)(4,1)} %bitcast.7), calls=%async_computation.2 | async-start | bytes 1048576
  54.5 8.8 %collective-permute-start.10 = (bf16[2,32,768]{2,1,0:T(8,128)(2,1)S(1)}, bf16[2,32,768]{2,1,0:T(8,128)(2,1)S(1)}, u32[]{:S(2)}, u32[]{:S(2)}) collective-permute-start(bf16[2,32,768]{2,1,0:T(8,128)(2,1)S(1)} %get-tuple-element.38), channel_id=1, source_target_pairs={{0,4},{4,0},{8,12},{12,8},{16,20},{20,16},{24,28},{28,24},{1,5},{5... | collective-permute-start | bytes 294920 | tf_op jit(solution)/shard_map/ppermute | solution.py:346
  55.2 8.2 %collective-permute-start.8 = (bf16[2,32,768]{2,1,0:T(8,128)(2,1)S(1)}, bf16[2,32,768]{2,1,0:T(8,128)(2,1)S(1)}, u32[]{:S(2)}, u32[]{:S(2)}) collective-permute-start(bf16[2,32,768]{2,1,0:T(8,128)(2,1)S(1)} %get-tuple-element.36), channel_id=1, source_target_pairs={{0,12},{4,8},{8,4},{12,0},{16,28},{20,24},{24,20},{28,16},{1,13},{... | collective-permute-start | bytes 294920 | tf_op jit(solution)/shard_map/ppermute | solution.py:346
  60.0 4.6 %copy-start.6 = (bf16[768,2]{0,1:T(2,128)(2,1)S(1)}, bf16[768,2]{0,1:T(2,128)(2,1)}, u32[]{:S(2)}) copy-start(bf16[768,2]{0,1:T(2,128)(2,1)} %param.29) | copy-start | bytes 9220
  60.0 4.6 %copy-start.7 = (s32[16]{0:T(128)S(1)}, s32[16]{0:T(128)}, u32[]{:S(2)}) copy-start(s32[16]{0:T(128)} %get-tuple-element.22.place) | copy-start | bytes 196
  60.0 4.6 %collective-permute-start.9 = (bf16[2,32,768]{2,1,0:T(8,128)(2,1)S(1)}, bf16[2,32,768]{2,1,0:T(8,128)(2,1)S(1)}, u32[]{:S(2)}, u32[]{:S(2)}) collective-permute-start(bf16[2,32,768]{2,1,0:T(8,128)(2,1)S(1)} %get-tuple-element.37), channel_id=1, source_target_pairs={{0,8},{4,12},{8,0},{12,4},{16,24},{20,28},{24,16},{28,20},{1,9},{5... | collective-permute-start | bytes 294920 | tf_op jit(solution)/shard_map/ppermute | solution.py:346

commit v2 on v1

--- a/solution.py
+++ b/solution.py
@@ -9,6 +9,7 @@
 
 HEADS = 12
 IMG_MOST = 2
+PIECES = 4
 CORES = 2
 PACK = 65536
 KEY_PAD = 256
@@ -20,6 +21,7 @@
 
 SMEM = pl.BlockSpec(memory_space=pltpu.SMEM)
 VMEM = pl.BlockSpec(memory_space=pltpu.VMEM)
+ANY = pl.BlockSpec(memory_space=pl.ANY)
 
 
 def params(mib):
@@ -38,7 +40,7 @@
     me = lax.axis_index("img")
     for owner in range(img_count):
         count[owner] = 0
-        for rank in range(IMG_MOST):
+        for rank in range(IMG_MOST if img_count * IMG_MOST > order.shape[0] else 0):
             for column in range(caption_count):
                 table[owner * caption_count + column, rank] = 0
     for row in range(order.shape[0]):
@@ -68,72 +70,87 @@
     )(pairs, order, image_slot, caption_slot)
 
 
-def read_slot(table, cap_count, column, distance, rank, caption_local):
-    verifier = jnp.bitwise_xor(lax.axis_index("img"), distance)
-    entry = table[verifier * cap_count + column, rank]
+def split_entry(entry, caption_local):
     caption = jnp.bitwise_and(entry, PACK - 1)
     owner = caption // caption_local
     return lax.shift_right_logical(entry, 16), owner, caption - owner * caption_local
 
 
-def pick_kernel(step, cap_count, chunks, table, own, sibling, *outs):
+def pick_kernel(step, cap_count, chunks, table, captions, sibling, slots, *rest):
+    outs, own, sems = rest[: len(chunks)], rest[len(chunks)], rest[len(chunks) + 1]
+    piece = own.shape[0] // PIECES
+    copies = []
+    for index in range(PIECES):
+        span = pl.ds(index * piece, piece)
+        copies.append(pltpu.make_async_copy(captions.at[span], own.at[span], sems.at[index]))
+        copies[-1].start()
+    me = lax.axis_index("img")
     mine = lax.axis_index("cap")
     asker = jnp.bitwise_xor(mine, step * CORES)
+    picks = []
     for chunk, out in zip(chunks, outs):
         for index, distance in enumerate(chunk):
+            verifier = jnp.bitwise_xor(me, distance) * cap_count
             for rank in range(IMG_MOST):
-                _, owner, local = read_slot(table, cap_count, asker, distance, rank, own.shape[0])
+                slots[distance * IMG_MOST + rank] = table[verifier + mine, rank]
+                _, owner, local = split_entry(table[verifier + asker, rank], own.shape[0])
                 near = owner == jnp.bitwise_xor(mine, 1)
+                picks.append((out, index * IMG_MOST + rank, near, local))
 
                 @pl.when(near)
                 def _():
                     out[index * IMG_MOST + rank] = sibling[local]
 
-                @pl.when(jnp.logical_not(near))
-                def _():
-                    out[index * IMG_MOST + rank] = own[local]
+    for copy in copies:
+        copy.wait()
+    for out, spot, near, local in picks:
+
+        @pl.when(jnp.logical_not(near))
+        def _():
+            out[spot] = own[local]
 
 
 def pick_blocks(step, cap_count, chunks, table, own, sibling):
+    slot_count = sum(len(chunk) for chunk in chunks) * IMG_MOST
     outs = tuple(
         jax.ShapeDtypeStruct((len(chunk) * IMG_MOST,) + own.shape[1:], own.dtype) for chunk in chunks
     )
     return pl.pallas_call(
         functools.partial(pick_kernel, step, cap_count, chunks),
-        out_shape=outs,
-        in_specs=[SMEM, VMEM, VMEM],
-        out_specs=(VMEM,) * len(outs),
+        out_shape=(jax.ShapeDtypeStruct((slot_count,), jnp.int32),) + outs,
+        in_specs=[SMEM, ANY, VMEM],
+        out_specs=(SMEM,) + (VMEM,) * len(outs),
+        scratch_shapes=[pltpu.VMEM(own.shape, own.dtype), pltpu.SemaphoreType.DMA((PIECES,))],
         compiler_params=params(8),
-        cost_estimate=pl.CostEstimate(flops=0, bytes_accessed=1 << 20, transcendentals=0),
+        cost_estimate=SMALL,
         name="pick_captions",
     )(table, own, sibling)
 
 
 def project_kernel(images, key_weight, value_weight, keys, values):
-    rows = images.shape[1]
-    patches = images[0]
-    for weight, out in ((key_weight, keys), (value_weight, values)):
-        out[0, rows // 16 * 16 :, :] = jnp.zeros((KEY_PAD - rows // 16 * 16, out.shape[2]), BF16)
-        out[0, :rows, :] = jnp.dot(patches, weight[...], preferred_element_type=F32).astype(BF16)
+    count, rows, width = images.shape
+    whole = rows // 16 * 16
+    for image in range(count):
+        for weight, out in ((key_weight, keys), (value_weight, values)):
+            out[image, whole:, :] = jnp.zeros((KEY_PAD - whole, width), BF16)
+            out[image, :rows, :] = jnp.dot(images[image], weight[...], preferred_element_type=F32).astype(BF16)
 
 
 def project_images(images, key_weight, value_weight):
     count, rows, width = images.shape
-    whole = pl.BlockSpec((width, width), lambda i: (0, 0))
     out = jax.ShapeDtypeStruct((count, KEY_PAD, width), BF16)
     return pl.pallas_call(
         project_kernel,
         out_shape=(out, out),
-        grid=(count,),
-        in_specs=[pl.BlockSpec((1, rows, width), lambda i: (i, 0, 0)), whole, whole],
-        out_specs=(pl.BlockSpec((1, KEY_PAD, width), lambda i: (i, 0, 0)),) * 2,
+        in_specs=[VMEM] * 3,
+        out_specs=(VMEM, VMEM),
         compiler_params=params(16),
         cost_estimate=SMALL,
         name="project_images",
     )(images, key_weight, value_weight)
 
 
-def attend_kernel(key_rows, cap_count, far_count, chunk, table, own, sibling, *rest):
+def attend_kernel(key_rows, far_count, chunk, slots, own, sibling, *rest):
     far = rest[:far_count]
     keys, values, query_weight, out_weight, gain = rest[far_count : far_count + 5]
     outs = rest[far_count + 5 : far_count + 5 + len(chunk)]
@@ -145,9 +162,8 @@
     pair_count = len(chunk) * IMG_MOST
     images = []
     for pair in range(pair_count):
-        image, owner, local = read_slot(
-            table, cap_count, column, chunk[pair // IMG_MOST], pair % IMG_MOST, own.shape[0]
-        )
+        entry = slots[chunk[pair // IMG_MOST] * IMG_MOST + pair % IMG_MOST]
+        image, owner, local = split_entry(entry, own.shape[0])
         images.append(image)
         apart = jnp.bitwise_xor(owner, column)
 
@@ -203,23 +219,21 @@
                 joined = jnp.where(lane_head == head, mixed[head * tokens : (head + 1) * tokens], joined)
             context[pair * tokens : (pair + 1) * tokens, span] = joined.astype(BF16)
 
-    found = score(0)
+    every = [score(pair) for pair in range(pair_count)]
     for pair in range(pair_count):
-        later = score(pair + 1) if pair + 1 < pair_count else None
-        mix(pair, found)
-        found = later
+        mix(pair, every[pair])
     hidden = flat.astype(F32) + jnp.dot(context[...], out_weight[...], preferred_element_type=F32)
     hidden = norm_rows(hidden, gain[...]).astype(BF16).reshape(pair_count, tokens, width)
     for index, out in enumerate(outs):
         out[...] = hidden[index * IMG_MOST : (index + 1) * IMG_MOST]
 
 
-def attend(key_rows, cap_count, chunk, table, own, sibling, far, keys, values, query_weight, out_weight, gain):
+def attend(key_rows, chunk, slots, own, sibling, far, keys, values, query_weight, out_weight, gain):
     tokens, width = own.shape[1:]
     pair_count = len(chunk) * IMG_MOST
     rows = pair_count * tokens
     return pl.pallas_call(
-        functools.partial(attend_kernel, key_rows, cap_count, len(far), chunk),
+        functools.partial(attend_kernel, key_rows, len(far), chunk),
         out_shape=(jax.ShapeDtypeStruct((IMG_MOST, tokens, width), BF16),) * len(chunk),
         in_specs=[SMEM] + [VMEM] * (7 + len(far)),
         out_specs=(VMEM,) * len(chunk),
@@ -231,7 +245,7 @@
         compiler_params=params(16),
         cost_estimate=SMALL,
         name="attend",
-    )(table, own, sibling, *far, keys, values, query_weight, out_weight, gain)
+    )(slots, own, sibling, *far, keys, values, query_weight, out_weight, gain)
 
 
 TILES = 3
@@ -336,10 +350,10 @@
     img_count = lax.axis_size("img")
     cap_count = lax.axis_size("cap")
     far_steps = range(1, cap_count // CORES)
-    half, quarter = img_count // 2, img_count // 4
-    distances = tuple(range(img_count - 1, -1, -1))
-    first_parts, last_parts = distances[:half], distances[half:]
-    chunks = (distances[:quarter], distances[quarter:half], distances[half:])
+    half = img_count // 2
+    chunks = tuple((img_count - 1 - index, index) for index in range(half))
+    first_parts = sum(chunks[: half // 2], ())
+    last_parts = sum(chunks[half // 2 :], ())
 
     def swap(array, axis, distance):
         size = lax.axis_size(axis)
@@ -351,24 +365,33 @@
     )
     table = lax.all_to_all(table, ("img", "cap"), split_axis=0, concat_axis=0, tiled=True)
     keys, values = project_images(images, key_weight, value_weight)
+    pinned = pltpu.with_memory_space_constraint(captions, pltpu.HBM)
     far = [[] for _ in chunks]
     for step in far_steps:
-        picked = pick_blocks(step, cap_count, chunks, table, captions, sibling)
+        slots, *picked = pick_blocks(step, cap_count, chunks, table, pinned, sibling)
         for blocks, block in zip(far, picked):
-            blocks.append(swap(block, "cap", step * CORES))
+            blocks.append(block)
     gain_attn = gain_attn.reshape(1, -1)
     gain_ffn = gain_ffn.reshape(1, -1)
     hidden = {}
+
+    def after(value, parts):
+        value, found = lax.optimization_barrier((value, [hidden[part] for part in parts]))
+        hidden.update(zip(parts, found))
+        return value
+
+    def fetch(index):
+        far[index] = [swap(block, "cap", step * CORES) for step, block in zip(far_steps, far[index])]
+
+    fetch(0)
+    fetch(1)
     for index, chunk in enumerate(chunks):
-        if index == 2:
-            sent = [hidden[distance] for distance in chunks[0]]
-            table, sent = lax.optimization_barrier((table, sent))
-            hidden.update(zip(chunks[0], sent))
+        if index >= 2:
+            slots = after(slots, chunks[index - 2])
         blocks = attend(
             images.shape[1],
-            cap_count,
             chunk,
-            table,
+            slots,
             captions,
             sibling,
             far[index],
@@ -378,8 +401,13 @@
             out_weight,
             gain_attn,
         )
+        if index == 0:
+            blocks, far[2:] = lax.optimization_barrier((blocks, far[2:]))
+            for later in range(2, len(chunks)):
+                fetch(later)
         for distance, block in zip(chunk, blocks):
             hidden[distance] = swap(block, "img", distance) if distance else block
+    gain_ffn = after(gain_ffn, sum(chunks[:-1], ()))
     earlier = feed_first([hidden[part] for part in first_parts], gain_ffn, in_weight, back_weight)
     merged, logits = feed_last(
         first_parts,

time: 69.5 us -> 59.4 us (0.85)
  waiting for transfers between devices: 8.23 us -> 1.89 us
  starting transfers between devices: 16.3 us -> 14 us
  local copies, waits for them, and re-layouts: 2.56 us -> 1.07 us
    ppermute x11 -> x12, waiting for transfers between devices: 8.23 us -> 1.89 us  [swap(): lax.ppermute(array, axis, [(peer, peer ^ distance) for peer in range(size)])]
    ppermute x11 -> x12, starting transfers between devices: 16.3 us -> 14 us  [swap(): lax.ppermute(array, axis, [(peer, peer ^ distance) for peer in range(size)])]
    pallas_call x4 -> x5, Pallas kernels: 16.4 us -> 14.4 us  [the longest x4 10.1 us: attend(): pl.pallas_call(functools.partial(attend_kernel, key_rows, len(far), chunk...]
    pallas_call x1, Pallas kernels: 1.13 us -> 2.9 us  [pick_blocks(): pl.pallas_call(functools.partial(pick_kernel, step, cap_count, chunks), o...]
    unnamed x31 -> x29, local copies, waits for them, and re-layouts: 2.55 us -> 1.06 us
  transfers between devices with their start and end apart: 11 -> 12, of which waited for: 2 -> 3; matrix products, arithmetic and copies ran while one was open for 1% -> 1% of each run, Pallas kernels for 31% -> 33%
where the time goes in v2:
time: 59.4 us; the launch traced here: 58.9 us
  Pallas kernels  27 us (45%)
  blocking collectives  14.1 us (24%)
  starting transfers between devices  14 us (24%)
  waiting for transfers between devices  1.89 us (3%)
  local copies, waits for them, and re-layouts  1.07 us (2%)
  between operations  0.85 us (1%)
    all_to_all x1, blocking collectives, body(): lax.all_to_all(table, ('img', 'cap'), split_axis=0, concat_axis=0, tiled=...  14.1 us
    ppermute x12, starting transfers between devices, swap(): lax.ppermute(array, axis, [(peer, peer ^ distance) for peer in range(size)])  14 us
    pallas_call x4, Pallas kernels, attend(): pl.pallas_call(functools.partial(attend_kernel, key_rows, len(far), chunk...  10.1 us
    pallas_call x1, Pallas kernels, feed_last(): pl.pallas_call(functools.partial(feed_last_kernel, first_parts, last_part...  4.72 us
    pallas_call x1, Pallas kernels, project_images(): pl.pallas_call(project_kernel, out_shape=(out, out), in_specs=[VMEM] * 3,...  4.22 us
    pallas_call x1, Pallas kernels, feed_first(): pl.pallas_call(feed_first_kernel, out_shape=jax.ShapeDtypeStruct((slots,...  3.29 us
    pallas_call x1, Pallas kernels, pick_blocks(): pl.pallas_call(functools.partial(pick_kernel, step, cap_count, chunks), o...  2.9 us
    ppermute x12, waiting for transfers between devices, swap(): lax.ppermute(array, axis, [(peer, peer ^ distance) for peer in range(size)])  1.89 us
  transfers between devices with their start and end apart: 12, of which 3 were waited for; matrix products, arithmetic and copies ran while one was open for 1% of the time, Pallas kernels for 33%

profile of v2, /device:TPU:0, one launch (start us, length us, event | category | flops | bytes accessed | tf_op | source)
XLA Modules:
  0.0 58.9 jit_solution(973756702949339348)
XLA Ops:
  0.6 0.5 collective-permute-start
  1.1 1.8 %slot_table.1 = (s32[32,128]{1,0:T(8,128)}, s32[16]{0:T(128)}) custom-call(s32[2,512]{1,0:T(2,128)} %bitcast.14, s32[16]{0:T(128)} %order.1, s32[64]{0:T(128)} %image_slot.1, s32[128]{0:T(128)} %caption_slot.1), custom_call_target="tpu_custom_call" | custom-call | tf_op jit(solution)/shard_map/slot_table/pallas_call | solution.py:60
  2.9 0.0 copy-start.7
  2.9 14.1 %all_to_all.11 = s32[32,1,128]{2,1,0:T(1,128)S(1)} all-to-all(s32[32,1,128]{2,1,0:T(1,128)} %bitcast.13), channel_id=1, replica_groups=mesh['img'=8,'cap'=4] {'img','cap'}, dimensions={0} | all-to-all | bytes 32768 | tf_op jit(solution)/shard_map/all_to_all | solution.py:366
  17.0 0.0 collective-permute-done.sibling
  17.0 2.9 %pick_captions.1 = (s32[16]{0:T(128)S(1)}, bf16[4,32,768]{2,1,0:T(8,128)(2,1)S(1)}, bf16[4,32,768]{2,1,0:T(8,128)(2,1)S(1)}, bf16[4,32,768]{2,1,0:T(8,128)(2,1)S(1)}, bf16[4,32,768]{2,1,0:T(8,128)(2,1)S(1)}) custom-call(s32[32,128]{1,0:T(8,128)S(1)} %bitcast.11, bf16[32,32,768]{2,1,0:T(8,128)(2,1)} %own.7, bf16[32,32,768]{2,1,0:T(8,128)(2,1)S(1)} %collective-permute-done.sibling), custom_call_target="tpu_custom_call" | custom-call | flops 65536 | bytes 1024 | tf_op jit(solution)/shard_map/pick_captions/pallas_call | solution.py:118
  19.9 0.0 copy-start.3
  19.9 0.0 copy-start.4
  19.9 0.6 %collective-permute-start.1 = (bf16[4,32,768]{2,1,0:T(8,128)(2,1)S(1)}, bf16[4,32,768]{2,1,0:T(8,128)(2,1)S(1)}, u32[]{:S(2)}, u32[]{:S(2)}) collective-permute-start(bf16[4,32,768]{2,1,0:T(8,128)(2,1)S(1)} %get-tuple-element.41), channel_id=1, source_target_pairs={{0,2},{1,3},{2,0},{3,1},{4,6},{5,7},{6,4},{7,5},{8,10},{9,11},{10,... | collective-permute-start | bytes 589832 | tf_op jit(solution)/shard_map/ppermute | solution.py:360
  20.5 0.0 copy-done.7
  20.5 0.5 copy.19.images
  21.0 0.2 copy-done.3
  21.2 0.4 copy-done.4
  21.5 0.0 copy-start.8
  21.5 0.0 copy-start
  21.5 0.0 copy-start.1
  21.5 0.0 copy-start.2
  21.5 4.2 %project_images.1 = (bf16[8,256,768]{2,1,0:T(8,128)(2,1)S(1)}, bf16[8,256,768]{2,1,0:T(8,128)(2,1)S(1)}) custom-call(bf16[8,197,768]{2,1,0:T(8,128)(2,1)S(1)} %copy.19.images, bf16[768,768]{1,0:T(8,128)(2,1)S(1)} %copy-done.3, bf16[768,768]{1,0:T(8,128)(2,1)S(1)} %copy-done.4), custom_call_target="tpu_custom_call" | custom-call | flops 65536 | bytes 1024 | tf_op jit(solution)/shard_map/project_images/pallas_call | solution.py:142
  25.8 0.0 copy-done.8
  25.8 1.1 %collective-permute-start.3 = (bf16[4,32,768]{2,1,0:T(8,128)(2,1)S(1)}, bf16[4,32,768]{2,1,0:T(8,128)(2,1)S(1)}, u32[]{:S(2)}, u32[]{:S(2)}) collective-permute-start(bf16[4,32,768]{2,1,0:T(8,128)(2,1)S(1)} %get-tuple-element.53), channel_id=1, source_target_pairs={{0,2},{1,3},{2,0},{3,1},{4,6},{5,7},{6,4},{7,5},{8,10},{9,11},{10,... | collective-permute-start | bytes 589832 | tf_op jit(solution)/shard_map/ppermute | solution.py:360
  26.9 0.0 collective-permute-done.1.rest_0_
  26.9 0.0 copy-done
  26.9 0.0 copy-done.1
  26.9 0.0 copy-done.2
  26.9 2.5 %attend.4 = (bf16[2,32,768]{2,1,0:T(8,128)(2,1)S(1)}, bf16[2,32,768]{2,1,0:T(8,128)(2,1)S(1)}) custom-call(s32[16]{0:T(128)S(1)} %get-tuple-element.68.slots, bf16[32,32,768]{2,1,0:T(8,128)(2,1)S(1)} %copy-done, bf16[32,32,768]{2,1,0:T(8,128)(2,1)S(1)} %collective-permute-done.sibling, bf16[4,32,768]{2,1,0:T(8,128)(2,1)S(1)} %collective-permute-done.1.rest_0_, ...), custom_call_target="tpu_custom_call" | custom-call | flops 65536 | bytes 1024 | tf_op jit(solution)/shard_map/attend/pallas_call | solution.py:235
  29.4 1.1 %collective-permute-start.6 = (bf16[4,32,768]{2,1,0:T(8,128)(2,1)S(1)}, bf16[4,32,768]{2,1,0:T(8,128)(2,1)S(1)}, u32[]{:S(2)}, u32[]{:S(2)}) collective-permute-start(bf16[4,32,768]{2,1,0:T(8,128)(2,1)S(1)} %get-tuple-element.58), channel_id=1, source_target_pairs={{0,2},{1,3},{2,0},{3,1},{4,6},{5,7},{6,4},{7,5},{8,10},{9,11},{10,... | collective-permute-start | bytes 589832 | tf_op jit(solution)/shard_map/ppermute | solution.py:360
  30.5 0.6 collective-permute-start.2
  31.0 1.0 %collective-permute-start.9 = (bf16[4,32,768]{2,1,0:T(8,128)(2,1)S(1)}, bf16[4,32,768]{2,1,0:T(8,128)(2,1)S(1)}, u32[]{:S(2)}, u32[]{:S(2)}) collective-permute-start(bf16[4,32,768]{2,1,0:T(8,128)(2,1)S(1)} %get-tuple-element.69), channel_id=1, source_target_pairs={{0,2},{1,3},{2,0},{3,1},{4,6},{5,7},{6,4},{7,5},{8,10},{9,11},{10,... | collective-permute-start | bytes 589832 | tf_op jit(solution)/shard_map/ppermute | solution.py:360
  32.0 1.6 %collective-permute-done.3.rest_0_ = bf16[4,32,768]{2,1,0:T(8,128)(2,1)S(1)} collective-permute-done((bf16[4,32,768]{2,1,0:T(8,128)(2,1)S(1)}, bf16[4,32,768]{2,1,0:T(8,128)(2,1)S(1)}, u32[]{:S(2)}, u32[]{:S(2)}) %collective-permute-start.3) | collective-permute-done | bytes 196640 | tf_op jit(solution)/shard_map/ppermute | solution.py:360
  33.6 0.0 slice-start.2
  33.6 2.5 %attend.5 = (bf16[2,32,768]{2,1,0:T(8,128)(2,1)S(1)}, bf16[2,32,768]{2,1,0:T(8,128)(2,1)S(1)}) custom-call(s32[16]{0:T(128)S(1)} %get-tuple-element.68.slots, bf16[32,32,768]{2,1,0:T(8,128)(2,1)S(1)} %copy-done, bf16[32,32,768]{2,1,0:T(8,128)(2,1)S(1)} %collective-permute-done.sibling, bf16[4,32,768]{2,1,0:T(8,128)(2,1)S(1)} %collective-permute-done.3.rest_0_, ...), custom_call_target="tpu_custom_call" | custom-call | flops 65536 | bytes 1024 | tf_op jit(solution)/shard_map/attend/pallas_call | solution.py:235
  36.1 1.7 %collective-permute-start.4 = (bf16[2,32,768]{2,1,0:T(8,128)(2,1)S(1)}, bf16[2,32,768]{2,1,0:T(8,128)(2,1)S(1)}, u32[]{:S(2)}, u32[]{:S(2)}) collective-permute-start(bf16[2,32,768]{2,1,0:T(8,128)(2,1)S(1)} %get-tuple-element.54), channel_id=1, source_target_pairs={{0,24},{4,28},{8,16},{12,20},{16,8},{20,12},{24,0},{28,4},{1,25},{... | collective-permute-start | bytes 294920 | tf_op jit(solution)/shard_map/ppermute | solution.py:360
  37.9 0.0 copy-start.9
  37.9 0.0 slice-start.3
  37.9 1.5 %collective-permute-start.5 = (bf16[2,32,768]{2,1,0:T(8,128)(2,1)S(1)}, bf16[2,32,768]{2,1,0:T(8,128)(2,1)S(1)}, u32[]{:S(2)}, u32[]{:S(2)}) collective-permute-start(bf16[2,32,768]{2,1,0:T(8,128)(2,1)S(1)} %get-tuple-element.55), channel_id=1, source_target_pairs={{0,4},{4,0},{8,12},{12,8},{16,20},{20,16},{24,28},{28,24},{1,5},{5... | collective-permute-start | bytes 294920 | tf_op jit(solution)/shard_map/ppermute | solution.py:360
  39.3 0.0 collective-permute-done.2.rest_0_
  39.3 0.0 collective-permute-done.6.rest_0_
  39.3 2.5 %attend.6 = (bf16[2,32,768]{2,1,0:T(8,128)(2,1)S(1)}, bf16[2,32,768]{2,1,0:T(8,128)(2,1)S(1)}) custom-call(s32[16]{0:T(128)S(1)} %get-tuple-element.68.slots, bf16[32,32,768]{2,1,0:T(8,128)(2,1)S(1)} %copy-done, bf16[32,32,768]{2,1,0:T(8,128)(2,1)S(1)} %collective-permute-done.sibling, bf16[4,32,768]{2,1,0:T(8,128)(2,1)S(1)} %collective-permute-done.6.rest_0_, ...), custom_call_target="tpu_custom_call" | custom-call | flops 65536 | bytes 1024 | tf_op jit(solution)/shard_map/attend/pallas_call | solution.py:235
  41.8 0.3 collective-permute-start.7
  42.2 2.5 %collective-permute-start.8 = (bf16[2,32,768]{2,1,0:T(8,128)(2,1)S(1)}, bf16[2,32,768]{2,1,0:T(8,128)(2,1)S(1)}, u32[]{:S(2)}, u32[]{:S(2)}) collective-permute-start(bf16[2,32,768]{2,1,0:T(8,128)(2,1)S(1)} %get-tuple-element.60), channel_id=1, source_target_pairs={{0,8},{4,12},{8,0},{12,4},{16,24},{20,28},{24,16},{28,20},{1,9},{5... | collective-permute-start | bytes 294920 | tf_op jit(solution)/shard_map/ppermute | solution.py:360
  44.6 0.0 copy-done.9
  44.6 0.0 slice-start
  44.6 0.0 slice-start.1
  44.6 0.0 collective-permute-done.4.rest_2_
  44.7 0.0 collective-permute-done.5.rest_3_
  44.7 0.0 collective-permute-done.9.rest_0_
  44.7 2.7 %attend.7 = (bf16[2,32,768]{2,1,0:T(8,128)(2,1)S(1)}, bf16[2,32,768]{2,1,0:T(8,128)(2,1)S(1)}) custom-call(s32[16]{0:T(128)S(1)} %get-tuple-element.68.slots, bf16[32,32,768]{2,1,0:T(8,128)(2,1)S(1)} %copy-done, bf16[32,32,768]{2,1,0:T(8,128)(2,1)S(1)} %collective-permute-done.sibling, bf16[4,32,768]{2,1,0:T(8,128)(2,1)S(1)} %collective-permute-done.9.rest_0_, ...), custom_call_target="tpu_custom_call" | custom-call | flops 65536 | bytes 1024 | tf_op jit(solution)/shard_map/attend/pallas_call | solution.py:235
  47.4 0.3 collective-permute-start.10
  47.6 0.0 copy-start.5
  47.6 0.0 copy-start.6
  47.6 2.9 %collective-permute-start.11 = (bf16[2,32,768]{2,1,0:T(8,128)(2,1)S(1)}, bf16[2,32,768]{2,1,0:T(8,128)(2,1)S(1)}, u32[]{:S(2)}, u32[]{:S(2)}) collective-permute-start(bf16[2,32,768]{2,1,0:T(8,128)(2,1)S(1)} %get-tuple-element.71), channel_id=1, source_target_pairs={{0,12},{4,8},{8,4},{12,0},{16,28},{20,24},{24,20},{28,16},{1,13},{... | collective-permute-start | bytes 294920 | tf_op jit(solution)/shard_map/ppermute | solution.py:360
  50.6 0.2 collective-permute-done.7.rest_0_
  50.7 0.0 collective-permute-done.8.rest_1_
  50.7 0.0 slice-done.2
  50.7 0.0 slice-done.3
  50.7 0.0 slice-done
  50.7 0.0 slice-done.1
  50.8 3.3 %feed_first.1.earlier = bf16[8,32,768]{2,1,0:T(8,128)(2,1)S(1)} custom-call(f32[1,768]{1,0:T(1,128)S(1)} %reshape.12.gain, bf16[768,3072]{1,0:T(8,128)(2,1)S(1)} %bitcast.8, bf16[3072,768]{1,0:T(8,128)(2,1)S(1)} %bitcast.10, bf16[2,32,768]{2,1,0:T(8,128)(2,1)S(1)} %collective-permute-done.2.rest_0_, bf16[2,32,768]{2,1,0:T(8,128)(2,1)S(1)} %get-tuple-element.63.rest_1_, ...), custom_call_target="tpu_custom_call" | custom-call | flops 2415919104 | bytes 9437184 | tf_op jit(solution)/shard_map/feed_first/pallas_call | solution.py:303
  54.1 0.0 collective-permute-done.10.rest_2_
  54.1 0.1 collective-permute-done.11.rest_3_
  54.2 0.0 copy-done.5
  54.2 0.0 copy-done.6
  54.2 4.7 %feed_last.1 = (bf16[16,32,768]{2,1,0:T(8,128)(2,1)}, f32[2,16]{1,0:T(2,128)}) custom-call(s32[16]{0:T(128)S(1)} %copy-done.6, f32[1,768]{1,0:T(1,128)S(1)} %reshape.12.gain, bf16[2,768]{1,0:T(2,128)(2,1)S(1)} %bitcast.12, bf16[768,3072]{1,0:T(8,128)(2,1)S(1)} %bitcast.8, bf16[3072,768]{1,0:T(8,128)(2,1)S(1)} %bitcast.10, ...), custom_call_target="tpu_custom_call" | custom-call | flops 2415919104 | bytes 9437184 | tf_op jit(solution)/shard_map/feed_last/pallas_call | solution.py:318
  (4 shorter events, 0.0 us)
Async XLA Ops:
  0.6 16.4 %collective-permute-start = (bf16[32,32,768]{2,1,0:T(8,128)(2,1)}, bf16[32,32,768]{2,1,0:T(8,128)(2,1)S(1)}, u32[]{:S(2)}, u32[]{:S(2)}) collective-permute-start(bf16[32,32,768]{2,1,0:T(8,128)(2,1)} %own.7), channel_id=1, source_target_pairs={{0,1},{1,0},{2,3},{3,2},{4,5},{5,4},{6,7},{7,6},{8,9},{9,8},{10,11... | collective-permute-start | bytes 4718600 | tf_op jit(solution)/shard_map/ppermute | solution.py:360
  2.9 17.6 %copy-start.7 = (bf16[8,197,768]{2,0,1:T(8,128)(2,1)S(1)}, bf16[8,197,768]{2,0,1:T(8,128)(2,1)}, u32[]{:S(2)}) copy-start(bf16[8,197,768]{2,0,1:T(8,128)(2,1)} %param.19) | copy-start | bytes 7262212
  19.9 1.3 %copy-start.3 = (bf16[768,768]{1,0:T(8,128)(2,1)S(1)}, bf16[768,768]{1,0:T(8,128)(2,1)}, u32[]{:S(2)}) copy-start(bf16[768,768]{1,0:T(8,128)(2,1)} %key_weight.1) | copy-start | bytes 3538948
  19.9 1.6 %copy-start.4 = (bf16[768,768]{1,0:T(8,128)(2,1)S(1)}, bf16[768,768]{1,0:T(8,128)(2,1)}, u32[]{:S(2)}) copy-start(bf16[768,768]{1,0:T(8,128)(2,1)} %value_weight.1) | copy-start | bytes 3538948
  19.9 6.9 %collective-permute-start.1 = (bf16[4,32,768]{2,1,0:T(8,128)(2,1)S(1)}, bf16[4,32,768]{2,1,0:T(8,128)(2,1)S(1)}, u32[]{:S(2)}, u32[]{:S(2)}) collective-permute-start(bf16[4,32,768]{2,1,0:T(8,128)(2,1)S(1)} %get-tuple-element.41), channel_id=1, source_target_pairs={{0,2},{1,3},{2,0},{3,1},{4,6},{5,7},{6,4},{7,5},{8,10},{9,11},{10,... | collective-permute-start | bytes 589832 | tf_op jit(solution)/shard_map/ppermute | solution.py:360
  21.5 4.2 %copy-start.8 = (f32[768]{0:T(1024)S(1)}, f32[768]{0:T(1024)}, u32[]{:S(2)}) copy-start(f32[768]{0:T(1024)} %param.25) | copy-start | bytes 9220
  21.5 5.3 %copy-start = (bf16[32,32,768]{2,1,0:T(8,128)(2,1)S(1)}, bf16[32,32,768]{2,1,0:T(8,128)(2,1)}, u32[]{:S(2)}) copy-start(bf16[32,32,768]{2,1,0:T(8,128)(2,1)} %own.7) | copy-start | bytes 4718596
  21.5 5.3 %copy-start.1 = (bf16[768,768]{1,0:T(8,128)(2,1)S(1)}, bf16[768,768]{1,0:T(8,128)(2,1)}, u32[]{:S(2)}) copy-start(bf16[768,768]{1,0:T(8,128)(2,1)} %rest_3_.7) | copy-start | bytes 3538948
  21.5 5.3 %copy-start.2 = (bf16[768,768]{1,0:T(8,128)(2,1)S(1)}, bf16[768,768]{1,0:T(8,128)(2,1)}, u32[]{:S(2)}) copy-start(bf16[768,768]{1,0:T(8,128)(2,1)} %rest_4_.7) | copy-start | bytes 3538948
  25.8 7.8 %collective-permute-start.3 = (bf16[4,32,768]{2,1,0:T(8,128)(2,1)S(1)}, bf16[4,32,768]{2,1,0:T(8,128)(2,1)S(1)}, u32[]{:S(2)}, u32[]{:S(2)}) collective-permute-start(bf16[4,32,768]{2,1,0:T(8,128)(2,1)S(1)} %get-tuple-element.53), channel_id=1, source_target_pairs={{0,2},{1,3},{2,0},{3,1},{4,6},{5,7},{6,4},{7,5},{8,10},{9,11},{10,... | collective-permute-start | bytes 589832 | tf_op jit(solution)/shard_map/ppermute | solution.py:360
  29.4 10.0 %collective-permute-start.6 = (bf16[4,32,768]{2,1,0:T(8,128)(2,1)S(1)}, bf16[4,32,768]{2,1,0:T(8,128)(2,1)S(1)}, u32[]{:S(2)}, u32[]{:S(2)}) collective-permute-start(bf16[4,32,768]{2,1,0:T(8,128)(2,1)S(1)} %get-tuple-element.58), channel_id=1, source_target_pairs={{0,2},{1,3},{2,0},{3,1},{4,6},{5,7},{6,4},{7,5},{8,10},{9,11},{10,... | collective-permute-start | bytes 589832 | tf_op jit(solution)/shard_map/ppermute | solution.py:360
  30.5 8.9 %collective-permute-start.2 = (bf16[2,32,768]{2,1,0:T(8,128)(2,1)S(1)}, bf16[2,32,768]{2,1,0:T(8,128)(2,1)S(1)}, u32[]{:S(2)}, u32[]{:S(2)}) collective-permute-start(bf16[2,32,768]{2,1,0:T(8,128)(2,1)S(1)} %get-tuple-element.48), channel_id=1, source_target_pairs={{0,28},{4,24},{8,20},{12,16},{16,12},{20,8},{24,4},{28,0},{1,29},{... | collective-permute-start | bytes 294920 | tf_op jit(solution)/shard_map/ppermute | solution.py:360
  31.0 13.6 %collective-permute-start.9 = (bf16[4,32,768]{2,1,0:T(8,128)(2,1)S(1)}, bf16[4,32,768]{2,1,0:T(8,128)(2,1)S(1)}, u32[]{:S(2)}, u32[]{:S(2)}) collective-permute-start(bf16[4,32,768]{2,1,0:T(8,128)(2,1)S(1)} %get-tuple-element.69), channel_id=1, source_target_pairs={{0,2},{1,3},{2,0},{3,1},{4,6},{5,7},{6,4},{7,5},{8,10},{9,11},{10,... | collective-permute-start | bytes 589832 | tf_op jit(solution)/shard_map/ppermute | solution.py:360
  33.6 17.1 %slice-start.2 = ((s8[4718592]{0:T(1024)(128)(4,1)}), s8[4194304]{0:T(1024)(128)(4,1)S(1)}, s32[]{:S(2)}) async-start(s8[4718592]{0:T(1024)(128)(4,1)} %bitcast.9), calls=%async_computation.3 | async-start | bytes 8388608
  36.1 8.5 %collective-permute-start.4 = (bf16[2,32,768]{2,1,0:T(8,128)(2,1)S(1)}, bf16[2,32,768]{2,1,0:T(8,128)(2,1)S(1)}, u32[]{:S(2)}, u32[]{:S(2)}) collective-permute-start(bf16[2,32,768]{2,1,0:T(8,128)(2,1)S(1)} %get-tuple-element.54), channel_id=1, source_target_pairs={{0,24},{4,28},{8,16},{12,20},{16,8},{20,12},{24,0},{28,4},{1,25},{... | collective-permute-start | bytes 294920 | tf_op jit(solution)/shard_map/ppermute | solution.py:360
  37.9 6.8 %copy-start.9 = (f32[768]{0:T(1024)S(1)}, f32[768]{0:T(1024)}, u32[]{:S(2)}) copy-start(f32[768]{0:T(1024)} %param.28) | copy-start | bytes 9220
  37.9 12.9 %slice-start.3 = ((s8[4718592]{0:T(1024)(128)(4,1)}), s8[524288]{0:T(1024)(128)(4,1)S(1)}, s32[]{:S(2)}) async-start(s8[4718592]{0:T(1024)(128)(4,1)} %bitcast.9), calls=%async_computation.4 | async-start | bytes 1048576
  37.9 6.8 %collective-permute-start.5 = (bf16[2,32,768]{2,1,0:T(8,128)(2,1)S(1)}, bf16[2,32,768]{2,1,0:T(8,128)(2,1)S(1)}, u32[]{:S(2)}, u32[]{:S(2)}) collective-permute-start(bf16[2,32,768]{2,1,0:T(8,128)(2,1)S(1)} %get-tuple-element.55), channel_id=1, source_target_pairs={{0,4},{4,0},{8,12},{12,8},{16,20},{20,16},{24,28},{28,24},{1,5},{5... | collective-permute-start | bytes 294920 | tf_op jit(solution)/shard_map/ppermute | solution.py:360
  41.8 8.9 %collective-permute-start.7 = (bf16[2,32,768]{2,1,0:T(8,128)(2,1)S(1)}, bf16[2,32,768]{2,1,0:T(8,128)(2,1)S(1)}, u32[]{:S(2)}, u32[]{:S(2)}) collective-permute-start(bf16[2,32,768]{2,1,0:T(8,128)(2,1)S(1)} %get-tuple-element.59), channel_id=1, source_target_pairs={{0,20},{4,16},{8,28},{12,24},{16,4},{20,0},{24,12},{28,8},{1,21},{... | collective-permute-start | bytes 294920 | tf_op jit(solution)/shard_map/ppermute | solution.py:360
  42.2 8.5 %collective-permute-start.8 = (bf16[2,32,768]{2,1,0:T(8,128)(2,1)S(1)}, bf16[2,32,768]{2,1,0:T(8,128)(2,1)S(1)}, u32[]{:S(2)}, u32[]{:S(2)}) collective-permute-start(bf16[2,32,768]{2,1,0:T(8,128)(2,1)S(1)} %get-tuple-element.60), channel_id=1, source_target_pairs={{0,8},{4,12},{8,0},{12,4},{16,24},{20,28},{24,16},{28,20},{1,9},{5... | collective-permute-start | bytes 294920 | tf_op jit(solution)/shard_map/ppermute | solution.py:360
  44.6 6.1 %slice-start = ((s8[4718592]{0:T(1024)(128)(4,1)}), s8[4194304]{0:T(1024)(128)(4,1)S(1)}, s32[]{:S(2)}) async-start(s8[4718592]{0:T(1024)(128)(4,1)} %bitcast.7), calls=%async_computation.1 | async-start | bytes 8388608
  44.6 6.1 %slice-start.1 = ((s8[4718592]{0:T(1024)(128)(4,1)}), s8[524288]{0:T(1024)(128)(4,1)S(1)}, s32[]{:S(2)}) async-start(s8[4718592]{0:T(1024)(128)(4,1)} %bitcast.7), calls=%async_computation.2 | async-start | bytes 1048576
  47.4 6.7 %collective-permute-start.10 = (bf16[2,32,768]{2,1,0:T(8,128)(2,1)S(1)}, bf16[2,32,768]{2,1,0:T(8,128)(2,1)S(1)}, u32[]{:S(2)}, u32[]{:S(2)}) collective-permute-start(bf16[2,32,768]{2,1,0:T(8,128)(2,1)S(1)} %get-tuple-element.70), channel_id=1, source_target_pairs={{0,16},{4,20},{8,24},{12,28},{16,0},{20,4},{24,8},{28,12},{1,17},{... | collective-permute-start | bytes 294920 | tf_op jit(solution)/shard_map/ppermute | solution.py:360
  47.6 6.6 %copy-start.5 = (bf16[768,2]{0,1:T(2,128)(2,1)S(1)}, bf16[768,2]{0,1:T(2,128)(2,1)}, u32[]{:S(2)}) copy-start(bf16[768,2]{0,1:T(2,128)(2,1)} %param.29) | copy-start | bytes 9220
  47.6 6.6 %copy-start.6 = (s32[16]{0:T(128)S(1)}, s32[16]{0:T(128)}, u32[]{:S(2)}) copy-start(s32[16]{0:T(128)} %get-tuple-element.38.place) | copy-start | bytes 196
  47.6 6.5 %collective-permute-start.11 = (bf16[2,32,768]{2,1,0:T(8,128)(2,1)S(1)}, bf16[2,32,768]{2,1,0:T(8,128)(2,1)S(1)}, u32[]{:S(2)}, u32[]{:S(2)}) collective-permute-start(bf16[2,32,768]{2,1,0:T(8,128)(2,1)S(1)} %get-tuple-element.71), channel_id=1, source_target_pairs={{0,12},{4,8},{8,4},{12,0},{16,28},{20,24},{24,20},{28,16},{1,13},{... | collective-permute-start | bytes 294920 | tf_op jit(solution)/shard_map/ppermute | solution.py:360

commit v3 on v2

--- a/solution.py
+++ b/solution.py
@@ -127,27 +127,25 @@
     )(table, own, sibling)
 
 
-def project_kernel(images, key_weight, value_weight, keys, values):
+def project_kernel(images, weight, out):
     count, rows, width = images.shape
     whole = rows // 16 * 16
     for image in range(count):
-        for weight, out in ((key_weight, keys), (value_weight, values)):
-            out[image, whole:, :] = jnp.zeros((KEY_PAD - whole, width), BF16)
-            out[image, :rows, :] = jnp.dot(images[image], weight[...], preferred_element_type=F32).astype(BF16)
-
-
-def project_images(images, key_weight, value_weight):
+        out[image, whole:, :] = jnp.zeros((KEY_PAD - whole, width), BF16)
+        out[image, :rows, :] = jnp.dot(images[image], weight[...], preferred_element_type=F32).astype(BF16)
+
+
+def project_images(images, weight):
     count, rows, width = images.shape
-    out = jax.ShapeDtypeStruct((count, KEY_PAD, width), BF16)
     return pl.pallas_call(
         project_kernel,
-        out_shape=(out, out),
-        in_specs=[VMEM] * 3,
-        out_specs=(VMEM, VMEM),
+        out_shape=jax.ShapeDtypeStruct((count, KEY_PAD, width), BF16),
+        in_specs=[VMEM] * 2,
+        out_specs=VMEM,
         compiler_params=params(16),
         cost_estimate=SMALL,
         name="project_images",
-    )(images, key_weight, value_weight)
+    )(images, weight)
 
 
 def attend_kernel(key_rows, far_count, chunk, slots, own, sibling, *rest):
@@ -364,7 +362,9 @@
         pair_list.T, verify_order, image_slot, caption_slot, images.shape[0], img_count, cap_count
     )
     table = lax.all_to_all(table, ("img", "cap"), split_axis=0, concat_axis=0, tiled=True)
-    keys, values = project_images(images, key_weight, value_weight)
+    keys = project_images(images, key_weight)
+    value_weight, keys = lax.optimization_barrier((value_weight, keys))
+    values = project_images(images, value_weight)
     pinned = pltpu.with_memory_space_constraint(captions, pltpu.HBM)
     far = [[] for _ in chunks]
     for step in far_steps:
@@ -384,7 +384,11 @@
         far[index] = [swap(block, "cap", step * CORES) for step, block in zip(far_steps, far[index])]
 
     fetch(0)
+    far[1], keys = lax.optimization_barrier((far[1], keys))
     fetch(1)
+    far[2:], values = lax.optimization_barrier((far[2:], values))
+    for later in range(2, len(chunks)):
+        fetch(later)
     for index, chunk in enumerate(chunks):
         if index >= 2:
             slots = after(slots, chunks[index - 2])
@@ -401,10 +405,6 @@
             out_weight,
             gain_attn,
         )
-        if index == 0:
-            blocks, far[2:] = lax.optimization_barrier((blocks, far[2:]))
-            for later in range(2, len(chunks)):
-                fetch(later)
         for distance, block in zip(chunk, blocks):
             hidden[distance] = swap(block, "img", distance) if distance else block
     gain_ffn = after(gain_ffn, sum(chunks[:-1], ()))

time: 59.4 us -> 59.4 us (level)
  starting transfers between devices: 14 us -> 16 us
  waiting for transfers between devices: 1.89 us -> 0.22 us
    ppermute x12, starting transfers between devices: 14 us -> 16 us  [swap(): lax.ppermute(array, axis, [(peer, peer ^ distance) for peer in range(size)])]
    ppermute x12, waiting for transfers between devices: 1.89 us -> 0.22 us  [swap(): lax.ppermute(array, axis, [(peer, peer ^ distance) for peer in range(size)])]
    pallas_call x1 -> x2, Pallas kernels: 4.22 us -> 4.39 us  [project_images(): pl.pallas_call(project_kernel, out_shape=jax.ShapeDtypeStruct((count, KEY...]
  transfers between devices with their start and end apart: 12 -> 12, of which waited for: 3 -> 1; matrix products, arithmetic and copies ran while one was open for 1% -> 1% of each run, Pallas kernels for 33% -> 33%
where the time goes in v3:
time: 59.4 us; the launch traced here: 59.1 us
  Pallas kernels  27.2 us (46%)
  starting transfers between devices  16 us (27%)
  blocking collectives  14.1 us (24%)
  between operations  0.91 us (2%)
  local copies, waits for them, and re-layouts  0.75 us (1%)
    ppermute x12, starting transfers between devices, swap(): lax.ppermute(array, axis, [(peer, peer ^ distance) for peer in range(size)])  16 us
    all_to_all x1, blocking collectives, body(): lax.all_to_all(table, ('img', 'cap'), split_axis=0, concat_axis=0, tiled=...  14.1 us
    pallas_call x4, Pallas kernels, attend(): pl.pallas_call(functools.partial(attend_kernel, key_rows, len(far), chunk...  10.1 us
    pallas_call x1, Pallas kernels, feed_last(): pl.pallas_call(functools.partial(feed_last_kernel, first_parts, last_part...  4.72 us
    pallas_call x2, Pallas kernels, project_images(): pl.pallas_call(project_kernel, out_shape=jax.ShapeDtypeStruct((count, KEY...  4.39 us
    pallas_call x1, Pallas kernels, feed_first(): pl.pallas_call(feed_first_kernel, out_shape=jax.ShapeDtypeStruct((slots,...  3.29 us
    pallas_call x1, Pallas kernels, pick_blocks(): pl.pallas_call(functools.partial(pick_kernel, step, cap_count, chunks), o...  2.91 us
    pallas_call x1, Pallas kernels, make_table(): pl.pallas_call(functools.partial(table_kernel, image_local, caption_count...  1.76 us
  transfers between devices with their start and end apart: 12, of which 1 were waited for; matrix products, arithmetic and copies ran while one was open for 1% of the time, Pallas kernels for 33%

profile of v3, /device:TPU:0, one launch (start us, length us, event | category | flops | bytes accessed | tf_op | source)
XLA Modules:
  0.0 59.1 jit_solution(602636685228838520)
XLA Ops:
  0.6 0.5 collective-permute-start
  1.1 1.8 %slot_table.1 = (s32[32,128]{1,0:T(8,128)}, s32[16]{0:T(128)}) custom-call(s32[2,512]{1,0:T(2,128)} %bitcast.14, s32[16]{0:T(128)} %order.1, s32[64]{0:T(128)} %image_slot.1, s32[128]{0:T(128)} %caption_slot.1), custom_call_target="tpu_custom_call" | custom-call | tf_op jit(solution)/shard_map/slot_table/pallas_call | solution.py:60
  2.9 0.0 copy-start.7
  2.9 14.1 %all_to_all.11 = s32[32,1,128]{2,1,0:T(1,128)S(1)} all-to-all(s32[32,1,128]{2,1,0:T(1,128)} %bitcast.13), channel_id=1, replica_groups=mesh['img'=8,'cap'=4] {'img','cap'}, dimensions={0} | all-to-all | bytes 32768 | tf_op jit(solution)/shard_map/all_to_all | solution.py:364
  17.0 0.0 collective-permute-done.sibling
  17.0 2.9 %pick_captions.1 = (s32[16]{0:T(128)S(1)}, bf16[4,32,768]{2,1,0:T(8,128)(2,1)S(1)}, bf16[4,32,768]{2,1,0:T(8,128)(2,1)S(1)}, bf16[4,32,768]{2,1,0:T(8,128)(2,1)S(1)}, bf16[4,32,768]{2,1,0:T(8,128)(2,1)S(1)}) custom-call(s32[32,128]{1,0:T(8,128)S(1)} %bitcast.11, bf16[32,32,768]{2,1,0:T(8,128)(2,1)} %own.7, bf16[32,32,768]{2,1,0:T(8,128)(2,1)S(1)} %collective-permute-done.sibling), custom_call_target="tpu_custom_call" | custom-call | flops 65536 | bytes 1024 | tf_op jit(solution)/shard_map/pick_captions/pallas_call | solution.py:118
  19.9 0.0 copy-start.3
  19.9 0.6 collective-permute-start.1
  20.5 0.0 copy-done.7
  20.5 0.5 copy.20.images
  21.0 0.2 copy-done.3
  21.2 0.0 copy-start.4
  21.2 2.2 %project_images.2.rest_1_ = bf16[8,256,768]{2,1,0:T(8,128)(2,1)S(1)} custom-call(bf16[8,197,768]{2,1,0:T(8,128)(2,1)S(1)} %copy.20.images, bf16[768,768]{1,0:T(8,128)(2,1)S(1)} %copy-done.3), custom_call_target="tpu_custom_call" | custom-call | flops 65536 | bytes 1024 | tf_op jit(solution)/shard_map/project_images/pallas_call | solution.py:140
  23.4 0.0 copy-start.8
  23.4 0.0 copy-start
  23.4 0.0 copy-start.1
  23.4 0.0 copy-start.2
  23.4 1.4 %collective-permute-start.3 = (bf16[4,32,768]{2,1,0:T(8,128)(2,1)S(1)}, bf16[4,32,768]{2,1,0:T(8,128)(2,1)S(1)}, u32[]{:S(2)}, u32[]{:S(2)}) collective-permute-start(bf16[4,32,768]{2,1,0:T(8,128)(2,1)S(1)} %get-tuple-element.55), channel_id=1, source_target_pairs={{0,2},{1,3},{2,0},{3,1},{4,6},{5,7},{6,4},{7,5},{8,10},{9,11},{10,... | collective-permute-start | bytes 589832 | tf_op jit(solution)/shard_map/ppermute | solution.py:358
  24.8 0.0 copy-done.4
  24.8 2.2 %project_images.3.rest_2_ = bf16[8,256,768]{2,1,0:T(8,128)(2,1)S(1)} custom-call(bf16[8,197,768]{2,1,0:T(8,128)(2,1)S(1)} %copy.20.images, bf16[768,768]{1,0:T(8,128)(2,1)S(1)} %copy-done.4), custom_call_target="tpu_custom_call" | custom-call | flops 65536 | bytes 1024 | tf_op jit(solution)/shard_map/project_images/pallas_call | solution.py:140
  27.0 0.8 %collective-permute-start.6 = (bf16[4,32,768]{2,1,0:T(8,128)(2,1)S(1)}, bf16[4,32,768]{2,1,0:T(8,128)(2,1)S(1)}, u32[]{:S(2)}, u32[]{:S(2)}) collective-permute-start(bf16[4,32,768]{2,1,0:T(8,128)(2,1)S(1)} %get-tuple-element.60), channel_id=1, source_target_pairs={{0,2},{1,3},{2,0},{3,1},{4,6},{5,7},{6,4},{7,5},{8,10},{9,11},{10,... | collective-permute-start | bytes 589832 | tf_op jit(solution)/shard_map/ppermute | solution.py:358
  27.8 0.0 copy-done.8
  27.8 0.0 collective-permute-done.1.rest_0_
  27.8 0.0 copy-done
  27.8 0.0 copy-done.1
  27.8 0.0 copy-done.2
  27.8 2.5 %attend.4 = (bf16[2,32,768]{2,1,0:T(8,128)(2,1)S(1)}, bf16[2,32,768]{2,1,0:T(8,128)(2,1)S(1)}) custom-call(s32[16]{0:T(128)S(1)} %get-tuple-element.70.slots, bf16[32,32,768]{2,1,0:T(8,128)(2,1)S(1)} %copy-done, bf16[32,32,768]{2,1,0:T(8,128)(2,1)S(1)} %collective-permute-done.sibling, bf16[4,32,768]{2,1,0:T(8,128)(2,1)S(1)} %collective-permute-done.1.rest_0_, ...), custom_call_target="tpu_custom_call" | custom-call | flops 65536 | bytes 1024 | tf_op jit(solution)/shard_map/attend/pallas_call | solution.py:233
  30.3 0.6 %collective-permute-start.2 = (bf16[2,32,768]{2,1,0:T(8,128)(2,1)S(1)}, bf16[2,32,768]{2,1,0:T(8,128)(2,1)S(1)}, u32[]{:S(2)}, u32[]{:S(2)}) collective-permute-start(bf16[2,32,768]{2,1,0:T(8,128)(2,1)S(1)} %get-tuple-element.50), channel_id=1, source_target_pairs={{0,28},{4,24},{8,20},{12,16},{16,12},{20,8},{24,4},{28,0},{1,29},{... | collective-permute-start | bytes 294920 | tf_op jit(solution)/shard_map/ppermute | solution.py:358
  30.9 1.3 %collective-permute-start.9 = (bf16[4,32,768]{2,1,0:T(8,128)(2,1)S(1)}, bf16[4,32,768]{2,1,0:T(8,128)(2,1)S(1)}, u32[]{:S(2)}, u32[]{:S(2)}) collective-permute-start(bf16[4,32,768]{2,1,0:T(8,128)(2,1)S(1)} %get-tuple-element.71), channel_id=1, source_target_pairs={{0,2},{1,3},{2,0},{3,1},{4,6},{5,7},{6,4},{7,5},{8,10},{9,11},{10,... | collective-permute-start | bytes 589832 | tf_op jit(solution)/shard_map/ppermute | solution.py:358
  32.3 0.0 collective-permute-done.3.rest_0_
  32.3 0.0 slice-start.2
  32.3 2.5 %attend.5 = (bf16[2,32,768]{2,1,0:T(8,128)(2,1)S(1)}, bf16[2,32,768]{2,1,0:T(8,128)(2,1)S(1)}) custom-call(s32[16]{0:T(128)S(1)} %get-tuple-element.70.slots, bf16[32,32,768]{2,1,0:T(8,128)(2,1)S(1)} %copy-done, bf16[32,32,768]{2,1,0:T(8,128)(2,1)S(1)} %collective-permute-done.sibling, bf16[4,32,768]{2,1,0:T(8,128)(2,1)S(1)} %collective-permute-done.3.rest_0_, ...), custom_call_target="tpu_custom_call" | custom-call | flops 65536 | bytes 1024 | tf_op jit(solution)/shard_map/attend/pallas_call | solution.py:233
  34.8 3.4 %collective-permute-start.4 = (bf16[2,32,768]{2,1,0:T(8,128)(2,1)S(1)}, bf16[2,32,768]{2,1,0:T(8,128)(2,1)S(1)}, u32[]{:S(2)}, u32[]{:S(2)}) collective-permute-start(bf16[2,32,768]{2,1,0:T(8,128)(2,1)S(1)} %get-tuple-element.56), channel_id=1, source_target_pairs={{0,24},{4,28},{8,16},{12,20},{16,8},{20,12},{24,0},{28,4},{1,25},{... | collective-permute-start | bytes 294920 | tf_op jit(solution)/shard_map/ppermute | solution.py:358
  38.1 1.5 %collective-permute-start.5 = (bf16[2,32,768]{2,1,0:T(8,128)(2,1)S(1)}, bf16[2,32,768]{2,1,0:T(8,128)(2,1)S(1)}, u32[]{:S(2)}, u32[]{:S(2)}) collective-permute-start(bf16[2,32,768]{2,1,0:T(8,128)(2,1)S(1)} %get-tuple-element.57), channel_id=1, source_target_pairs={{0,4},{4,0},{8,12},{12,8},{16,20},{20,16},{24,28},{28,24},{1,5},{5... | collective-permute-start | bytes 294920 | tf_op jit(solution)/shard_map/ppermute | solution.py:358
  39.6 0.0 collective-permute-done.2.rest_0_
  39.6 0.0 copy-start.9
  39.6 0.0 slice-start.3
  39.6 0.0 collective-permute-done.6.rest_0_
  39.6 2.5 %attend.6 = (bf16[2,32,768]{2,1,0:T(8,128)(2,1)S(1)}, bf16[2,32,768]{2,1,0:T(8,128)(2,1)S(1)}) custom-call(s32[16]{0:T(128)S(1)} %get-tuple-element.70.slots, bf16[32,32,768]{2,1,0:T(8,128)(2,1)S(1)} %copy-done, bf16[32,32,768]{2,1,0:T(8,128)(2,1)S(1)} %collective-permute-done.sibling, bf16[4,32,768]{2,1,0:T(8,128)(2,1)S(1)} %collective-permute-done.6.rest_0_, ...), custom_call_target="tpu_custom_call" | custom-call | flops 65536 | bytes 1024 | tf_op jit(solution)/shard_map/attend/pallas_call | solution.py:233
  42.1 0.1 collective-permute-start.7
  42.2 1.1 %collective-permute-start.8 = (bf16[2,32,768]{2,1,0:T(8,128)(2,1)S(1)}, bf16[2,32,768]{2,1,0:T(8,128)(2,1)S(1)}, u32[]{:S(2)}, u32[]{:S(2)}) collective-permute-start(bf16[2,32,768]{2,1,0:T(8,128)(2,1)S(1)} %get-tuple-element.62), channel_id=1, source_target_pairs={{0,8},{4,12},{8,0},{12,4},{16,24},{20,28},{24,16},{28,20},{1,9},{5... | collective-permute-start | bytes 294920 | tf_op jit(solution)/shard_map/ppermute | solution.py:358
  43.3 0.0 copy-done.9
  43.3 0.0 slice-start
  43.3 0.0 slice-start.1
  43.3 0.0 collective-permute-done.4.rest_2_
  43.3 0.0 collective-permute-done.5.rest_3_
  43.3 0.0 collective-permute-done.9.rest_0_
  43.3 2.7 %attend.7 = (bf16[2,32,768]{2,1,0:T(8,128)(2,1)S(1)}, bf16[2,32,768]{2,1,0:T(8,128)(2,1)S(1)}) custom-call(s32[16]{0:T(128)S(1)} %get-tuple-element.70.slots, bf16[32,32,768]{2,1,0:T(8,128)(2,1)S(1)} %copy-done, bf16[32,32,768]{2,1,0:T(8,128)(2,1)S(1)} %collective-permute-done.sibling, bf16[4,32,768]{2,1,0:T(8,128)(2,1)S(1)} %collective-permute-done.9.rest_0_, ...), custom_call_target="tpu_custom_call" | custom-call | flops 65536 | bytes 1024 | tf_op jit(solution)/shard_map/attend/pallas_call | solution.py:233
  46.0 1.9 %collective-permute-start.10 = (bf16[2,32,768]{2,1,0:T(8,128)(2,1)S(1)}, bf16[2,32,768]{2,1,0:T(8,128)(2,1)S(1)}, u32[]{:S(2)}, u32[]{:S(2)}) collective-permute-start(bf16[2,32,768]{2,1,0:T(8,128)(2,1)S(1)} %get-tuple-element.72), channel_id=1, source_target_pairs={{0,16},{4,20},{8,24},{12,28},{16,0},{20,4},{24,8},{28,12},{1,17},{... | collective-permute-start | bytes 294920 | tf_op jit(solution)/shard_map/ppermute | solution.py:358
  47.9 0.0 copy-start.5
  47.9 0.0 copy-start.6
  47.9 2.9 %collective-permute-start.11 = (bf16[2,32,768]{2,1,0:T(8,128)(2,1)S(1)}, bf16[2,32,768]{2,1,0:T(8,128)(2,1)S(1)}, u32[]{:S(2)}, u32[]{:S(2)}) collective-permute-start(bf16[2,32,768]{2,1,0:T(8,128)(2,1)S(1)} %get-tuple-element.73), channel_id=1, source_target_pairs={{0,12},{4,8},{8,4},{12,0},{16,28},{20,24},{24,20},{28,16},{1,13},{... | collective-permute-start | bytes 294920 | tf_op jit(solution)/shard_map/ppermute | solution.py:358
  50.8 0.2 collective-permute-done.7.rest_0_
  51.0 0.0 collective-permute-done.8.rest_1_
  51.0 0.0 slice-done.2
  51.0 0.0 slice-done.3
  51.0 0.0 slice-done
  51.0 0.0 slice-done.1
  51.1 3.3 %feed_first.1.earlier = bf16[8,32,768]{2,1,0:T(8,128)(2,1)S(1)} custom-call(f32[1,768]{1,0:T(1,128)S(1)} %reshape.12.gain, bf16[768,3072]{1,0:T(8,128)(2,1)S(1)} %bitcast.8, bf16[3072,768]{1,0:T(8,128)(2,1)S(1)} %bitcast.10, bf16[2,32,768]{2,1,0:T(8,128)(2,1)S(1)} %collective-permute-done.2.rest_0_, bf16[2,32,768]{2,1,0:T(8,128)(2,1)S(1)} %get-tuple-element.65.rest_1_, ...), custom_call_target="tpu_custom_call" | custom-call | flops 2415919104 | bytes 9437184 | tf_op jit(solution)/shard_map/feed_first/pallas_call | solution.py:301
  54.4 0.0 collective-permute-done.10.rest_2_
  54.4 0.0 collective-permute-done.11.rest_3_
  54.4 0.0 copy-done.5
  54.4 0.0 copy-done.6
  54.4 4.7 %feed_last.1 = (bf16[16,32,768]{2,1,0:T(8,128)(2,1)}, f32[2,16]{1,0:T(2,128)}) custom-call(s32[16]{0:T(128)S(1)} %copy-done.6, f32[1,768]{1,0:T(1,128)S(1)} %reshape.12.gain, bf16[2,768]{1,0:T(2,128)(2,1)S(1)} %bitcast.12, bf16[768,3072]{1,0:T(8,128)(2,1)S(1)} %bitcast.8, bf16[3072,768]{1,0:T(8,128)(2,1)S(1)} %bitcast.10, ...), custom_call_target="tpu_custom_call" | custom-call | flops 2415919104 | bytes 9437184 | tf_op jit(solution)/shard_map/feed_last/pallas_call | solution.py:316
  (4 shorter events, 0.0 us)
Async XLA Ops:
  0.6 16.4 %collective-permute-start = (bf16[32,32,768]{2,1,0:T(8,128)(2,1)}, bf16[32,32,768]{2,1,0:T(8,128)(2,1)S(1)}, u32[]{:S(2)}, u32[]{:S(2)}) collective-permute-start(bf16[32,32,768]{2,1,0:T(8,128)(2,1)} %own.7), channel_id=1, source_target_pairs={{0,1},{1,0},{2,3},{3,2},{4,5},{5,4},{6,7},{7,6},{8,9},{9,8},{10,11... | collective-permute-start | bytes 4718600 | tf_op jit(solution)/shard_map/ppermute | solution.py:358
  2.9 17.6 %copy-start.7 = (bf16[8,197,768]{2,0,1:T(8,128)(2,1)S(1)}, bf16[8,197,768]{2,0,1:T(8,128)(2,1)}, u32[]{:S(2)}) copy-start(bf16[8,197,768]{2,0,1:T(8,128)(2,1)} %param.19) | copy-start | bytes 7262212
  19.9 1.3 %copy-start.3 = (bf16[768,768]{1,0:T(8,128)(2,1)S(1)}, bf16[768,768]{1,0:T(8,128)(2,1)}, u32[]{:S(2)}) copy-start(bf16[768,768]{1,0:T(8,128)(2,1)} %weight.1) | copy-start | bytes 3538948
  19.9 7.9 %collective-permute-start.1 = (bf16[4,32,768]{2,1,0:T(8,128)(2,1)S(1)}, bf16[4,32,768]{2,1,0:T(8,128)(2,1)S(1)}, u32[]{:S(2)}, u32[]{:S(2)}) collective-permute-start(bf16[4,32,768]{2,1,0:T(8,128)(2,1)S(1)} %get-tuple-element.42), channel_id=1, source_target_pairs={{0,2},{1,3},{2,0},{3,1},{4,6},{5,7},{6,4},{7,5},{8,10},{9,11},{10,... | collective-permute-start | bytes 589832 | tf_op jit(solution)/shard_map/ppermute | solution.py:358
  21.2 3.6 %copy-start.4 = (bf16[768,768]{1,0:T(8,128)(2,1)S(1)}, bf16[768,768]{1,0:T(8,128)(2,1)}, u32[]{:S(2)}) copy-start(bf16[768,768]{1,0:T(8,128)(2,1)} %weight.2) | copy-start | bytes 3538948
  23.4 4.4 %copy-start.8 = (f32[768]{0:T(1024)S(1)}, f32[768]{0:T(1024)}, u32[]{:S(2)}) copy-start(f32[768]{0:T(1024)} %param.25) | copy-start | bytes 9220
  23.4 4.4 %copy-start = (bf16[32,32,768]{2,1,0:T(8,128)(2,1)S(1)}, bf16[32,32,768]{2,1,0:T(8,128)(2,1)}, u32[]{:S(2)}) copy-start(bf16[32,32,768]{2,1,0:T(8,128)(2,1)} %own.7) | copy-start | bytes 4718596
  23.4 4.4 %copy-start.1 = (bf16[768,768]{1,0:T(8,128)(2,1)S(1)}, bf16[768,768]{1,0:T(8,128)(2,1)}, u32[]{:S(2)}) copy-start(bf16[768,768]{1,0:T(8,128)(2,1)} %rest_3_.7) | copy-start | bytes 3538948
  23.4 4.4 %copy-start.2 = (bf16[768,768]{1,0:T(8,128)(2,1)S(1)}, bf16[768,768]{1,0:T(8,128)(2,1)}, u32[]{:S(2)}) copy-start(bf16[768,768]{1,0:T(8,128)(2,1)} %rest_4_.7) | copy-start | bytes 3538948
  23.4 8.8 %collective-permute-start.3 = (bf16[4,32,768]{2,1,0:T(8,128)(2,1)S(1)}, bf16[4,32,768]{2,1,0:T(8,128)(2,1)S(1)}, u32[]{:S(2)}, u32[]{:S(2)}) collective-permute-start(bf16[4,32,768]{2,1,0:T(8,128)(2,1)S(1)} %get-tuple-element.55), channel_id=1, source_target_pairs={{0,2},{1,3},{2,0},{3,1},{4,6},{5,7},{6,4},{7,5},{8,10},{9,11},{10,... | collective-permute-start | bytes 589832 | tf_op jit(solution)/shard_map/ppermute | solution.py:358
  27.0 12.6 %collective-permute-start.6 = (bf16[4,32,768]{2,1,0:T(8,128)(2,1)S(1)}, bf16[4,32,768]{2,1,0:T(8,128)(2,1)S(1)}, u32[]{:S(2)}, u32[]{:S(2)}) collective-permute-start(bf16[4,32,768]{2,1,0:T(8,128)(2,1)S(1)} %get-tuple-element.60), channel_id=1, source_target_pairs={{0,2},{1,3},{2,0},{3,1},{4,6},{5,7},{6,4},{7,5},{8,10},{9,11},{10,... | collective-permute-start | bytes 589832 | tf_op jit(solution)/shard_map/ppermute | solution.py:358
  30.3 9.3 %collective-permute-start.2 = (bf16[2,32,768]{2,1,0:T(8,128)(2,1)S(1)}, bf16[2,32,768]{2,1,0:T(8,128)(2,1)S(1)}, u32[]{:S(2)}, u32[]{:S(2)}) collective-permute-start(bf16[2,32,768]{2,1,0:T(8,128)(2,1)S(1)} %get-tuple-element.50), channel_id=1, source_target_pairs={{0,28},{4,24},{8,20},{12,16},{16,12},{20,8},{24,4},{28,0},{1,29},{... | collective-permute-start | bytes 294920 | tf_op jit(solution)/shard_map/ppermute | solution.py:358
  30.9 12.4 %collective-permute-start.9 = (bf16[4,32,768]{2,1,0:T(8,128)(2,1)S(1)}, bf16[4,32,768]{2,1,0:T(8,128)(2,1)S(1)}, u32[]{:S(2)}, u32[]{:S(2)}) collective-permute-start(bf16[4,32,768]{2,1,0:T(8,128)(2,1)S(1)} %get-tuple-element.71), channel_id=1, source_target_pairs={{0,2},{1,3},{2,0},{3,1},{4,6},{5,7},{6,4},{7,5},{8,10},{9,11},{10,... | collective-permute-start | bytes 589832 | tf_op jit(solution)/shard_map/ppermute | solution.py:358
  32.3 18.7 %slice-start.2 = ((s8[4718592]{0:T(1024)(128)(4,1)}), s8[4194304]{0:T(1024)(128)(4,1)S(1)}, s32[]{:S(2)}) async-start(s8[4718592]{0:T(1024)(128)(4,1)} %bitcast.9), calls=%async_computation.3 | async-start | bytes 8388608
  34.8 8.5 %collective-permute-start.4 = (bf16[2,32,768]{2,1,0:T(8,128)(2,1)S(1)}, bf16[2,32,768]{2,1,0:T(8,128)(2,1)S(1)}, u32[]{:S(2)}, u32[]{:S(2)}) collective-permute-start(bf16[2,32,768]{2,1,0:T(8,128)(2,1)S(1)} %get-tuple-element.56), channel_id=1, source_target_pairs={{0,24},{4,28},{8,16},{12,20},{16,8},{20,12},{24,0},{28,4},{1,25},{... | collective-permute-start | bytes 294920 | tf_op jit(solution)/shard_map/ppermute | solution.py:358
  38.1 5.2 %collective-permute-start.5 = (bf16[2,32,768]{2,1,0:T(8,128)(2,1)S(1)}, bf16[2,32,768]{2,1,0:T(8,128)(2,1)S(1)}, u32[]{:S(2)}, u32[]{:S(2)}) collective-permute-start(bf16[2,32,768]{2,1,0:T(8,128)(2,1)S(1)} %get-tuple-element.57), channel_id=1, source_target_pairs={{0,4},{4,0},{8,12},{12,8},{16,20},{20,16},{24,28},{28,24},{1,5},{5... | collective-permute-start | bytes 294920 | tf_op jit(solution)/shard_map/ppermute | solution.py:358
  39.6 3.7 %copy-start.9 = (f32[768]{0:T(1024)S(1)}, f32[768]{0:T(1024)}, u32[]{:S(2)}) copy-start(f32[768]{0:T(1024)} %param.28) | copy-start | bytes 9220
  39.6 11.4 %slice-start.3 = ((s8[4718592]{0:T(1024)(128)(4,1)}), s8[524288]{0:T(1024)(128)(4,1)S(1)}, s32[]{:S(2)}) async-start(s8[4718592]{0:T(1024)(128)(4,1)} %bitcast.9), calls=%async_computation.4 | async-start | bytes 1048576
  42.1 8.9 %collective-permute-start.7 = (bf16[2,32,768]{2,1,0:T(8,128)(2,1)S(1)}, bf16[2,32,768]{2,1,0:T(8,128)(2,1)S(1)}, u32[]{:S(2)}, u32[]{:S(2)}) collective-permute-start(bf16[2,32,768]{2,1,0:T(8,128)(2,1)S(1)} %get-tuple-element.61), channel_id=1, source_target_pairs={{0,20},{4,16},{8,28},{12,24},{16,4},{20,0},{24,12},{28,8},{1,21},{... | collective-permute-start | bytes 294920 | tf_op jit(solution)/shard_map/ppermute | solution.py:358
  42.2 8.8 %collective-permute-start.8 = (bf16[2,32,768]{2,1,0:T(8,128)(2,1)S(1)}, bf16[2,32,768]{2,1,0:T(8,128)(2,1)S(1)}, u32[]{:S(2)}, u32[]{:S(2)}) collective-permute-start(bf16[2,32,768]{2,1,0:T(8,128)(2,1)S(1)} %get-tuple-element.62), channel_id=1, source_target_pairs={{0,8},{4,12},{8,0},{12,4},{16,24},{20,28},{24,16},{28,20},{1,9},{5... | collective-permute-start | bytes 294920 | tf_op jit(solution)/shard_map/ppermute | solution.py:358
  43.3 7.8 %slice-start = ((s8[4718592]{0:T(1024)(128)(4,1)}), s8[4194304]{0:T(1024)(128)(4,1)S(1)}, s32[]{:S(2)}) async-start(s8[4718592]{0:T(1024)(128)(4,1)} %bitcast.7), calls=%async_computation.1 | async-start | bytes 8388608
  43.3 7.8 %slice-start.1 = ((s8[4718592]{0:T(1024)(128)(4,1)}), s8[524288]{0:T(1024)(128)(4,1)S(1)}, s32[]{:S(2)}) async-start(s8[4718592]{0:T(1024)(128)(4,1)} %bitcast.7), calls=%async_computation.2 | async-start | bytes 1048576
  46.0 8.4 %collective-permute-start.10 = (bf16[2,32,768]{2,1,0:T(8,128)(2,1)S(1)}, bf16[2,32,768]{2,1,0:T(8,128)(2,1)S(1)}, u32[]{:S(2)}, u32[]{:S(2)}) collective-permute-start(bf16[2,32,768]{2,1,0:T(8,128)(2,1)S(1)} %get-tuple-element.72), channel_id=1, source_target_pairs={{0,16},{4,20},{8,24},{12,28},{16,0},{20,4},{24,8},{28,12},{1,17},{... | collective-permute-start | bytes 294920 | tf_op jit(solution)/shard_map/ppermute | solution.py:358
  47.9 6.5 %copy-start.5 = (bf16[768,2]{0,1:T(2,128)(2,1)S(1)}, bf16[768,2]{0,1:T(2,128)(2,1)}, u32[]{:S(2)}) copy-start(bf16[768,2]{0,1:T(2,128)(2,1)} %param.29) | copy-start | bytes 9220
  47.9 6.5 %copy-start.6 = (s32[16]{0:T(128)S(1)}, s32[16]{0:T(128)}, u32[]{:S(2)}) copy-start(s32[16]{0:T(128)} %get-tuple-element.39.place) | copy-start | bytes 196
  47.9 6.5 %collective-permute-start.11 = (bf16[2,32,768]{2,1,0:T(8,128)(2,1)S(1)}, bf16[2,32,768]{2,1,0:T(8,128)(2,1)S(1)}, u32[]{:S(2)}, u32[]{:S(2)}) collective-permute-start(bf16[2,32,768]{2,1,0:T(8,128)(2,1)S(1)} %get-tuple-element.73), channel_id=1, source_target_pairs={{0,12},{4,8},{8,4},{12,0},{16,28},{20,24},{24,20},{28,16},{1,13},{... | collective-permute-start | bytes 294920 | tf_op jit(solution)/shard_map/ppermute | solution.py:358

commit v4 on v3

--- a/solution.py
+++ b/solution.py
@@ -246,7 +246,7 @@
     )(slots, own, sibling, *far, keys, values, query_weight, out_weight, gain)
 
 
-TILES = 3
+TILES = 2
 
 
 def feed_rows(parts, gain, in_weight, back_weight):

time: 59.4 us -> 58.9 us (level)
  no operation moved by 1% of the time
where the time goes in v4:
time: 58.9 us; the launch traced here: 58.6 us
  Pallas kernels  26.7 us (45%)
  starting transfers between devices  16 us (27%)
  blocking collectives  14.1 us (24%)
  between operations  0.91 us (2%)
  local copies, waits for them, and re-layouts  0.73 us (1%)
    ppermute x12, starting transfers between devices, swap(): lax.ppermute(array, axis, [(peer, peer ^ distance) for peer in range(size)])  16 us
    all_to_all x1, blocking collectives, body(): lax.all_to_all(table, ('img', 'cap'), split_axis=0, concat_axis=0, tiled=...  14.1 us
    pallas_call x4, Pallas kernels, attend(): pl.pallas_call(functools.partial(attend_kernel, key_rows, len(far), chunk...  10.1 us
    pallas_call x1, Pallas kernels, feed_last(): pl.pallas_call(functools.partial(feed_last_kernel, first_parts, last_part...  4.47 us
    pallas_call x2, Pallas kernels, project_images(): pl.pallas_call(project_kernel, out_shape=jax.ShapeDtypeStruct((count, KEY...  4.39 us
    pallas_call x1, Pallas kernels, feed_first(): pl.pallas_call(feed_first_kernel, out_shape=jax.ShapeDtypeStruct((slots,...  3.04 us
    pallas_call x1, Pallas kernels, pick_blocks(): pl.pallas_call(functools.partial(pick_kernel, step, cap_count, chunks), o...  2.91 us
    pallas_call x1, Pallas kernels, make_table(): pl.pallas_call(functools.partial(table_kernel, image_local, caption_count...  1.76 us
  transfers between devices with their start and end apart: 12, of which 1 were waited for; matrix products, arithmetic and copies ran while one was open for 1% of the time, Pallas kernels for 33%

profile of v4, /device:TPU:0, one launch (start us, length us, event | category | flops | bytes accessed | tf_op | source)
XLA Modules:
  0.0 58.6 jit_solution(17588982519570414401)
XLA Ops:
  0.6 0.5 collective-permute-start
  1.1 1.8 %slot_table.1 = (s32[32,128]{1,0:T(8,128)}, s32[16]{0:T(128)}) custom-call(s32[2,512]{1,0:T(2,128)} %bitcast.14, s32[16]{0:T(128)} %order.1, s32[64]{0:T(128)} %image_slot.1, s32[128]{0:T(128)} %caption_slot.1), custom_call_target="tpu_custom_call" | custom-call | tf_op jit(solution)/shard_map/slot_table/pallas_call | solution.py:60
  2.9 0.0 copy-start.7
  2.9 14.1 %all_to_all.11 = s32[32,1,128]{2,1,0:T(1,128)S(1)} all-to-all(s32[32,1,128]{2,1,0:T(1,128)} %bitcast.13), channel_id=1, replica_groups=mesh['img'=8,'cap'=4] {'img','cap'}, dimensions={0} | all-to-all | bytes 32768 | tf_op jit(solution)/shard_map/all_to_all | solution.py:364
  17.0 0.0 collective-permute-done.sibling
  17.0 2.9 %pick_captions.1 = (s32[16]{0:T(128)S(1)}, bf16[4,32,768]{2,1,0:T(8,128)(2,1)S(1)}, bf16[4,32,768]{2,1,0:T(8,128)(2,1)S(1)}, bf16[4,32,768]{2,1,0:T(8,128)(2,1)S(1)}, bf16[4,32,768]{2,1,0:T(8,128)(2,1)S(1)}) custom-call(s32[32,128]{1,0:T(8,128)S(1)} %bitcast.11, bf16[32,32,768]{2,1,0:T(8,128)(2,1)} %own.7, bf16[32,32,768]{2,1,0:T(8,128)(2,1)S(1)} %collective-permute-done.sibling), custom_call_target="tpu_custom_call" | custom-call | flops 65536 | bytes 1024 | tf_op jit(solution)/shard_map/pick_captions/pallas_call | solution.py:118
  19.9 0.0 copy-start.3
  19.9 0.6 %collective-permute-start.1 = (bf16[4,32,768]{2,1,0:T(8,128)(2,1)S(1)}, bf16[4,32,768]{2,1,0:T(8,128)(2,1)S(1)}, u32[]{:S(2)}, u32[]{:S(2)}) collective-permute-start(bf16[4,32,768]{2,1,0:T(8,128)(2,1)S(1)} %get-tuple-element.42), channel_id=1, source_target_pairs={{0,2},{1,3},{2,0},{3,1},{4,6},{5,7},{6,4},{7,5},{8,10},{9,11},{10,... | collective-permute-start | bytes 589832 | tf_op jit(solution)/shard_map/ppermute | solution.py:358
  20.5 0.0 copy-done.7
  20.5 0.5 copy.20.images
  21.0 0.2 copy-done.3
  21.2 0.0 copy-start.4
  21.2 2.2 %project_images.2.rest_1_ = bf16[8,256,768]{2,1,0:T(8,128)(2,1)S(1)} custom-call(bf16[8,197,768]{2,1,0:T(8,128)(2,1)S(1)} %copy.20.images, bf16[768,768]{1,0:T(8,128)(2,1)S(1)} %copy-done.3), custom_call_target="tpu_custom_call" | custom-call | flops 65536 | bytes 1024 | tf_op jit(solution)/shard_map/project_images/pallas_call | solution.py:140
  23.4 0.0 copy-start.8
  23.4 0.0 copy-start
  23.4 0.0 copy-start.1
  23.4 0.0 copy-start.2
  23.4 1.4 %collective-permute-start.3 = (bf16[4,32,768]{2,1,0:T(8,128)(2,1)S(1)}, bf16[4,32,768]{2,1,0:T(8,128)(2,1)S(1)}, u32[]{:S(2)}, u32[]{:S(2)}) collective-permute-start(bf16[4,32,768]{2,1,0:T(8,128)(2,1)S(1)} %get-tuple-element.55), channel_id=1, source_target_pairs={{0,2},{1,3},{2,0},{3,1},{4,6},{5,7},{6,4},{7,5},{8,10},{9,11},{10,... | collective-permute-start | bytes 589832 | tf_op jit(solution)/shard_map/ppermute | solution.py:358
  24.8 0.0 copy-done.4
  24.8 2.2 %project_images.3.rest_2_ = bf16[8,256,768]{2,1,0:T(8,128)(2,1)S(1)} custom-call(bf16[8,197,768]{2,1,0:T(8,128)(2,1)S(1)} %copy.20.images, bf16[768,768]{1,0:T(8,128)(2,1)S(1)} %copy-done.4), custom_call_target="tpu_custom_call" | custom-call | flops 65536 | bytes 1024 | tf_op jit(solution)/shard_map/project_images/pallas_call | solution.py:140
  27.0 0.8 %collective-permute-start.6 = (bf16[4,32,768]{2,1,0:T(8,128)(2,1)S(1)}, bf16[4,32,768]{2,1,0:T(8,128)(2,1)S(1)}, u32[]{:S(2)}, u32[]{:S(2)}) collective-permute-start(bf16[4,32,768]{2,1,0:T(8,128)(2,1)S(1)} %get-tuple-element.60), channel_id=1, source_target_pairs={{0,2},{1,3},{2,0},{3,1},{4,6},{5,7},{6,4},{7,5},{8,10},{9,11},{10,... | collective-permute-start | bytes 589832 | tf_op jit(solution)/shard_map/ppermute | solution.py:358
  27.8 0.0 copy-done.8
  27.8 0.0 collective-permute-done.1.rest_0_
  27.8 0.0 copy-done
  27.8 0.0 copy-done.1
  27.8 0.0 copy-done.2
  27.8 2.5 %attend.4 = (bf16[2,32,768]{2,1,0:T(8,128)(2,1)S(1)}, bf16[2,32,768]{2,1,0:T(8,128)(2,1)S(1)}) custom-call(s32[16]{0:T(128)S(1)} %get-tuple-element.70.slots, bf16[32,32,768]{2,1,0:T(8,128)(2,1)S(1)} %copy-done, bf16[32,32,768]{2,1,0:T(8,128)(2,1)S(1)} %collective-permute-done.sibling, bf16[4,32,768]{2,1,0:T(8,128)(2,1)S(1)} %collective-permute-done.1.rest_0_, ...), custom_call_target="tpu_custom_call" | custom-call | flops 65536 | bytes 1024 | tf_op jit(solution)/shard_map/attend/pallas_call | solution.py:233
  30.3 0.6 %collective-permute-start.2 = (bf16[2,32,768]{2,1,0:T(8,128)(2,1)S(1)}, bf16[2,32,768]{2,1,0:T(8,128)(2,1)S(1)}, u32[]{:S(2)}, u32[]{:S(2)}) collective-permute-start(bf16[2,32,768]{2,1,0:T(8,128)(2,1)S(1)} %get-tuple-element.50), channel_id=1, source_target_pairs={{0,28},{4,24},{8,20},{12,16},{16,12},{20,8},{24,4},{28,0},{1,29},{... | collective-permute-start | bytes 294920 | tf_op jit(solution)/shard_map/ppermute | solution.py:358
  30.9 1.3 %collective-permute-start.9 = (bf16[4,32,768]{2,1,0:T(8,128)(2,1)S(1)}, bf16[4,32,768]{2,1,0:T(8,128)(2,1)S(1)}, u32[]{:S(2)}, u32[]{:S(2)}) collective-permute-start(bf16[4,32,768]{2,1,0:T(8,128)(2,1)S(1)} %get-tuple-element.71), channel_id=1, source_target_pairs={{0,2},{1,3},{2,0},{3,1},{4,6},{5,7},{6,4},{7,5},{8,10},{9,11},{10,... | collective-permute-start | bytes 589832 | tf_op jit(solution)/shard_map/ppermute | solution.py:358
  32.3 0.0 collective-permute-done.3.rest_0_
  32.3 0.0 slice-start.2
  32.3 2.5 %attend.5 = (bf16[2,32,768]{2,1,0:T(8,128)(2,1)S(1)}, bf16[2,32,768]{2,1,0:T(8,128)(2,1)S(1)}) custom-call(s32[16]{0:T(128)S(1)} %get-tuple-element.70.slots, bf16[32,32,768]{2,1,0:T(8,128)(2,1)S(1)} %copy-done, bf16[32,32,768]{2,1,0:T(8,128)(2,1)S(1)} %collective-permute-done.sibling, bf16[4,32,768]{2,1,0:T(8,128)(2,1)S(1)} %collective-permute-done.3.rest_0_, ...), custom_call_target="tpu_custom_call" | custom-call | flops 65536 | bytes 1024 | tf_op jit(solution)/shard_map/attend/pallas_call | solution.py:233
  34.8 3.3 %collective-permute-start.4 = (bf16[2,32,768]{2,1,0:T(8,128)(2,1)S(1)}, bf16[2,32,768]{2,1,0:T(8,128)(2,1)S(1)}, u32[]{:S(2)}, u32[]{:S(2)}) collective-permute-start(bf16[2,32,768]{2,1,0:T(8,128)(2,1)S(1)} %get-tuple-element.56), channel_id=1, source_target_pairs={{0,24},{4,28},{8,16},{12,20},{16,8},{20,12},{24,0},{28,4},{1,25},{... | collective-permute-start | bytes 294920 | tf_op jit(solution)/shard_map/ppermute | solution.py:358
  38.1 1.5 %collective-permute-start.5 = (bf16[2,32,768]{2,1,0:T(8,128)(2,1)S(1)}, bf16[2,32,768]{2,1,0:T(8,128)(2,1)S(1)}, u32[]{:S(2)}, u32[]{:S(2)}) collective-permute-start(bf16[2,32,768]{2,1,0:T(8,128)(2,1)S(1)} %get-tuple-element.57), channel_id=1, source_target_pairs={{0,4},{4,0},{8,12},{12,8},{16,20},{20,16},{24,28},{28,24},{1,5},{5... | collective-permute-start | bytes 294920 | tf_op jit(solution)/shard_map/ppermute | solution.py:358
  39.6 0.0 collective-permute-done.2.rest_0_
  39.6 0.0 copy-start.9
  39.6 0.0 slice-start.3
  39.6 0.0 collective-permute-done.6.rest_0_
  39.6 2.5 %attend.6 = (bf16[2,32,768]{2,1,0:T(8,128)(2,1)S(1)}, bf16[2,32,768]{2,1,0:T(8,128)(2,1)S(1)}) custom-call(s32[16]{0:T(128)S(1)} %get-tuple-element.70.slots, bf16[32,32,768]{2,1,0:T(8,128)(2,1)S(1)} %copy-done, bf16[32,32,768]{2,1,0:T(8,128)(2,1)S(1)} %collective-permute-done.sibling, bf16[4,32,768]{2,1,0:T(8,128)(2,1)S(1)} %collective-permute-done.6.rest_0_, ...), custom_call_target="tpu_custom_call" | custom-call | flops 65536 | bytes 1024 | tf_op jit(solution)/shard_map/attend/pallas_call | solution.py:233
  42.1 0.1 collective-permute-start.7
  42.2 1.1 %collective-permute-start.8 = (bf16[2,32,768]{2,1,0:T(8,128)(2,1)S(1)}, bf16[2,32,768]{2,1,0:T(8,128)(2,1)S(1)}, u32[]{:S(2)}, u32[]{:S(2)}) collective-permute-start(bf16[2,32,768]{2,1,0:T(8,128)(2,1)S(1)} %get-tuple-element.62), channel_id=1, source_target_pairs={{0,8},{4,12},{8,0},{12,4},{16,24},{20,28},{24,16},{28,20},{1,9},{5... | collective-permute-start | bytes 294920 | tf_op jit(solution)/shard_map/ppermute | solution.py:358
  43.3 0.0 copy-done.9
  43.3 0.0 slice-start
  43.3 0.0 slice-start.1
  43.3 0.0 collective-permute-done.4.rest_2_
  43.3 0.0 collective-permute-done.5.rest_3_
  43.3 0.0 collective-permute-done.9.rest_0_
  43.3 2.7 %attend.7 = (bf16[2,32,768]{2,1,0:T(8,128)(2,1)S(1)}, bf16[2,32,768]{2,1,0:T(8,128)(2,1)S(1)}) custom-call(s32[16]{0:T(128)S(1)} %get-tuple-element.70.slots, bf16[32,32,768]{2,1,0:T(8,128)(2,1)S(1)} %copy-done, bf16[32,32,768]{2,1,0:T(8,128)(2,1)S(1)} %collective-permute-done.sibling, bf16[4,32,768]{2,1,0:T(8,128)(2,1)S(1)} %collective-permute-done.9.rest_0_, ...), custom_call_target="tpu_custom_call" | custom-call | flops 65536 | bytes 1024 | tf_op jit(solution)/shard_map/attend/pallas_call | solution.py:233
  46.0 1.9 %collective-permute-start.10 = (bf16[2,32,768]{2,1,0:T(8,128)(2,1)S(1)}, bf16[2,32,768]{2,1,0:T(8,128)(2,1)S(1)}, u32[]{:S(2)}, u32[]{:S(2)}) collective-permute-start(bf16[2,32,768]{2,1,0:T(8,128)(2,1)S(1)} %get-tuple-element.72), channel_id=1, source_target_pairs={{0,16},{4,20},{8,24},{12,28},{16,0},{20,4},{24,8},{28,12},{1,17},{... | collective-permute-start | bytes 294920 | tf_op jit(solution)/shard_map/ppermute | solution.py:358
  47.9 0.0 copy-start.5
  47.9 0.0 copy-start.6
  47.9 2.9 %collective-permute-start.11 = (bf16[2,32,768]{2,1,0:T(8,128)(2,1)S(1)}, bf16[2,32,768]{2,1,0:T(8,128)(2,1)S(1)}, u32[]{:S(2)}, u32[]{:S(2)}) collective-permute-start(bf16[2,32,768]{2,1,0:T(8,128)(2,1)S(1)} %get-tuple-element.73), channel_id=1, source_target_pairs={{0,12},{4,8},{8,4},{12,0},{16,28},{20,24},{24,20},{28,16},{1,13},{... | collective-permute-start | bytes 294920 | tf_op jit(solution)/shard_map/ppermute | solution.py:358
  50.8 0.2 collective-permute-done.7.rest_0_
  51.0 0.0 collective-permute-done.8.rest_1_
  51.0 0.0 slice-done.2
  51.0 0.0 slice-done.3
  51.0 0.0 slice-done
  51.0 0.0 slice-done.1
  51.0 3.0 %feed_first.1.earlier = bf16[8,32,768]{2,1,0:T(8,128)(2,1)S(1)} custom-call(f32[1,768]{1,0:T(1,128)S(1)} %reshape.12.gain, bf16[768,3072]{1,0:T(8,128)(2,1)S(1)} %bitcast.8, bf16[3072,768]{1,0:T(8,128)(2,1)S(1)} %bitcast.10, bf16[2,32,768]{2,1,0:T(8,128)(2,1)S(1)} %collective-permute-done.2.rest_0_, bf16[2,32,768]{2,1,0:T(8,128)(2,1)S(1)} %get-tuple-element.65.rest_1_, ...), custom_call_target="tpu_custom_call" | custom-call | flops 2415919104 | bytes 9437184 | tf_op jit(solution)/shard_map/feed_first/pallas_call | solution.py:301
  54.1 0.0 collective-permute-done.10.rest_2_
  54.1 0.0 collective-permute-done.11.rest_3_
  54.1 0.0 copy-done.5
  54.1 0.0 copy-done.6
  54.1 4.5 %feed_last.1 = (bf16[16,32,768]{2,1,0:T(8,128)(2,1)}, f32[2,16]{1,0:T(2,128)}) custom-call(s32[16]{0:T(128)S(1)} %copy-done.6, f32[1,768]{1,0:T(1,128)S(1)} %reshape.12.gain, bf16[2,768]{1,0:T(2,128)(2,1)S(1)} %bitcast.12, bf16[768,3072]{1,0:T(8,128)(2,1)S(1)} %bitcast.8, bf16[3072,768]{1,0:T(8,128)(2,1)S(1)} %bitcast.10, ...), custom_call_target="tpu_custom_call" | custom-call | flops 2415919104 | bytes 9437184 | tf_op jit(solution)/shard_map/feed_last/pallas_call | solution.py:316
  (4 shorter events, 0.0 us)
Async XLA Ops:
  0.6 16.4 %collective-permute-start = (bf16[32,32,768]{2,1,0:T(8,128)(2,1)}, bf16[32,32,768]{2,1,0:T(8,128)(2,1)S(1)}, u32[]{:S(2)}, u32[]{:S(2)}) collective-permute-start(bf16[32,32,768]{2,1,0:T(8,128)(2,1)} %own.7), channel_id=1, source_target_pairs={{0,1},{1,0},{2,3},{3,2},{4,5},{5,4},{6,7},{7,6},{8,9},{9,8},{10,11... | collective-permute-start | bytes 4718600 | tf_op jit(solution)/shard_map/ppermute | solution.py:358
  2.9 17.6 %copy-start.7 = (bf16[8,197,768]{2,0,1:T(8,128)(2,1)S(1)}, bf16[8,197,768]{2,0,1:T(8,128)(2,1)}, u32[]{:S(2)}) copy-start(bf16[8,197,768]{2,0,1:T(8,128)(2,1)} %param.19) | copy-start | bytes 7262212
  19.9 1.3 %copy-start.3 = (bf16[768,768]{1,0:T(8,128)(2,1)S(1)}, bf16[768,768]{1,0:T(8,128)(2,1)}, u32[]{:S(2)}) copy-start(bf16[768,768]{1,0:T(8,128)(2,1)} %weight.1) | copy-start | bytes 3538948
  19.9 7.9 %collective-permute-start.1 = (bf16[4,32,768]{2,1,0:T(8,128)(2,1)S(1)}, bf16[4,32,768]{2,1,0:T(8,128)(2,1)S(1)}, u32[]{:S(2)}, u32[]{:S(2)}) collective-permute-start(bf16[4,32,768]{2,1,0:T(8,128)(2,1)S(1)} %get-tuple-element.42), channel_id=1, source_target_pairs={{0,2},{1,3},{2,0},{3,1},{4,6},{5,7},{6,4},{7,5},{8,10},{9,11},{10,... | collective-permute-start | bytes 589832 | tf_op jit(solution)/shard_map/ppermute | solution.py:358
  21.2 3.6 %copy-start.4 = (bf16[768,768]{1,0:T(8,128)(2,1)S(1)}, bf16[768,768]{1,0:T(8,128)(2,1)}, u32[]{:S(2)}) copy-start(bf16[768,768]{1,0:T(8,128)(2,1)} %weight.2) | copy-start | bytes 3538948
  23.4 4.4 %copy-start.8 = (f32[768]{0:T(1024)S(1)}, f32[768]{0:T(1024)}, u32[]{:S(2)}) copy-start(f32[768]{0:T(1024)} %param.25) | copy-start | bytes 9220
  23.4 4.4 %copy-start = (bf16[32,32,768]{2,1,0:T(8,128)(2,1)S(1)}, bf16[32,32,768]{2,1,0:T(8,128)(2,1)}, u32[]{:S(2)}) copy-start(bf16[32,32,768]{2,1,0:T(8,128)(2,1)} %own.7) | copy-start | bytes 4718596
  23.4 4.4 %copy-start.1 = (bf16[768,768]{1,0:T(8,128)(2,1)S(1)}, bf16[768,768]{1,0:T(8,128)(2,1)}, u32[]{:S(2)}) copy-start(bf16[768,768]{1,0:T(8,128)(2,1)} %rest_3_.7) | copy-start | bytes 3538948
  23.4 4.4 %copy-start.2 = (bf16[768,768]{1,0:T(8,128)(2,1)S(1)}, bf16[768,768]{1,0:T(8,128)(2,1)}, u32[]{:S(2)}) copy-start(bf16[768,768]{1,0:T(8,128)(2,1)} %rest_4_.7) | copy-start | bytes 3538948
  23.4 8.8 %collective-permute-start.3 = (bf16[4,32,768]{2,1,0:T(8,128)(2,1)S(1)}, bf16[4,32,768]{2,1,0:T(8,128)(2,1)S(1)}, u32[]{:S(2)}, u32[]{:S(2)}) collective-permute-start(bf16[4,32,768]{2,1,0:T(8,128)(2,1)S(1)} %get-tuple-element.55), channel_id=1, source_target_pairs={{0,2},{1,3},{2,0},{3,1},{4,6},{5,7},{6,4},{7,5},{8,10},{9,11},{10,... | collective-permute-start | bytes 589832 | tf_op jit(solution)/shard_map/ppermute | solution.py:358
  27.0 12.6 %collective-permute-start.6 = (bf16[4,32,768]{2,1,0:T(8,128)(2,1)S(1)}, bf16[4,32,768]{2,1,0:T(8,128)(2,1)S(1)}, u32[]{:S(2)}, u32[]{:S(2)}) collective-permute-start(bf16[4,32,768]{2,1,0:T(8,128)(2,1)S(1)} %get-tuple-element.60), channel_id=1, source_target_pairs={{0,2},{1,3},{2,0},{3,1},{4,6},{5,7},{6,4},{7,5},{8,10},{9,11},{10,... | collective-permute-start | bytes 589832 | tf_op jit(solution)/shard_map/ppermute | solution.py:358
  30.3 9.2 %collective-permute-start.2 = (bf16[2,32,768]{2,1,0:T(8,128)(2,1)S(1)}, bf16[2,32,768]{2,1,0:T(8,128)(2,1)S(1)}, u32[]{:S(2)}, u32[]{:S(2)}) collective-permute-start(bf16[2,32,768]{2,1,0:T(8,128)(2,1)S(1)} %get-tuple-element.50), channel_id=1, source_target_pairs={{0,28},{4,24},{8,20},{12,16},{16,12},{20,8},{24,4},{28,0},{1,29},{... | collective-permute-start | bytes 294920 | tf_op jit(solution)/shard_map/ppermute | solution.py:358
  30.9 12.4 %collective-permute-start.9 = (bf16[4,32,768]{2,1,0:T(8,128)(2,1)S(1)}, bf16[4,32,768]{2,1,0:T(8,128)(2,1)S(1)}, u32[]{:S(2)}, u32[]{:S(2)}) collective-permute-start(bf16[4,32,768]{2,1,0:T(8,128)(2,1)S(1)} %get-tuple-element.71), channel_id=1, source_target_pairs={{0,2},{1,3},{2,0},{3,1},{4,6},{5,7},{6,4},{7,5},{8,10},{9,11},{10,... | collective-permute-start | bytes 589832 | tf_op jit(solution)/shard_map/ppermute | solution.py:358
  32.3 18.7 %slice-start.2 = ((s8[4718592]{0:T(1024)(128)(4,1)}), s8[4194304]{0:T(1024)(128)(4,1)S(1)}, s32[]{:S(2)}) async-start(s8[4718592]{0:T(1024)(128)(4,1)} %bitcast.9), calls=%async_computation.3 | async-start | bytes 8388608
  34.8 8.5 %collective-permute-start.4 = (bf16[2,32,768]{2,1,0:T(8,128)(2,1)S(1)}, bf16[2,32,768]{2,1,0:T(8,128)(2,1)S(1)}, u32[]{:S(2)}, u32[]{:S(2)}) collective-permute-start(bf16[2,32,768]{2,1,0:T(8,128)(2,1)S(1)} %get-tuple-element.56), channel_id=1, source_target_pairs={{0,24},{4,28},{8,16},{12,20},{16,8},{20,12},{24,0},{28,4},{1,25},{... | collective-permute-start | bytes 294920 | tf_op jit(solution)/shard_map/ppermute | solution.py:358
  38.1 5.2 %collective-permute-start.5 = (bf16[2,32,768]{2,1,0:T(8,128)(2,1)S(1)}, bf16[2,32,768]{2,1,0:T(8,128)(2,1)S(1)}, u32[]{:S(2)}, u32[]{:S(2)}) collective-permute-start(bf16[2,32,768]{2,1,0:T(8,128)(2,1)S(1)} %get-tuple-element.57), channel_id=1, source_target_pairs={{0,4},{4,0},{8,12},{12,8},{16,20},{20,16},{24,28},{28,24},{1,5},{5... | collective-permute-start | bytes 294920 | tf_op jit(solution)/shard_map/ppermute | solution.py:358
  39.6 3.7 %copy-start.9 = (f32[768]{0:T(1024)S(1)}, f32[768]{0:T(1024)}, u32[]{:S(2)}) copy-start(f32[768]{0:T(1024)} %param.28) | copy-start | bytes 9220
  39.6 11.4 %slice-start.3 = ((s8[4718592]{0:T(1024)(128)(4,1)}), s8[524288]{0:T(1024)(128)(4,1)S(1)}, s32[]{:S(2)}) async-start(s8[4718592]{0:T(1024)(128)(4,1)} %bitcast.9), calls=%async_computation.4 | async-start | bytes 1048576
  42.1 8.9 %collective-permute-start.7 = (bf16[2,32,768]{2,1,0:T(8,128)(2,1)S(1)}, bf16[2,32,768]{2,1,0:T(8,128)(2,1)S(1)}, u32[]{:S(2)}, u32[]{:S(2)}) collective-permute-start(bf16[2,32,768]{2,1,0:T(8,128)(2,1)S(1)} %get-tuple-element.61), channel_id=1, source_target_pairs={{0,20},{4,16},{8,28},{12,24},{16,4},{20,0},{24,12},{28,8},{1,21},{... | collective-permute-start | bytes 294920 | tf_op jit(solution)/shard_map/ppermute | solution.py:358
  42.2 8.8 %collective-permute-start.8 = (bf16[2,32,768]{2,1,0:T(8,128)(2,1)S(1)}, bf16[2,32,768]{2,1,0:T(8,128)(2,1)S(1)}, u32[]{:S(2)}, u32[]{:S(2)}) collective-permute-start(bf16[2,32,768]{2,1,0:T(8,128)(2,1)S(1)} %get-tuple-element.62), channel_id=1, source_target_pairs={{0,8},{4,12},{8,0},{12,4},{16,24},{20,28},{24,16},{28,20},{1,9},{5... | collective-permute-start | bytes 294920 | tf_op jit(solution)/shard_map/ppermute | solution.py:358
  43.3 7.7 %slice-start = ((s8[4718592]{0:T(1024)(128)(4,1)}), s8[4194304]{0:T(1024)(128)(4,1)S(1)}, s32[]{:S(2)}) async-start(s8[4718592]{0:T(1024)(128)(4,1)} %bitcast.7), calls=%async_computation.1 | async-start | bytes 8388608
  43.3 7.7 %slice-start.1 = ((s8[4718592]{0:T(1024)(128)(4,1)}), s8[524288]{0:T(1024)(128)(4,1)S(1)}, s32[]{:S(2)}) async-start(s8[4718592]{0:T(1024)(128)(4,1)} %bitcast.7), calls=%async_computation.2 | async-start | bytes 1048576
  46.0 8.1 %collective-permute-start.10 = (bf16[2,32,768]{2,1,0:T(8,128)(2,1)S(1)}, bf16[2,32,768]{2,1,0:T(8,128)(2,1)S(1)}, u32[]{:S(2)}, u32[]{:S(2)}) collective-permute-start(bf16[2,32,768]{2,1,0:T(8,128)(2,1)S(1)} %get-tuple-element.72), channel_id=1, source_target_pairs={{0,16},{4,20},{8,24},{12,28},{16,0},{20,4},{24,8},{28,12},{1,17},{... | collective-permute-start | bytes 294920 | tf_op jit(solution)/shard_map/ppermute | solution.py:358
  47.9 6.2 %copy-start.5 = (bf16[768,2]{0,1:T(2,128)(2,1)S(1)}, bf16[768,2]{0,1:T(2,128)(2,1)}, u32[]{:S(2)}) copy-start(bf16[768,2]{0,1:T(2,128)(2,1)} %param.29) | copy-start | bytes 9220
  47.9 6.3 %copy-start.6 = (s32[16]{0:T(128)S(1)}, s32[16]{0:T(128)}, u32[]{:S(2)}) copy-start(s32[16]{0:T(128)} %get-tuple-element.39.place) | copy-start | bytes 196
  47.9 6.2 %collective-permute-start.11 = (bf16[2,32,768]{2,1,0:T(8,128)(2,1)S(1)}, bf16[2,32,768]{2,1,0:T(8,128)(2,1)S(1)}, u32[]{:S(2)}, u32[]{:S(2)}) collective-permute-start(bf16[2,32,768]{2,1,0:T(8,128)(2,1)S(1)} %get-tuple-element.73), channel_id=1, source_target_pairs={{0,12},{4,8},{8,4},{12,0},{16,28},{20,24},{24,20},{28,16},{1,13},{... | collective-permute-start | bytes 294920 | tf_op jit(solution)/shard_map/ppermute | solution.py:358

commit v5 on v4

--- a/solution.py
+++ b/solution.py
@@ -127,19 +127,24 @@
     )(table, own, sibling)
 
 
-def project_kernel(images, weight, out):
+def project_kernel(turned, images, weight, out):
     count, rows, width = images.shape
     whole = rows // 16 * 16
     for image in range(count):
-        out[image, whole:, :] = jnp.zeros((KEY_PAD - whole, width), BF16)
-        out[image, :rows, :] = jnp.dot(images[image], weight[...], preferred_element_type=F32).astype(BF16)
-
-
-def project_images(images, weight):
+        found = jnp.dot(images[image], weight[...], preferred_element_type=F32).astype(BF16)
+        if turned:
+            out[image] = jnp.concatenate([found, jnp.zeros((KEY_PAD - rows, width), BF16)], axis=0).T
+        else:
+            out[image, whole:, :] = jnp.zeros((KEY_PAD - whole, width), BF16)
+            out[image, :rows, :] = found
+
+
+def project_images(images, weight, turned):
     count, rows, width = images.shape
-    return pl.pallas_call(
-        project_kernel,
-        out_shape=jax.ShapeDtypeStruct((count, KEY_PAD, width), BF16),
+    shape = (count, width, KEY_PAD) if turned else (count, KEY_PAD, width)
+    return pl.pallas_call(
+        functools.partial(project_kernel, turned),
+        out_shape=jax.ShapeDtypeStruct(shape, BF16),
         in_specs=[VMEM] * 2,
         out_specs=VMEM,
         compiler_params=params(16),
@@ -195,12 +200,7 @@
                 axis=0,
             )
             found.append(
-                lax.dot_general(
-                    stacked,
-                    keys[images[pair], :, span],
-                    (((1,), (1,)), ((), ())),
-                    preferred_element_type=F32,
-                )
+                jnp.dot(stacked, keys[images[pair], span, :], preferred_element_type=F32)
             )
         return found
 
@@ -210,8 +210,10 @@
             top = jnp.max(scores, axis=-1, keepdims=True)
             weights = jnp.exp(scores - top)
             share = 1.0 / jnp.sum(weights, axis=-1, keepdims=True)
-            probs = (weights * share).astype(BF16)
-            mixed = jnp.dot(probs, values[images[pair], :, span], preferred_element_type=F32)
+            mixed = jnp.dot(
+                weights.astype(BF16), values[images[pair], :, span], preferred_element_type=F32
+            )
+            mixed = mixed * share
             joined = mixed[:tokens]
             for head in range(1, heads):
                 joined = jnp.where(lane_head == head, mixed[head * tokens : (head + 1) * tokens], joined)
@@ -362,9 +364,9 @@
         pair_list.T, verify_order, image_slot, caption_slot, images.shape[0], img_count, cap_count
     )
     table = lax.all_to_all(table, ("img", "cap"), split_axis=0, concat_axis=0, tiled=True)
-    keys = project_images(images, key_weight)
+    keys = project_images(images, key_weight, True)
     value_weight, keys = lax.optimization_barrier((value_weight, keys))
-    values = project_images(images, value_weight)
+    values = project_images(images, value_weight, False)
     pinned = pltpu.with_memory_space_constraint(captions, pltpu.HBM)
     far = [[] for _ in chunks]
     for step in far_steps:

time: 58.9 us -> 59.1 us (level)
  waiting for transfers between devices: 0.22 us -> 1.25 us
  Pallas kernels: 26.7 us -> 25.9 us
    ppermute x12, waiting for transfers between devices: 0.22 us -> 1.25 us  [swap(): lax.ppermute(array, axis, [(peer, peer ^ distance) for peer in range(size)])]
    pallas_call x4, Pallas kernels: 10.1 us -> 9.19 us  [attend(): pl.pallas_call(functools.partial(attend_kernel, key_rows, len(far), chunk...]
  transfers between devices with their start and end apart: 12 -> 12, of which waited for: 1 -> 1; matrix products, arithmetic and copies ran while one was open for 1% -> 1% of each run, Pallas kernels for 33% -> 31%
where the time goes in v5:
time: 59.1 us; the launch traced here: 58.8 us
  Pallas kernels  25.9 us (44%)
  starting transfers between devices  16 us (27%)
  blocking collectives  14.1 us (24%)
  waiting for transfers between devices  1.25 us (2%)
  between operations  0.91 us (2%)
  local copies, waits for them, and re-layouts  0.74 us (1%)
    ppermute x12, starting transfers between devices, swap(): lax.ppermute(array, axis, [(peer, peer ^ distance) for peer in range(size)])  16 us
    all_to_all x1, blocking collectives, body(): lax.all_to_all(table, ('img', 'cap'), split_axis=0, concat_axis=0, tiled=...  14.1 us
    pallas_call x4, Pallas kernels, attend(): pl.pallas_call(functools.partial(attend_kernel, key_rows, len(far), chunk...  9.19 us
    pallas_call x2, Pallas kernels, project_images(): pl.pallas_call(functools.partial(project_kernel, turned), out_shape=jax.S...  4.5 us
    pallas_call x1, Pallas kernels, feed_last(): pl.pallas_call(functools.partial(feed_last_kernel, first_parts, last_part...  4.47 us
    pallas_call x1, Pallas kernels, feed_first(): pl.pallas_call(feed_first_kernel, out_shape=jax.ShapeDtypeStruct((slots,...  3.04 us
    pallas_call x1, Pallas kernels, pick_blocks(): pl.pallas_call(functools.partial(pick_kernel, step, cap_count, chunks), o...  2.92 us
    pallas_call x1, Pallas kernels, make_table(): pl.pallas_call(functools.partial(table_kernel, image_local, caption_count...  1.76 us
  transfers between devices with their start and end apart: 12, of which 1 were waited for; matrix products, arithmetic and copies ran while one was open for 1% of the time, Pallas kernels for 31%

profile of v5, /device:TPU:0, one launch (start us, length us, event | category | flops | bytes accessed | tf_op | source)
XLA Modules:
  0.0 58.8 jit_solution(6037816339731856160)
XLA Ops:
  0.6 0.5 collective-permute-start
  1.1 1.8 %slot_table.1 = (s32[32,128]{1,0:T(8,128)}, s32[16]{0:T(128)}) custom-call(s32[2,512]{1,0:T(2,128)} %bitcast.14, s32[16]{0:T(128)} %order.1, s32[64]{0:T(128)} %image_slot.1, s32[128]{0:T(128)} %caption_slot.1), custom_call_target="tpu_custom_call" | custom-call | tf_op jit(solution)/shard_map/slot_table/pallas_call | solution.py:60
  2.9 0.0 copy-start.7
  2.9 14.1 %all_to_all.11 = s32[32,1,128]{2,1,0:T(1,128)S(1)} all-to-all(s32[32,1,128]{2,1,0:T(1,128)} %bitcast.13), channel_id=1, replica_groups=mesh['img'=8,'cap'=4] {'img','cap'}, dimensions={0} | all-to-all | bytes 32768 | tf_op jit(solution)/shard_map/all_to_all | solution.py:366
  17.0 0.0 collective-permute-done.sibling
  17.0 2.9 %pick_captions.1 = (s32[16]{0:T(128)S(1)}, bf16[4,32,768]{2,1,0:T(8,128)(2,1)S(1)}, bf16[4,32,768]{2,1,0:T(8,128)(2,1)S(1)}, bf16[4,32,768]{2,1,0:T(8,128)(2,1)S(1)}, bf16[4,32,768]{2,1,0:T(8,128)(2,1)S(1)}) custom-call(s32[32,128]{1,0:T(8,128)S(1)} %bitcast.11, bf16[32,32,768]{2,1,0:T(8,128)(2,1)} %own.7, bf16[32,32,768]{2,1,0:T(8,128)(2,1)S(1)} %collective-permute-done.sibling), custom_call_target="tpu_custom_call" | custom-call | flops 65536 | bytes 1024 | tf_op jit(solution)/shard_map/pick_captions/pallas_call | solution.py:118
  19.9 0.0 copy-start.3
  19.9 0.6 collective-permute-start.1
  20.5 0.0 copy-done.7
  20.5 0.5 copy.20.images
  21.0 0.2 copy-done.3
  21.2 0.0 copy-start.4
  21.2 2.3 %project_images.2.rest_1_ = bf16[8,768,256]{2,1,0:T(8,128)(2,1)S(1)} custom-call(bf16[8,197,768]{2,1,0:T(8,128)(2,1)S(1)} %copy.20.images, bf16[768,768]{1,0:T(8,128)(2,1)S(1)} %copy-done.3), custom_call_target="tpu_custom_call" | custom-call | flops 65536 | bytes 1024 | tf_op jit(solution)/shard_map/project_images/pallas_call | solution.py:145
  23.5 0.0 copy-start.8
  23.5 0.0 copy-start
  23.5 0.0 copy-start.1
  23.5 0.0 copy-start.2
  23.6 1.4 %collective-permute-start.3 = (bf16[4,32,768]{2,1,0:T(8,128)(2,1)S(1)}, bf16[4,32,768]{2,1,0:T(8,128)(2,1)S(1)}, u32[]{:S(2)}, u32[]{:S(2)}) collective-permute-start(bf16[4,32,768]{2,1,0:T(8,128)(2,1)S(1)} %get-tuple-element.55), channel_id=1, source_target_pairs={{0,2},{1,3},{2,0},{3,1},{4,6},{5,7},{6,4},{7,5},{8,10},{9,11},{10,... | collective-permute-start | bytes 589832 | tf_op jit(solution)/shard_map/ppermute | solution.py:360
  24.9 0.0 copy-done.4
  24.9 2.2 %project_images.3.rest_2_ = bf16[8,256,768]{2,1,0:T(8,128)(2,1)S(1)} custom-call(bf16[8,197,768]{2,1,0:T(8,128)(2,1)S(1)} %copy.20.images, bf16[768,768]{1,0:T(8,128)(2,1)S(1)} %copy-done.4), custom_call_target="tpu_custom_call" | custom-call | flops 65536 | bytes 1024 | tf_op jit(solution)/shard_map/project_images/pallas_call | solution.py:145
  27.1 0.8 %collective-permute-start.6 = (bf16[4,32,768]{2,1,0:T(8,128)(2,1)S(1)}, bf16[4,32,768]{2,1,0:T(8,128)(2,1)S(1)}, u32[]{:S(2)}, u32[]{:S(2)}) collective-permute-start(bf16[4,32,768]{2,1,0:T(8,128)(2,1)S(1)} %get-tuple-element.60), channel_id=1, source_target_pairs={{0,2},{1,3},{2,0},{3,1},{4,6},{5,7},{6,4},{7,5},{8,10},{9,11},{10,... | collective-permute-start | bytes 589832 | tf_op jit(solution)/shard_map/ppermute | solution.py:360
  27.9 0.0 copy-done.8
  27.9 0.0 collective-permute-done.1.rest_0_
  27.9 0.0 copy-done
  27.9 0.0 copy-done.1
  27.9 0.0 copy-done.2
  28.0 2.3 %attend.4 = (bf16[2,32,768]{2,1,0:T(8,128)(2,1)S(1)}, bf16[2,32,768]{2,1,0:T(8,128)(2,1)S(1)}) custom-call(s32[16]{0:T(128)S(1)} %get-tuple-element.70.slots, bf16[32,32,768]{2,1,0:T(8,128)(2,1)S(1)} %copy-done, bf16[32,32,768]{2,1,0:T(8,128)(2,1)S(1)} %collective-permute-done.sibling, bf16[4,32,768]{2,1,0:T(8,128)(2,1)S(1)} %collective-permute-done.1.rest_0_, ...), custom_call_target="tpu_custom_call" | custom-call | flops 65536 | bytes 1024 | tf_op jit(solution)/shard_map/attend/pallas_call | solution.py:235
  30.2 0.6 %collective-permute-start.2 = (bf16[2,32,768]{2,1,0:T(8,128)(2,1)S(1)}, bf16[2,32,768]{2,1,0:T(8,128)(2,1)S(1)}, u32[]{:S(2)}, u32[]{:S(2)}) collective-permute-start(bf16[2,32,768]{2,1,0:T(8,128)(2,1)S(1)} %get-tuple-element.50), channel_id=1, source_target_pairs={{0,28},{4,24},{8,20},{12,16},{16,12},{20,8},{24,4},{28,0},{1,29},{... | collective-permute-start | bytes 294920 | tf_op jit(solution)/shard_map/ppermute | solution.py:360
  30.8 1.3 %collective-permute-start.9 = (bf16[4,32,768]{2,1,0:T(8,128)(2,1)S(1)}, bf16[4,32,768]{2,1,0:T(8,128)(2,1)S(1)}, u32[]{:S(2)}, u32[]{:S(2)}) collective-permute-start(bf16[4,32,768]{2,1,0:T(8,128)(2,1)S(1)} %get-tuple-element.71), channel_id=1, source_target_pairs={{0,2},{1,3},{2,0},{3,1},{4,6},{5,7},{6,4},{7,5},{8,10},{9,11},{10,... | collective-permute-start | bytes 589832 | tf_op jit(solution)/shard_map/ppermute | solution.py:360
  32.1 0.0 collective-permute-done.3.rest_0_
  32.1 0.0 slice-start.2
  32.1 2.2 %attend.5 = (bf16[2,32,768]{2,1,0:T(8,128)(2,1)S(1)}, bf16[2,32,768]{2,1,0:T(8,128)(2,1)S(1)}) custom-call(s32[16]{0:T(128)S(1)} %get-tuple-element.70.slots, bf16[32,32,768]{2,1,0:T(8,128)(2,1)S(1)} %copy-done, bf16[32,32,768]{2,1,0:T(8,128)(2,1)S(1)} %collective-permute-done.sibling, bf16[4,32,768]{2,1,0:T(8,128)(2,1)S(1)} %collective-permute-done.3.rest_0_, ...), custom_call_target="tpu_custom_call" | custom-call | flops 65536 | bytes 1024 | tf_op jit(solution)/shard_map/attend/pallas_call | solution.py:235
  34.4 3.3 %collective-permute-start.4 = (bf16[2,32,768]{2,1,0:T(8,128)(2,1)S(1)}, bf16[2,32,768]{2,1,0:T(8,128)(2,1)S(1)}, u32[]{:S(2)}, u32[]{:S(2)}) collective-permute-start(bf16[2,32,768]{2,1,0:T(8,128)(2,1)S(1)} %get-tuple-element.56), channel_id=1, source_target_pairs={{0,24},{4,28},{8,16},{12,20},{16,8},{20,12},{24,0},{28,4},{1,25},{... | collective-permute-start | bytes 294920 | tf_op jit(solution)/shard_map/ppermute | solution.py:360
  37.7 1.5 %collective-permute-start.5 = (bf16[2,32,768]{2,1,0:T(8,128)(2,1)S(1)}, bf16[2,32,768]{2,1,0:T(8,128)(2,1)S(1)}, u32[]{:S(2)}, u32[]{:S(2)}) collective-permute-start(bf16[2,32,768]{2,1,0:T(8,128)(2,1)S(1)} %get-tuple-element.57), channel_id=1, source_target_pairs={{0,4},{4,0},{8,12},{12,8},{16,20},{20,16},{24,28},{28,24},{1,5},{5... | collective-permute-start | bytes 294920 | tf_op jit(solution)/shard_map/ppermute | solution.py:360
  39.2 0.0 collective-permute-done.2.rest_0_
  39.2 0.0 copy-start.9
  39.2 0.0 slice-start.3
  39.2 0.0 collective-permute-done.6.rest_0_
  39.2 2.3 %attend.6 = (bf16[2,32,768]{2,1,0:T(8,128)(2,1)S(1)}, bf16[2,32,768]{2,1,0:T(8,128)(2,1)S(1)}) custom-call(s32[16]{0:T(128)S(1)} %get-tuple-element.70.slots, bf16[32,32,768]{2,1,0:T(8,128)(2,1)S(1)} %copy-done, bf16[32,32,768]{2,1,0:T(8,128)(2,1)S(1)} %collective-permute-done.sibling, bf16[4,32,768]{2,1,0:T(8,128)(2,1)S(1)} %collective-permute-done.6.rest_0_, ...), custom_call_target="tpu_custom_call" | custom-call | flops 65536 | bytes 1024 | tf_op jit(solution)/shard_map/attend/pallas_call | solution.py:235
  41.5 0.1 collective-permute-start.7
  41.6 1.1 %collective-permute-start.8 = (bf16[2,32,768]{2,1,0:T(8,128)(2,1)S(1)}, bf16[2,32,768]{2,1,0:T(8,128)(2,1)S(1)}, u32[]{:S(2)}, u32[]{:S(2)}) collective-permute-start(bf16[2,32,768]{2,1,0:T(8,128)(2,1)S(1)} %get-tuple-element.62), channel_id=1, source_target_pairs={{0,8},{4,12},{8,0},{12,4},{16,24},{20,28},{24,16},{28,20},{1,9},{5... | collective-permute-start | bytes 294920 | tf_op jit(solution)/shard_map/ppermute | solution.py:360
  42.7 0.0 copy-done.9
  42.7 0.0 slice-start
  42.7 0.0 slice-start.1
  42.7 0.0 collective-permute-done.4.rest_2_
  42.7 0.0 collective-permute-done.5.rest_3_
  42.7 0.0 collective-permute-done.9.rest_0_
  42.7 2.4 %attend.7 = (bf16[2,32,768]{2,1,0:T(8,128)(2,1)S(1)}, bf16[2,32,768]{2,1,0:T(8,128)(2,1)S(1)}) custom-call(s32[16]{0:T(128)S(1)} %get-tuple-element.70.slots, bf16[32,32,768]{2,1,0:T(8,128)(2,1)S(1)} %copy-done, bf16[32,32,768]{2,1,0:T(8,128)(2,1)S(1)} %collective-permute-done.sibling, bf16[4,32,768]{2,1,0:T(8,128)(2,1)S(1)} %collective-permute-done.9.rest_0_, ...), custom_call_target="tpu_custom_call" | custom-call | flops 65536 | bytes 1024 | tf_op jit(solution)/shard_map/attend/pallas_call | solution.py:235
  45.2 1.9 %collective-permute-start.10 = (bf16[2,32,768]{2,1,0:T(8,128)(2,1)S(1)}, bf16[2,32,768]{2,1,0:T(8,128)(2,1)S(1)}, u32[]{:S(2)}, u32[]{:S(2)}) collective-permute-start(bf16[2,32,768]{2,1,0:T(8,128)(2,1)S(1)} %get-tuple-element.72), channel_id=1, source_target_pairs={{0,16},{4,20},{8,24},{12,28},{16,0},{20,4},{24,8},{28,12},{1,17},{... | collective-permute-start | bytes 294920 | tf_op jit(solution)/shard_map/ppermute | solution.py:360
  47.0 0.0 copy-start.5
  47.0 0.0 copy-start.6
  47.0 2.9 %collective-permute-start.11 = (bf16[2,32,768]{2,1,0:T(8,128)(2,1)S(1)}, bf16[2,32,768]{2,1,0:T(8,128)(2,1)S(1)}, u32[]{:S(2)}, u32[]{:S(2)}) collective-permute-start(bf16[2,32,768]{2,1,0:T(8,128)(2,1)S(1)} %get-tuple-element.73), channel_id=1, source_target_pairs={{0,12},{4,8},{8,4},{12,0},{16,28},{20,24},{24,20},{28,16},{1,13},{... | collective-permute-start | bytes 294920 | tf_op jit(solution)/shard_map/ppermute | solution.py:360
  50.0 1.2 %collective-permute-done.7.rest_0_ = bf16[2,32,768]{2,1,0:T(8,128)(2,1)S(1)} collective-permute-done((bf16[2,32,768]{2,1,0:T(8,128)(2,1)S(1)}, bf16[2,32,768]{2,1,0:T(8,128)(2,1)S(1)}, u32[]{:S(2)}, u32[]{:S(2)}) %collective-permute-start.7) | collective-permute-done | bytes 98336 | tf_op jit(solution)/shard_map/ppermute | solution.py:360
  51.2 0.0 collective-permute-done.8.rest_1_
  51.2 0.0 slice-done.2
  51.2 0.0 slice-done.3
  51.2 0.0 slice-done
  51.2 0.0 slice-done.1
  51.2 3.0 %feed_first.1.earlier = bf16[8,32,768]{2,1,0:T(8,128)(2,1)S(1)} custom-call(f32[1,768]{1,0:T(1,128)S(1)} %reshape.12.gain, bf16[768,3072]{1,0:T(8,128)(2,1)S(1)} %bitcast.8, bf16[3072,768]{1,0:T(8,128)(2,1)S(1)} %bitcast.10, bf16[2,32,768]{2,1,0:T(8,128)(2,1)S(1)} %collective-permute-done.2.rest_0_, bf16[2,32,768]{2,1,0:T(8,128)(2,1)S(1)} %get-tuple-element.65.rest_1_, ...), custom_call_target="tpu_custom_call" | custom-call | flops 2415919104 | bytes 9437184 | tf_op jit(solution)/shard_map/feed_first/pallas_call | solution.py:303
  54.3 0.0 collective-permute-done.10.rest_2_
  54.3 0.0 collective-permute-done.11.rest_3_
  54.3 0.0 copy-done.5
  54.3 0.0 copy-done.6
  54.3 4.5 %feed_last.1 = (bf16[16,32,768]{2,1,0:T(8,128)(2,1)}, f32[2,16]{1,0:T(2,128)}) custom-call(s32[16]{0:T(128)S(1)} %copy-done.6, f32[1,768]{1,0:T(1,128)S(1)} %reshape.12.gain, bf16[2,768]{1,0:T(2,128)(2,1)S(1)} %bitcast.12, bf16[768,3072]{1,0:T(8,128)(2,1)S(1)} %bitcast.8, bf16[3072,768]{1,0:T(8,128)(2,1)S(1)} %bitcast.10, ...), custom_call_target="tpu_custom_call" | custom-call | flops 2415919104 | bytes 9437184 | tf_op jit(solution)/shard_map/feed_last/pallas_call | solution.py:318
  (4 shorter events, 0.0 us)
Async XLA Ops:
  0.6 16.4 %collective-permute-start = (bf16[32,32,768]{2,1,0:T(8,128)(2,1)}, bf16[32,32,768]{2,1,0:T(8,128)(2,1)S(1)}, u32[]{:S(2)}, u32[]{:S(2)}) collective-permute-start(bf16[32,32,768]{2,1,0:T(8,128)(2,1)} %own.7), channel_id=1, source_target_pairs={{0,1},{1,0},{2,3},{3,2},{4,5},{5,4},{6,7},{7,6},{8,9},{9,8},{10,11... | collective-permute-start | bytes 4718600 | tf_op jit(solution)/shard_map/ppermute | solution.py:360
  2.9 17.6 %copy-start.7 = (bf16[8,197,768]{2,0,1:T(8,128)(2,1)S(1)}, bf16[8,197,768]{2,0,1:T(8,128)(2,1)}, u32[]{:S(2)}) copy-start(bf16[8,197,768]{2,0,1:T(8,128)(2,1)} %param.19) | copy-start | bytes 7262212
  19.9 1.3 %copy-start.3 = (bf16[768,768]{1,0:T(8,128)(2,1)S(1)}, bf16[768,768]{1,0:T(8,128)(2,1)}, u32[]{:S(2)}) copy-start(bf16[768,768]{1,0:T(8,128)(2,1)} %weight.1) | copy-start | bytes 3538948
  19.9 8.0 %collective-permute-start.1 = (bf16[4,32,768]{2,1,0:T(8,128)(2,1)S(1)}, bf16[4,32,768]{2,1,0:T(8,128)(2,1)S(1)}, u32[]{:S(2)}, u32[]{:S(2)}) collective-permute-start(bf16[4,32,768]{2,1,0:T(8,128)(2,1)S(1)} %get-tuple-element.42), channel_id=1, source_target_pairs={{0,2},{1,3},{2,0},{3,1},{4,6},{5,7},{6,4},{7,5},{8,10},{9,11},{10,... | collective-permute-start | bytes 589832 | tf_op jit(solution)/shard_map/ppermute | solution.py:360
  21.2 3.8 %copy-start.4 = (bf16[768,768]{1,0:T(8,128)(2,1)S(1)}, bf16[768,768]{1,0:T(8,128)(2,1)}, u32[]{:S(2)}) copy-start(bf16[768,768]{1,0:T(8,128)(2,1)} %weight.2) | copy-start | bytes 3538948
  23.5 4.4 %copy-start.8 = (f32[768]{0:T(1024)S(1)}, f32[768]{0:T(1024)}, u32[]{:S(2)}) copy-start(f32[768]{0:T(1024)} %param.25) | copy-start | bytes 9220
  23.5 4.4 %copy-start = (bf16[32,32,768]{2,1,0:T(8,128)(2,1)S(1)}, bf16[32,32,768]{2,1,0:T(8,128)(2,1)}, u32[]{:S(2)}) copy-start(bf16[32,32,768]{2,1,0:T(8,128)(2,1)} %own.7) | copy-start | bytes 4718596
  23.5 4.4 %copy-start.1 = (bf16[768,768]{1,0:T(8,128)(2,1)S(1)}, bf16[768,768]{1,0:T(8,128)(2,1)}, u32[]{:S(2)}) copy-start(bf16[768,768]{1,0:T(8,128)(2,1)} %rest_3_.7) | copy-start | bytes 3538948
  23.5 4.4 %copy-start.2 = (bf16[768,768]{1,0:T(8,128)(2,1)S(1)}, bf16[768,768]{1,0:T(8,128)(2,1)}, u32[]{:S(2)}) copy-start(bf16[768,768]{1,0:T(8,128)(2,1)} %rest_4_.7) | copy-start | bytes 3538948
  23.6 8.6 %collective-permute-start.3 = (bf16[4,32,768]{2,1,0:T(8,128)(2,1)S(1)}, bf16[4,32,768]{2,1,0:T(8,128)(2,1)S(1)}, u32[]{:S(2)}, u32[]{:S(2)}) collective-permute-start(bf16[4,32,768]{2,1,0:T(8,128)(2,1)S(1)} %get-tuple-element.55), channel_id=1, source_target_pairs={{0,2},{1,3},{2,0},{3,1},{4,6},{5,7},{6,4},{7,5},{8,10},{9,11},{10,... | collective-permute-start | bytes 589832 | tf_op jit(solution)/shard_map/ppermute | solution.py:360
  27.1 12.1 %collective-permute-start.6 = (bf16[4,32,768]{2,1,0:T(8,128)(2,1)S(1)}, bf16[4,32,768]{2,1,0:T(8,128)(2,1)S(1)}, u32[]{:S(2)}, u32[]{:S(2)}) collective-permute-start(bf16[4,32,768]{2,1,0:T(8,128)(2,1)S(1)} %get-tuple-element.60), channel_id=1, source_target_pairs={{0,2},{1,3},{2,0},{3,1},{4,6},{5,7},{6,4},{7,5},{8,10},{9,11},{10,... | collective-permute-start | bytes 589832 | tf_op jit(solution)/shard_map/ppermute | solution.py:360
  30.2 9.0 %collective-permute-start.2 = (bf16[2,32,768]{2,1,0:T(8,128)(2,1)S(1)}, bf16[2,32,768]{2,1,0:T(8,128)(2,1)S(1)}, u32[]{:S(2)}, u32[]{:S(2)}) collective-permute-start(bf16[2,32,768]{2,1,0:T(8,128)(2,1)S(1)} %get-tuple-element.50), channel_id=1, source_target_pairs={{0,28},{4,24},{8,20},{12,16},{16,12},{20,8},{24,4},{28,0},{1,29},{... | collective-permute-start | bytes 294920 | tf_op jit(solution)/shard_map/ppermute | solution.py:360
  30.8 11.9 %collective-permute-start.9 = (bf16[4,32,768]{2,1,0:T(8,128)(2,1)S(1)}, bf16[4,32,768]{2,1,0:T(8,128)(2,1)S(1)}, u32[]{:S(2)}, u32[]{:S(2)}) collective-permute-start(bf16[4,32,768]{2,1,0:T(8,128)(2,1)S(1)} %get-tuple-element.71), channel_id=1, source_target_pairs={{0,2},{1,3},{2,0},{3,1},{4,6},{5,7},{6,4},{7,5},{8,10},{9,11},{10,... | collective-permute-start | bytes 589832 | tf_op jit(solution)/shard_map/ppermute | solution.py:360
  32.1 19.1 %slice-start.2 = ((s8[4718592]{0:T(1024)(128)(4,1)}), s8[4194304]{0:T(1024)(128)(4,1)S(1)}, s32[]{:S(2)}) async-start(s8[4718592]{0:T(1024)(128)(4,1)} %bitcast.9), calls=%async_computation.3 | async-start | bytes 8388608
  34.4 8.3 %collective-permute-start.4 = (bf16[2,32,768]{2,1,0:T(8,128)(2,1)S(1)}, bf16[2,32,768]{2,1,0:T(8,128)(2,1)S(1)}, u32[]{:S(2)}, u32[]{:S(2)}) collective-permute-start(bf16[2,32,768]{2,1,0:T(8,128)(2,1)S(1)} %get-tuple-element.56), channel_id=1, source_target_pairs={{0,24},{4,28},{8,16},{12,20},{16,8},{20,12},{24,0},{28,4},{1,25},{... | collective-permute-start | bytes 294920 | tf_op jit(solution)/shard_map/ppermute | solution.py:360
  37.7 5.0 %collective-permute-start.5 = (bf16[2,32,768]{2,1,0:T(8,128)(2,1)S(1)}, bf16[2,32,768]{2,1,0:T(8,128)(2,1)S(1)}, u32[]{:S(2)}, u32[]{:S(2)}) collective-permute-start(bf16[2,32,768]{2,1,0:T(8,128)(2,1)S(1)} %get-tuple-element.57), channel_id=1, source_target_pairs={{0,4},{4,0},{8,12},{12,8},{16,20},{20,16},{24,28},{28,24},{1,5},{5... | collective-permute-start | bytes 294920 | tf_op jit(solution)/shard_map/ppermute | solution.py:360
  39.2 3.4 %copy-start.9 = (f32[768]{0:T(1024)S(1)}, f32[768]{0:T(1024)}, u32[]{:S(2)}) copy-start(f32[768]{0:T(1024)} %param.28) | copy-start | bytes 9220
  39.2 12.0 %slice-start.3 = ((s8[4718592]{0:T(1024)(128)(4,1)}), s8[524288]{0:T(1024)(128)(4,1)S(1)}, s32[]{:S(2)}) async-start(s8[4718592]{0:T(1024)(128)(4,1)} %bitcast.9), calls=%async_computation.4 | async-start | bytes 1048576
  41.5 9.7 %collective-permute-start.7 = (bf16[2,32,768]{2,1,0:T(8,128)(2,1)S(1)}, bf16[2,32,768]{2,1,0:T(8,128)(2,1)S(1)}, u32[]{:S(2)}, u32[]{:S(2)}) collective-permute-start(bf16[2,32,768]{2,1,0:T(8,128)(2,1)S(1)} %get-tuple-element.61), channel_id=1, source_target_pairs={{0,20},{4,16},{8,28},{12,24},{16,4},{20,0},{24,12},{28,8},{1,21},{... | collective-permute-start | bytes 294920 | tf_op jit(solution)/shard_map/ppermute | solution.py:360
  41.6 9.6 %collective-permute-start.8 = (bf16[2,32,768]{2,1,0:T(8,128)(2,1)S(1)}, bf16[2,32,768]{2,1,0:T(8,128)(2,1)S(1)}, u32[]{:S(2)}, u32[]{:S(2)}) collective-permute-start(bf16[2,32,768]{2,1,0:T(8,128)(2,1)S(1)} %get-tuple-element.62), channel_id=1, source_target_pairs={{0,8},{4,12},{8,0},{12,4},{16,24},{20,28},{24,16},{28,20},{1,9},{5... | collective-permute-start | bytes 294920 | tf_op jit(solution)/shard_map/ppermute | solution.py:360
  42.7 8.6 %slice-start = ((s8[4718592]{0:T(1024)(128)(4,1)}), s8[4194304]{0:T(1024)(128)(4,1)S(1)}, s32[]{:S(2)}) async-start(s8[4718592]{0:T(1024)(128)(4,1)} %bitcast.7), calls=%async_computation.1 | async-start | bytes 8388608
  42.7 8.6 %slice-start.1 = ((s8[4718592]{0:T(1024)(128)(4,1)}), s8[524288]{0:T(1024)(128)(4,1)S(1)}, s32[]{:S(2)}) async-start(s8[4718592]{0:T(1024)(128)(4,1)} %bitcast.7), calls=%async_computation.2 | async-start | bytes 1048576
  45.2 9.1 %collective-permute-start.10 = (bf16[2,32,768]{2,1,0:T(8,128)(2,1)S(1)}, bf16[2,32,768]{2,1,0:T(8,128)(2,1)S(1)}, u32[]{:S(2)}, u32[]{:S(2)}) collective-permute-start(bf16[2,32,768]{2,1,0:T(8,128)(2,1)S(1)} %get-tuple-element.72), channel_id=1, source_target_pairs={{0,16},{4,20},{8,24},{12,28},{16,0},{20,4},{24,8},{28,12},{1,17},{... | collective-permute-start | bytes 294920 | tf_op jit(solution)/shard_map/ppermute | solution.py:360
  47.0 7.3 %copy-start.5 = (bf16[768,2]{0,1:T(2,128)(2,1)S(1)}, bf16[768,2]{0,1:T(2,128)(2,1)}, u32[]{:S(2)}) copy-start(bf16[768,2]{0,1:T(2,128)(2,1)} %param.29) | copy-start | bytes 9220
  47.0 7.3 %copy-start.6 = (s32[16]{0:T(128)S(1)}, s32[16]{0:T(128)}, u32[]{:S(2)}) copy-start(s32[16]{0:T(128)} %get-tuple-element.39.place) | copy-start | bytes 196
  47.0 7.3 %collective-permute-start.11 = (bf16[2,32,768]{2,1,0:T(8,128)(2,1)S(1)}, bf16[2,32,768]{2,1,0:T(8,128)(2,1)S(1)}, u32[]{:S(2)}, u32[]{:S(2)}) collective-permute-start(bf16[2,32,768]{2,1,0:T(8,128)(2,1)S(1)} %get-tuple-element.73), channel_id=1, source_target_pairs={{0,12},{4,8},{8,4},{12,0},{16,28},{20,24},{24,20},{28,16},{1,13},{... | collective-permute-start | bytes 294920 | tf_op jit(solution)/shard_map/ppermute | solution.py:360

commit v6 on v5

--- a/solution.py
+++ b/solution.py
@@ -351,7 +351,7 @@
     cap_count = lax.axis_size("cap")
     far_steps = range(1, cap_count // CORES)
     half = img_count // 2
-    chunks = tuple((img_count - 1 - index, index) for index in range(half))
+    chunks = tuple((img_count - 1 - index, index ^ 1) for index in range(half))
     first_parts = sum(chunks[: half // 2], ())
     last_parts = sum(chunks[half // 2 :], ())
 

time: 59.1 us -> 57.9 us (0.980)
  waiting for transfers between devices: 1.25 us -> 0.12 us
    ppermute x12, waiting for transfers between devices: 1.25 us -> 0.12 us  [swap(): lax.ppermute(array, axis, [(peer, peer ^ distance) for peer in range(size)])]
  transfers between devices with their start and end apart: 12 -> 12, of which waited for: 1 -> 1; matrix products, arithmetic and copies ran while one was open for 1% -> 1% of each run, Pallas kernels for 31% -> 32%
where the time goes in v6:
time: 57.9 us; the launch traced here: 57.7 us
  Pallas kernels  25.9 us (45%)
  starting transfers between devices  16 us (28%)
  blocking collectives  14.1 us (24%)
  between operations  0.9 us (2%)
  local copies, waits for them, and re-layouts  0.77 us (1%)
    ppermute x12, starting transfers between devices, swap(): lax.ppermute(array, axis, [(peer, peer ^ distance) for peer in range(size)])  16 us
    all_to_all x1, blocking collectives, body(): lax.all_to_all(table, ('img', 'cap'), split_axis=0, concat_axis=0, tiled=...  14.1 us
    pallas_call x4, Pallas kernels, attend(): pl.pallas_call(functools.partial(attend_kernel, key_rows, len(far), chunk...  9.18 us
    pallas_call x2, Pallas kernels, project_images(): pl.pallas_call(functools.partial(project_kernel, turned), out_shape=jax.S...  4.5 us
    pallas_call x1, Pallas kernels, feed_last(): pl.pallas_call(functools.partial(feed_last_kernel, first_parts, last_part...  4.47 us
    pallas_call x1, Pallas kernels, feed_first(): pl.pallas_call(feed_first_kernel, out_shape=jax.ShapeDtypeStruct((slots,...  3.04 us
    pallas_call x1, Pallas kernels, pick_blocks(): pl.pallas_call(functools.partial(pick_kernel, step, cap_count, chunks), o...  2.92 us
    pallas_call x1, Pallas kernels, make_table(): pl.pallas_call(functools.partial(table_kernel, image_local, caption_count...  1.76 us
  transfers between devices with their start and end apart: 12, of which 1 were waited for; matrix products, arithmetic and copies ran while one was open for 1% of the time, Pallas kernels for 32%

profile of v6, /device:TPU:0, one launch (start us, length us, event | category | flops | bytes accessed | tf_op | source)
XLA Modules:
  0.0 57.7 jit_solution(14664919115349963180)
XLA Ops:
  0.6 0.5 collective-permute-start
  1.1 1.8 %slot_table.1 = (s32[32,128]{1,0:T(8,128)}, s32[16]{0:T(128)}) custom-call(s32[2,512]{1,0:T(2,128)} %bitcast.14, s32[16]{0:T(128)} %order.1, s32[64]{0:T(128)} %image_slot.1, s32[128]{0:T(128)} %caption_slot.1), custom_call_target="tpu_custom_call" | custom-call | tf_op jit(solution)/shard_map/slot_table/pallas_call | solution.py:60
  2.9 0.0 copy-start.7
  2.9 14.1 %all_to_all.11 = s32[32,1,128]{2,1,0:T(1,128)S(1)} all-to-all(s32[32,1,128]{2,1,0:T(1,128)} %bitcast.13), channel_id=1, replica_groups=mesh['img'=8,'cap'=4] {'img','cap'}, dimensions={0} | all-to-all | bytes 32768 | tf_op jit(solution)/shard_map/all_to_all | solution.py:366
  17.0 0.0 collective-permute-done.sibling
  17.0 2.9 %pick_captions.1 = (s32[16]{0:T(128)S(1)}, bf16[4,32,768]{2,1,0:T(8,128)(2,1)S(1)}, bf16[4,32,768]{2,1,0:T(8,128)(2,1)S(1)}, bf16[4,32,768]{2,1,0:T(8,128)(2,1)S(1)}, bf16[4,32,768]{2,1,0:T(8,128)(2,1)S(1)}) custom-call(s32[32,128]{1,0:T(8,128)S(1)} %bitcast.11, bf16[32,32,768]{2,1,0:T(8,128)(2,1)} %own.7, bf16[32,32,768]{2,1,0:T(8,128)(2,1)S(1)} %collective-permute-done.sibling), custom_call_target="tpu_custom_call" | custom-call | flops 65536 | bytes 1024 | tf_op jit(solution)/shard_map/pick_captions/pallas_call | solution.py:118
  19.9 0.0 copy-start.3
  19.9 0.6 collective-permute-start.1
  20.5 0.0 copy-done.7
  20.5 0.5 copy.20.images
  21.0 0.2 copy-done.3
  21.2 0.0 copy-start.4
  21.2 2.3 %project_images.2.rest_1_ = bf16[8,768,256]{2,1,0:T(8,128)(2,1)S(1)} custom-call(bf16[8,197,768]{2,1,0:T(8,128)(2,1)S(1)} %copy.20.images, bf16[768,768]{1,0:T(8,128)(2,1)S(1)} %copy-done.3), custom_call_target="tpu_custom_call" | custom-call | flops 65536 | bytes 1024 | tf_op jit(solution)/shard_map/project_images/pallas_call | solution.py:145
  23.5 0.0 copy-start.8
  23.5 0.0 copy-start
  23.5 0.0 copy-start.1
  23.5 0.0 copy-start.2
  23.6 1.4 %collective-permute-start.4 = (bf16[4,32,768]{2,1,0:T(8,128)(2,1)S(1)}, bf16[4,32,768]{2,1,0:T(8,128)(2,1)S(1)}, u32[]{:S(2)}, u32[]{:S(2)}) collective-permute-start(bf16[4,32,768]{2,1,0:T(8,128)(2,1)S(1)} %get-tuple-element.55), channel_id=1, source_target_pairs={{0,2},{1,3},{2,0},{3,1},{4,6},{5,7},{6,4},{7,5},{8,10},{9,11},{10,... | collective-permute-start | bytes 589832 | tf_op jit(solution)/shard_map/ppermute | solution.py:360
  24.9 0.0 copy-done.4
  24.9 2.2 %project_images.3.rest_2_ = bf16[8,256,768]{2,1,0:T(8,128)(2,1)S(1)} custom-call(bf16[8,197,768]{2,1,0:T(8,128)(2,1)S(1)} %copy.20.images, bf16[768,768]{1,0:T(8,128)(2,1)S(1)} %copy-done.4), custom_call_target="tpu_custom_call" | custom-call | flops 65536 | bytes 1024 | tf_op jit(solution)/shard_map/project_images/pallas_call | solution.py:145
  27.1 0.8 %collective-permute-start.6 = (bf16[4,32,768]{2,1,0:T(8,128)(2,1)S(1)}, bf16[4,32,768]{2,1,0:T(8,128)(2,1)S(1)}, u32[]{:S(2)}, u32[]{:S(2)}) collective-permute-start(bf16[4,32,768]{2,1,0:T(8,128)(2,1)S(1)} %get-tuple-element.60), channel_id=1, source_target_pairs={{0,2},{1,3},{2,0},{3,1},{4,6},{5,7},{6,4},{7,5},{8,10},{9,11},{10,... | collective-permute-start | bytes 589832 | tf_op jit(solution)/shard_map/ppermute | solution.py:360
  27.9 0.0 copy-done.8
  27.9 0.0 collective-permute-done.1.rest_0_
  27.9 0.0 copy-done
  27.9 0.0 copy-done.1
  27.9 0.0 copy-done.2
  28.0 2.2 %attend.4 = (bf16[2,32,768]{2,1,0:T(8,128)(2,1)S(1)}, bf16[2,32,768]{2,1,0:T(8,128)(2,1)S(1)}) custom-call(s32[16]{0:T(128)S(1)} %get-tuple-element.70.slots, bf16[32,32,768]{2,1,0:T(8,128)(2,1)S(1)} %copy-done, bf16[32,32,768]{2,1,0:T(8,128)(2,1)S(1)} %collective-permute-done.sibling, bf16[4,32,768]{2,1,0:T(8,128)(2,1)S(1)} %collective-permute-done.1.rest_0_, ...), custom_call_target="tpu_custom_call" | custom-call | flops 65536 | bytes 1024 | tf_op jit(solution)/shard_map/attend/pallas_call | solution.py:235
  30.2 0.6 %collective-permute-start.2 = (bf16[2,32,768]{2,1,0:T(8,128)(2,1)S(1)}, bf16[2,32,768]{2,1,0:T(8,128)(2,1)S(1)}, u32[]{:S(2)}, u32[]{:S(2)}) collective-permute-start(bf16[2,32,768]{2,1,0:T(8,128)(2,1)S(1)} %get-tuple-element.50), channel_id=1, source_target_pairs={{0,28},{4,24},{8,20},{12,16},{16,12},{20,8},{24,4},{28,0},{1,29},{... | collective-permute-start | bytes 294920 | tf_op jit(solution)/shard_map/ppermute | solution.py:360
  30.8 1.5 %collective-permute-start.3 = (bf16[2,32,768]{2,1,0:T(8,128)(2,1)S(1)}, bf16[2,32,768]{2,1,0:T(8,128)(2,1)S(1)}, u32[]{:S(2)}, u32[]{:S(2)}) collective-permute-start(bf16[2,32,768]{2,1,0:T(8,128)(2,1)S(1)} %get-tuple-element.51), channel_id=1, source_target_pairs={{0,4},{4,0},{8,12},{12,8},{16,20},{20,16},{24,28},{28,24},{1,5},{5... | collective-permute-start | bytes 294920 | tf_op jit(solution)/shard_map/ppermute | solution.py:360
  32.3 1.3 %collective-permute-start.9 = (bf16[4,32,768]{2,1,0:T(8,128)(2,1)S(1)}, bf16[4,32,768]{2,1,0:T(8,128)(2,1)S(1)}, u32[]{:S(2)}, u32[]{:S(2)}) collective-permute-start(bf16[4,32,768]{2,1,0:T(8,128)(2,1)S(1)} %get-tuple-element.71), channel_id=1, source_target_pairs={{0,2},{1,3},{2,0},{3,1},{4,6},{5,7},{6,4},{7,5},{8,10},{9,11},{10,... | collective-permute-start | bytes 589832 | tf_op jit(solution)/shard_map/ppermute | solution.py:360
  33.6 0.0 collective-permute-done.4.rest_0_
  33.6 0.0 slice-start.2
  33.6 2.2 %attend.5 = (bf16[2,32,768]{2,1,0:T(8,128)(2,1)S(1)}, bf16[2,32,768]{2,1,0:T(8,128)(2,1)S(1)}) custom-call(s32[16]{0:T(128)S(1)} %get-tuple-element.70.slots, bf16[32,32,768]{2,1,0:T(8,128)(2,1)S(1)} %copy-done, bf16[32,32,768]{2,1,0:T(8,128)(2,1)S(1)} %collective-permute-done.sibling, bf16[4,32,768]{2,1,0:T(8,128)(2,1)S(1)} %collective-permute-done.4.rest_0_, ...), custom_call_target="tpu_custom_call" | custom-call | flops 65536 | bytes 1024 | tf_op jit(solution)/shard_map/attend/pallas_call | solution.py:235
  35.9 0.0 copy-start.9
  35.9 0.0 slice-start.3
  35.9 3.3 %collective-permute-start.5 = (bf16[2,32,768]{2,1,0:T(8,128)(2,1)S(1)}, bf16[2,32,768]{2,1,0:T(8,128)(2,1)S(1)}, u32[]{:S(2)}, u32[]{:S(2)}) collective-permute-start(bf16[2,32,768]{2,1,0:T(8,128)(2,1)S(1)} %get-tuple-element.56), channel_id=1, source_target_pairs={{0,24},{4,28},{8,16},{12,20},{16,8},{20,12},{24,0},{28,4},{1,25},{... | collective-permute-start | bytes 294920 | tf_op jit(solution)/shard_map/ppermute | solution.py:360
  39.2 0.0 collective-permute-done.2.rest_0_
  39.3 0.0 collective-permute-done.3.rest_1_
  39.3 0.0 collective-permute-done.6.rest_0_
  39.3 2.3 %attend.6 = (bf16[2,32,768]{2,1,0:T(8,128)(2,1)S(1)}, bf16[2,32,768]{2,1,0:T(8,128)(2,1)S(1)}) custom-call(s32[16]{0:T(128)S(1)} %get-tuple-element.70.slots, bf16[32,32,768]{2,1,0:T(8,128)(2,1)S(1)} %copy-done, bf16[32,32,768]{2,1,0:T(8,128)(2,1)S(1)} %collective-permute-done.sibling, bf16[4,32,768]{2,1,0:T(8,128)(2,1)S(1)} %collective-permute-done.6.rest_0_, ...), custom_call_target="tpu_custom_call" | custom-call | flops 65536 | bytes 1024 | tf_op jit(solution)/shard_map/attend/pallas_call | solution.py:235
  41.5 0.1 collective-permute-start.7
  41.6 2.0 %collective-permute-start.8 = (bf16[2,32,768]{2,1,0:T(8,128)(2,1)S(1)}, bf16[2,32,768]{2,1,0:T(8,128)(2,1)S(1)}, u32[]{:S(2)}, u32[]{:S(2)}) collective-permute-start(bf16[2,32,768]{2,1,0:T(8,128)(2,1)S(1)} %get-tuple-element.62), channel_id=1, source_target_pairs={{0,12},{4,8},{8,4},{12,0},{16,28},{20,24},{24,20},{28,16},{1,13},{... | collective-permute-start | bytes 294920 | tf_op jit(solution)/shard_map/ppermute | solution.py:360
  43.6 0.0 copy-done.9
  43.6 0.0 collective-permute-done.5.rest_2_
  43.6 0.0 slice-start
  43.6 0.0 slice-start.1
  43.7 0.0 collective-permute-done.9.rest_0_
  43.7 2.4 %attend.7 = (bf16[2,32,768]{2,1,0:T(8,128)(2,1)S(1)}, bf16[2,32,768]{2,1,0:T(8,128)(2,1)S(1)}) custom-call(s32[16]{0:T(128)S(1)} %get-tuple-element.70.slots, bf16[32,32,768]{2,1,0:T(8,128)(2,1)S(1)} %copy-done, bf16[32,32,768]{2,1,0:T(8,128)(2,1)S(1)} %collective-permute-done.sibling, bf16[4,32,768]{2,1,0:T(8,128)(2,1)S(1)} %collective-permute-done.9.rest_0_, ...), custom_call_target="tpu_custom_call" | custom-call | flops 65536 | bytes 1024 | tf_op jit(solution)/shard_map/attend/pallas_call | solution.py:235
  46.1 1.2 %collective-permute-start.10 = (bf16[2,32,768]{2,1,0:T(8,128)(2,1)S(1)}, bf16[2,32,768]{2,1,0:T(8,128)(2,1)S(1)}, u32[]{:S(2)}, u32[]{:S(2)}) collective-permute-start(bf16[2,32,768]{2,1,0:T(8,128)(2,1)S(1)} %get-tuple-element.72), channel_id=1, source_target_pairs={{0,16},{4,20},{8,24},{12,28},{16,0},{20,4},{24,8},{28,12},{1,17},{... | collective-permute-start | bytes 294920 | tf_op jit(solution)/shard_map/ppermute | solution.py:360
  47.4 0.0 copy-start.5
  47.4 0.0 copy-start.6
  47.4 2.6 %collective-permute-start.11 = (bf16[2,32,768]{2,1,0:T(8,128)(2,1)S(1)}, bf16[2,32,768]{2,1,0:T(8,128)(2,1)S(1)}, u32[]{:S(2)}, u32[]{:S(2)}) collective-permute-start(bf16[2,32,768]{2,1,0:T(8,128)(2,1)S(1)} %get-tuple-element.73), channel_id=1, source_target_pairs={{0,8},{4,12},{8,0},{12,4},{16,24},{20,28},{24,16},{28,20},{1,9},{5... | collective-permute-start | bytes 294920 | tf_op jit(solution)/shard_map/ppermute | solution.py:360
  50.0 0.0 collective-permute-done.7.rest_0_
  50.0 0.0 collective-permute-done.8.rest_1_
  50.0 0.0 slice-done.2
  50.0 0.0 slice-done.3
  50.0 0.0 slice-done
  50.0 0.0 slice-done.1
  50.0 3.0 %feed_first.1.earlier = bf16[8,32,768]{2,1,0:T(8,128)(2,1)S(1)} custom-call(f32[1,768]{1,0:T(1,128)S(1)} %reshape.12.gain, bf16[768,3072]{1,0:T(8,128)(2,1)S(1)} %bitcast.8, bf16[3072,768]{1,0:T(8,128)(2,1)S(1)} %bitcast.10, bf16[2,32,768]{2,1,0:T(8,128)(2,1)S(1)} %collective-permute-done.2.rest_0_, bf16[2,32,768]{2,1,0:T(8,128)(2,1)S(1)} %collective-permute-done.3.rest_1_, ...), custom_call_target="tpu_custom_call" | custom-call | flops 2415919104 | bytes 9437184 | tf_op jit(solution)/shard_map/feed_first/pallas_call | solution.py:303
  53.1 0.0 collective-permute-done.10.rest_2_
  53.1 0.1 collective-permute-done.11.rest_3_
  53.2 0.0 copy-done.5
  53.2 0.0 copy-done.6
  53.2 4.5 %feed_last.1 = (bf16[16,32,768]{2,1,0:T(8,128)(2,1)}, f32[2,16]{1,0:T(2,128)}) custom-call(s32[16]{0:T(128)S(1)} %copy-done.6, f32[1,768]{1,0:T(1,128)S(1)} %reshape.12.gain, bf16[2,768]{1,0:T(2,128)(2,1)S(1)} %bitcast.12, bf16[768,3072]{1,0:T(8,128)(2,1)S(1)} %bitcast.8, bf16[3072,768]{1,0:T(8,128)(2,1)S(1)} %bitcast.10, ...), custom_call_target="tpu_custom_call" | custom-call | flops 2415919104 | bytes 9437184 | tf_op jit(solution)/shard_map/feed_last/pallas_call | solution.py:318
  (4 shorter events, 0.0 us)
Async XLA Ops:
  0.6 16.4 %collective-permute-start = (bf16[32,32,768]{2,1,0:T(8,128)(2,1)}, bf16[32,32,768]{2,1,0:T(8,128)(2,1)S(1)}, u32[]{:S(2)}, u32[]{:S(2)}) collective-permute-start(bf16[32,32,768]{2,1,0:T(8,128)(2,1)} %own.7), channel_id=1, source_target_pairs={{0,1},{1,0},{2,3},{3,2},{4,5},{5,4},{6,7},{7,6},{8,9},{9,8},{10,11... | collective-permute-start | bytes 4718600 | tf_op jit(solution)/shard_map/ppermute | solution.py:360
  2.9 17.6 %copy-start.7 = (bf16[8,197,768]{2,0,1:T(8,128)(2,1)S(1)}, bf16[8,197,768]{2,0,1:T(8,128)(2,1)}, u32[]{:S(2)}) copy-start(bf16[8,197,768]{2,0,1:T(8,128)(2,1)} %param.19) | copy-start | bytes 7262212
  19.9 1.3 %copy-start.3 = (bf16[768,768]{1,0:T(8,128)(2,1)S(1)}, bf16[768,768]{1,0:T(8,128)(2,1)}, u32[]{:S(2)}) copy-start(bf16[768,768]{1,0:T(8,128)(2,1)} %weight.1) | copy-start | bytes 3538948
  19.9 8.0 %collective-permute-start.1 = (bf16[4,32,768]{2,1,0:T(8,128)(2,1)S(1)}, bf16[4,32,768]{2,1,0:T(8,128)(2,1)S(1)}, u32[]{:S(2)}, u32[]{:S(2)}) collective-permute-start(bf16[4,32,768]{2,1,0:T(8,128)(2,1)S(1)} %get-tuple-element.42), channel_id=1, source_target_pairs={{0,2},{1,3},{2,0},{3,1},{4,6},{5,7},{6,4},{7,5},{8,10},{9,11},{10,... | collective-permute-start | bytes 589832 | tf_op jit(solution)/shard_map/ppermute | solution.py:360
  21.2 3.8 %copy-start.4 = (bf16[768,768]{1,0:T(8,128)(2,1)S(1)}, bf16[768,768]{1,0:T(8,128)(2,1)}, u32[]{:S(2)}) copy-start(bf16[768,768]{1,0:T(8,128)(2,1)} %weight.2) | copy-start | bytes 3538948
  23.5 4.4 %copy-start.8 = (f32[768]{0:T(1024)S(1)}, f32[768]{0:T(1024)}, u32[]{:S(2)}) copy-start(f32[768]{0:T(1024)} %param.25) | copy-start | bytes 9220
  23.5 4.4 %copy-start = (bf16[32,32,768]{2,1,0:T(8,128)(2,1)S(1)}, bf16[32,32,768]{2,1,0:T(8,128)(2,1)}, u32[]{:S(2)}) copy-start(bf16[32,32,768]{2,1,0:T(8,128)(2,1)} %own.7) | copy-start | bytes 4718596
  23.5 4.4 %copy-start.1 = (bf16[768,768]{1,0:T(8,128)(2,1)S(1)}, bf16[768,768]{1,0:T(8,128)(2,1)}, u32[]{:S(2)}) copy-start(bf16[768,768]{1,0:T(8,128)(2,1)} %rest_3_.7) | copy-start | bytes 3538948
  23.5 4.4 %copy-start.2 = (bf16[768,768]{1,0:T(8,128)(2,1)S(1)}, bf16[768,768]{1,0:T(8,128)(2,1)}, u32[]{:S(2)}) copy-start(bf16[768,768]{1,0:T(8,128)(2,1)} %rest_4_.7) | copy-start | bytes 3538948
  23.6 10.1 %collective-permute-start.4 = (bf16[4,32,768]{2,1,0:T(8,128)(2,1)S(1)}, bf16[4,32,768]{2,1,0:T(8,128)(2,1)S(1)}, u32[]{:S(2)}, u32[]{:S(2)}) collective-permute-start(bf16[4,32,768]{2,1,0:T(8,128)(2,1)S(1)} %get-tuple-element.55), channel_id=1, source_target_pairs={{0,2},{1,3},{2,0},{3,1},{4,6},{5,7},{6,4},{7,5},{8,10},{9,11},{10,... | collective-permute-start | bytes 589832 | tf_op jit(solution)/shard_map/ppermute | solution.py:360
  27.1 12.1 %collective-permute-start.6 = (bf16[4,32,768]{2,1,0:T(8,128)(2,1)S(1)}, bf16[4,32,768]{2,1,0:T(8,128)(2,1)S(1)}, u32[]{:S(2)}, u32[]{:S(2)}) collective-permute-start(bf16[4,32,768]{2,1,0:T(8,128)(2,1)S(1)} %get-tuple-element.60), channel_id=1, source_target_pairs={{0,2},{1,3},{2,0},{3,1},{4,6},{5,7},{6,4},{7,5},{8,10},{9,11},{10,... | collective-permute-start | bytes 589832 | tf_op jit(solution)/shard_map/ppermute | solution.py:360
  30.2 9.0 %collective-permute-start.2 = (bf16[2,32,768]{2,1,0:T(8,128)(2,1)S(1)}, bf16[2,32,768]{2,1,0:T(8,128)(2,1)S(1)}, u32[]{:S(2)}, u32[]{:S(2)}) collective-permute-start(bf16[2,32,768]{2,1,0:T(8,128)(2,1)S(1)} %get-tuple-element.50), channel_id=1, source_target_pairs={{0,28},{4,24},{8,20},{12,16},{16,12},{20,8},{24,4},{28,0},{1,29},{... | collective-permute-start | bytes 294920 | tf_op jit(solution)/shard_map/ppermute | solution.py:360
  30.8 8.4 %collective-permute-start.3 = (bf16[2,32,768]{2,1,0:T(8,128)(2,1)S(1)}, bf16[2,32,768]{2,1,0:T(8,128)(2,1)S(1)}, u32[]{:S(2)}, u32[]{:S(2)}) collective-permute-start(bf16[2,32,768]{2,1,0:T(8,128)(2,1)S(1)} %get-tuple-element.51), channel_id=1, source_target_pairs={{0,4},{4,0},{8,12},{12,8},{16,20},{20,16},{24,28},{28,24},{1,5},{5... | collective-permute-start | bytes 294920 | tf_op jit(solution)/shard_map/ppermute | solution.py:360
  32.3 11.3 %collective-permute-start.9 = (bf16[4,32,768]{2,1,0:T(8,128)(2,1)S(1)}, bf16[4,32,768]{2,1,0:T(8,128)(2,1)S(1)}, u32[]{:S(2)}, u32[]{:S(2)}) collective-permute-start(bf16[4,32,768]{2,1,0:T(8,128)(2,1)S(1)} %get-tuple-element.71), channel_id=1, source_target_pairs={{0,2},{1,3},{2,0},{3,1},{4,6},{5,7},{6,4},{7,5},{8,10},{9,11},{10,... | collective-permute-start | bytes 589832 | tf_op jit(solution)/shard_map/ppermute | solution.py:360
  33.6 16.4 %slice-start.2 = ((s8[4718592]{0:T(1024)(128)(4,1)}), s8[4194304]{0:T(1024)(128)(4,1)S(1)}, s32[]{:S(2)}) async-start(s8[4718592]{0:T(1024)(128)(4,1)} %bitcast.9), calls=%async_computation.3 | async-start | bytes 8388608
  35.9 7.7 %copy-start.9 = (f32[768]{0:T(1024)S(1)}, f32[768]{0:T(1024)}, u32[]{:S(2)}) copy-start(f32[768]{0:T(1024)} %param.28) | copy-start | bytes 9220
  35.9 14.1 %slice-start.3 = ((s8[4718592]{0:T(1024)(128)(4,1)}), s8[524288]{0:T(1024)(128)(4,1)S(1)}, s32[]{:S(2)}) async-start(s8[4718592]{0:T(1024)(128)(4,1)} %bitcast.9), calls=%async_computation.4 | async-start | bytes 1048576
  35.9 7.7 %collective-permute-start.5 = (bf16[2,32,768]{2,1,0:T(8,128)(2,1)S(1)}, bf16[2,32,768]{2,1,0:T(8,128)(2,1)S(1)}, u32[]{:S(2)}, u32[]{:S(2)}) collective-permute-start(bf16[2,32,768]{2,1,0:T(8,128)(2,1)S(1)} %get-tuple-element.56), channel_id=1, source_target_pairs={{0,24},{4,28},{8,16},{12,20},{16,8},{20,12},{24,0},{28,4},{1,25},{... | collective-permute-start | bytes 294920 | tf_op jit(solution)/shard_map/ppermute | solution.py:360
  41.5 8.5 %collective-permute-start.7 = (bf16[2,32,768]{2,1,0:T(8,128)(2,1)S(1)}, bf16[2,32,768]{2,1,0:T(8,128)(2,1)S(1)}, u32[]{:S(2)}, u32[]{:S(2)}) collective-permute-start(bf16[2,32,768]{2,1,0:T(8,128)(2,1)S(1)} %get-tuple-element.61), channel_id=1, source_target_pairs={{0,20},{4,16},{8,28},{12,24},{16,4},{20,0},{24,12},{28,8},{1,21},{... | collective-permute-start | bytes 294920 | tf_op jit(solution)/shard_map/ppermute | solution.py:360
  41.6 8.4 %collective-permute-start.8 = (bf16[2,32,768]{2,1,0:T(8,128)(2,1)S(1)}, bf16[2,32,768]{2,1,0:T(8,128)(2,1)S(1)}, u32[]{:S(2)}, u32[]{:S(2)}) collective-permute-start(bf16[2,32,768]{2,1,0:T(8,128)(2,1)S(1)} %get-tuple-element.62), channel_id=1, source_target_pairs={{0,12},{4,8},{8,4},{12,0},{16,28},{20,24},{24,20},{28,16},{1,13},{... | collective-permute-start | bytes 294920 | tf_op jit(solution)/shard_map/ppermute | solution.py:360
  43.6 6.4 %slice-start = ((s8[4718592]{0:T(1024)(128)(4,1)}), s8[4194304]{0:T(1024)(128)(4,1)S(1)}, s32[]{:S(2)}) async-start(s8[4718592]{0:T(1024)(128)(4,1)} %bitcast.7), calls=%async_computation.1 | async-start | bytes 8388608
  43.6 6.4 %slice-start.1 = ((s8[4718592]{0:T(1024)(128)(4,1)}), s8[524288]{0:T(1024)(128)(4,1)S(1)}, s32[]{:S(2)}) async-start(s8[4718592]{0:T(1024)(128)(4,1)} %bitcast.7), calls=%async_computation.2 | async-start | bytes 1048576
  46.1 7.0 %collective-permute-start.10 = (bf16[2,32,768]{2,1,0:T(8,128)(2,1)S(1)}, bf16[2,32,768]{2,1,0:T(8,128)(2,1)S(1)}, u32[]{:S(2)}, u32[]{:S(2)}) collective-permute-start(bf16[2,32,768]{2,1,0:T(8,128)(2,1)S(1)} %get-tuple-element.72), channel_id=1, source_target_pairs={{0,16},{4,20},{8,24},{12,28},{16,0},{20,4},{24,8},{28,12},{1,17},{... | collective-permute-start | bytes 294920 | tf_op jit(solution)/shard_map/ppermute | solution.py:360
  47.4 5.9 %copy-start.5 = (bf16[768,2]{0,1:T(2,128)(2,1)S(1)}, bf16[768,2]{0,1:T(2,128)(2,1)}, u32[]{:S(2)}) copy-start(bf16[768,2]{0,1:T(2,128)(2,1)} %param.29) | copy-start | bytes 9220
  47.4 5.9 %copy-start.6 = (s32[16]{0:T(128)S(1)}, s32[16]{0:T(128)}, u32[]{:S(2)}) copy-start(s32[16]{0:T(128)} %get-tuple-element.39.place) | copy-start | bytes 196
  47.4 5.8 %collective-permute-start.11 = (bf16[2,32,768]{2,1,0:T(8,128)(2,1)S(1)}, bf16[2,32,768]{2,1,0:T(8,128)(2,1)S(1)}, u32[]{:S(2)}, u32[]{:S(2)}) collective-permute-start(bf16[2,32,768]{2,1,0:T(8,128)(2,1)S(1)} %get-tuple-element.73), channel_id=1, source_target_pairs={{0,8},{4,12},{8,0},{12,4},{16,24},{20,28},{24,16},{28,20},{1,9},{5... | collective-permute-start | bytes 294920 | tf_op jit(solution)/shard_map/ppermute | solution.py:360

commit v7 on v6

--- a/solution.py
+++ b/solution.py
@@ -351,7 +351,7 @@
     cap_count = lax.axis_size("cap")
     far_steps = range(1, cap_count // CORES)
     half = img_count // 2
-    chunks = tuple((img_count - 1 - index, index ^ 1) for index in range(half))
+    chunks = tuple((img_count - 1 - (index ^ 1), index ^ 1) for index in range(half))
     first_parts = sum(chunks[: half // 2], ())
     last_parts = sum(chunks[half // 2 :], ())
 

time: 57.9 us -> 58.9 us (1.017)
  waiting for transfers between devices: 0.12 us -> 1.17 us
    ppermute x12, waiting for transfers between devices: 0.12 us -> 1.17 us  [swap(): lax.ppermute(array, axis, [(peer, peer ^ distance) for peer in range(size)])]
  transfers between devices with their start and end apart: 12 -> 12, of which waited for: 1 -> 2; matrix products, arithmetic and copies ran while one was open for 1% -> 1% of each run, Pallas kernels for 32% -> 32%
where the time goes in v7:
time: 58.9 us; the launch traced here: 58.6 us
  Pallas kernels  25.8 us (44%)
  starting transfers between devices  16 us (27%)
  blocking collectives  14.1 us (24%)
  waiting for transfers between devices  1.17 us (2%)
  between operations  0.88 us (1%)
  local copies, waits for them, and re-layouts  0.7 us (1%)
    ppermute x12, starting transfers between devices, swap(): lax.ppermute(array, axis, [(peer, peer ^ distance) for peer in range(size)])  16 us
    all_to_all x1, blocking collectives, body(): lax.all_to_all(table, ('img', 'cap'), split_axis=0, concat_axis=0, tiled=...  14.1 us
    pallas_call x4, Pallas kernels, attend(): pl.pallas_call(functools.partial(attend_kernel, key_rows, len(far), chunk...  9.18 us
    pallas_call x2, Pallas kernels, project_images(): pl.pallas_call(functools.partial(project_kernel, turned), out_shape=jax.S...  4.5 us
    pallas_call x1, Pallas kernels, feed_last(): pl.pallas_call(functools.partial(feed_last_kernel, first_parts, last_part...  4.46 us
    pallas_call x1, Pallas kernels, feed_first(): pl.pallas_call(feed_first_kernel, out_shape=jax.ShapeDtypeStruct((slots,...  3.04 us
    pallas_call x1, Pallas kernels, pick_blocks(): pl.pallas_call(functools.partial(pick_kernel, step, cap_count, chunks), o...  2.89 us
    pallas_call x1, Pallas kernels, make_table(): pl.pallas_call(functools.partial(table_kernel, image_local, caption_count...  1.76 us
  transfers between devices with their start and end apart: 12, of which 2 were waited for; matrix products, arithmetic and copies ran while one was open for 1% of the time, Pallas kernels for 32%

profile of v7, /device:TPU:0, one launch (start us, length us, event | category | flops | bytes accessed | tf_op | source)
XLA Modules:
  0.0 58.6 jit_solution(17054800691464465584)
XLA Ops:
  0.6 0.5 collective-permute-start
  1.1 1.8 %slot_table.1 = (s32[32,128]{1,0:T(8,128)}, s32[16]{0:T(128)}) custom-call(s32[2,512]{1,0:T(2,128)} %bitcast.14, s32[16]{0:T(128)} %order.1, s32[64]{0:T(128)} %image_slot.1, s32[128]{0:T(128)} %caption_slot.1), custom_call_target="tpu_custom_call" | custom-call | tf_op jit(solution)/shard_map/slot_table/pallas_call | solution.py:60
  2.9 0.0 copy-start.7
  2.9 14.1 %all_to_all.11 = s32[32,1,128]{2,1,0:T(1,128)S(1)} all-to-all(s32[32,1,128]{2,1,0:T(1,128)} %bitcast.13), channel_id=1, replica_groups=mesh['img'=8,'cap'=4] {'img','cap'}, dimensions={0} | all-to-all | bytes 32768 | tf_op jit(solution)/shard_map/all_to_all | solution.py:366
  17.0 0.0 collective-permute-done.sibling
  17.0 2.9 %pick_captions.1 = (s32[16]{0:T(128)S(1)}, bf16[4,32,768]{2,1,0:T(8,128)(2,1)S(1)}, bf16[4,32,768]{2,1,0:T(8,128)(2,1)S(1)}, bf16[4,32,768]{2,1,0:T(8,128)(2,1)S(1)}, bf16[4,32,768]{2,1,0:T(8,128)(2,1)S(1)}) custom-call(s32[32,128]{1,0:T(8,128)S(1)} %bitcast.11, bf16[32,32,768]{2,1,0:T(8,128)(2,1)} %own.7, bf16[32,32,768]{2,1,0:T(8,128)(2,1)S(1)} %collective-permute-done.sibling), custom_call_target="tpu_custom_call" | custom-call | flops 65536 | bytes 1024 | tf_op jit(solution)/shard_map/pick_captions/pallas_call | solution.py:118
  19.9 0.0 copy-start.3
  19.9 0.6 %collective-permute-start.1 = (bf16[4,32,768]{2,1,0:T(8,128)(2,1)S(1)}, bf16[4,32,768]{2,1,0:T(8,128)(2,1)S(1)}, u32[]{:S(2)}, u32[]{:S(2)}) collective-permute-start(bf16[4,32,768]{2,1,0:T(8,128)(2,1)S(1)} %get-tuple-element.42), channel_id=1, source_target_pairs={{0,2},{1,3},{2,0},{3,1},{4,6},{5,7},{6,4},{7,5},{8,10},{9,11},{10,... | collective-permute-start | bytes 589832 | tf_op jit(solution)/shard_map/ppermute | solution.py:360
  20.5 0.0 copy-done.7
  20.5 0.5 copy.20.images
  21.0 0.2 copy-done.3
  21.2 0.0 copy-start.4
  21.2 2.3 %project_images.2.rest_1_ = bf16[8,768,256]{2,1,0:T(8,128)(2,1)S(1)} custom-call(bf16[8,197,768]{2,1,0:T(8,128)(2,1)S(1)} %copy.20.images, bf16[768,768]{1,0:T(8,128)(2,1)S(1)} %copy-done.3), custom_call_target="tpu_custom_call" | custom-call | flops 65536 | bytes 1024 | tf_op jit(solution)/shard_map/project_images/pallas_call | solution.py:145
  23.5 0.0 copy-start.8
  23.5 0.0 copy-start
  23.5 0.0 copy-start.1
  23.5 0.0 copy-start.2
  23.5 1.4 %collective-permute-start.4 = (bf16[4,32,768]{2,1,0:T(8,128)(2,1)S(1)}, bf16[4,32,768]{2,1,0:T(8,128)(2,1)S(1)}, u32[]{:S(2)}, u32[]{:S(2)}) collective-permute-start(bf16[4,32,768]{2,1,0:T(8,128)(2,1)S(1)} %get-tuple-element.55), channel_id=1, source_target_pairs={{0,2},{1,3},{2,0},{3,1},{4,6},{5,7},{6,4},{7,5},{8,10},{9,11},{10,... | collective-permute-start | bytes 589832 | tf_op jit(solution)/shard_map/ppermute | solution.py:360
  24.9 0.0 copy-done.4
  24.9 2.2 %project_images.3.rest_2_ = bf16[8,256,768]{2,1,0:T(8,128)(2,1)S(1)} custom-call(bf16[8,197,768]{2,1,0:T(8,128)(2,1)S(1)} %copy.20.images, bf16[768,768]{1,0:T(8,128)(2,1)S(1)} %copy-done.4), custom_call_target="tpu_custom_call" | custom-call | flops 65536 | bytes 1024 | tf_op jit(solution)/shard_map/project_images/pallas_call | solution.py:145
  27.1 0.8 %collective-permute-start.6 = (bf16[4,32,768]{2,1,0:T(8,128)(2,1)S(1)}, bf16[4,32,768]{2,1,0:T(8,128)(2,1)S(1)}, u32[]{:S(2)}, u32[]{:S(2)}) collective-permute-start(bf16[4,32,768]{2,1,0:T(8,128)(2,1)S(1)} %get-tuple-element.60), channel_id=1, source_target_pairs={{0,2},{1,3},{2,0},{3,1},{4,6},{5,7},{6,4},{7,5},{8,10},{9,11},{10,... | collective-permute-start | bytes 589832 | tf_op jit(solution)/shard_map/ppermute | solution.py:360
  27.9 0.0 copy-done.8
  27.9 0.0 collective-permute-done.1.rest_0_
  27.9 0.0 copy-done
  27.9 0.0 copy-done.1
  27.9 0.0 copy-done.2
  27.9 2.3 %attend.4 = (bf16[2,32,768]{2,1,0:T(8,128)(2,1)S(1)}, bf16[2,32,768]{2,1,0:T(8,128)(2,1)S(1)}) custom-call(s32[16]{0:T(128)S(1)} %get-tuple-element.70.slots, bf16[32,32,768]{2,1,0:T(8,128)(2,1)S(1)} %copy-done, bf16[32,32,768]{2,1,0:T(8,128)(2,1)S(1)} %collective-permute-done.sibling, bf16[4,32,768]{2,1,0:T(8,128)(2,1)S(1)} %collective-permute-done.1.rest_0_, ...), custom_call_target="tpu_custom_call" | custom-call | flops 65536 | bytes 1024 | tf_op jit(solution)/shard_map/attend/pallas_call | solution.py:235
  30.2 0.6 %collective-permute-start.2 = (bf16[2,32,768]{2,1,0:T(8,128)(2,1)S(1)}, bf16[2,32,768]{2,1,0:T(8,128)(2,1)S(1)}, u32[]{:S(2)}, u32[]{:S(2)}) collective-permute-start(bf16[2,32,768]{2,1,0:T(8,128)(2,1)S(1)} %get-tuple-element.50), channel_id=1, source_target_pairs={{0,24},{4,28},{8,16},{12,20},{16,8},{20,12},{24,0},{28,4},{1,25},{... | collective-permute-start | bytes 294920 | tf_op jit(solution)/shard_map/ppermute | solution.py:360
  30.8 0.5 collective-permute-start.3
  31.3 1.3 %collective-permute-start.9 = (bf16[4,32,768]{2,1,0:T(8,128)(2,1)S(1)}, bf16[4,32,768]{2,1,0:T(8,128)(2,1)S(1)}, u32[]{:S(2)}, u32[]{:S(2)}) collective-permute-start(bf16[4,32,768]{2,1,0:T(8,128)(2,1)S(1)} %get-tuple-element.71), channel_id=1, source_target_pairs={{0,2},{1,3},{2,0},{3,1},{4,6},{5,7},{6,4},{7,5},{8,10},{9,11},{10,... | collective-permute-start | bytes 589832 | tf_op jit(solution)/shard_map/ppermute | solution.py:360
  32.7 0.0 collective-permute-done.4.rest_0_
  32.7 0.0 slice-start.2
  32.7 2.2 %attend.5 = (bf16[2,32,768]{2,1,0:T(8,128)(2,1)S(1)}, bf16[2,32,768]{2,1,0:T(8,128)(2,1)S(1)}) custom-call(s32[16]{0:T(128)S(1)} %get-tuple-element.70.slots, bf16[32,32,768]{2,1,0:T(8,128)(2,1)S(1)} %copy-done, bf16[32,32,768]{2,1,0:T(8,128)(2,1)S(1)} %collective-permute-done.sibling, bf16[4,32,768]{2,1,0:T(8,128)(2,1)S(1)} %collective-permute-done.4.rest_0_, ...), custom_call_target="tpu_custom_call" | custom-call | flops 65536 | bytes 1024 | tf_op jit(solution)/shard_map/attend/pallas_call | solution.py:235
  34.9 0.0 copy-start.9
  34.9 0.0 slice-start.3
  35.0 4.3 %collective-permute-start.5 = (bf16[2,32,768]{2,1,0:T(8,128)(2,1)S(1)}, bf16[2,32,768]{2,1,0:T(8,128)(2,1)S(1)}, u32[]{:S(2)}, u32[]{:S(2)}) collective-permute-start(bf16[2,32,768]{2,1,0:T(8,128)(2,1)S(1)} %get-tuple-element.56), channel_id=1, source_target_pairs={{0,28},{4,24},{8,20},{12,16},{16,12},{20,8},{24,4},{28,0},{1,29},{... | collective-permute-start | bytes 294920 | tf_op jit(solution)/shard_map/ppermute | solution.py:360
  39.2 0.0 collective-permute-done.2.rest_0_
  39.2 0.0 collective-permute-done.3.rest_1_
  39.2 0.0 collective-permute-done.6.rest_0_
  39.2 2.2 %attend.6 = (bf16[2,32,768]{2,1,0:T(8,128)(2,1)S(1)}, bf16[2,32,768]{2,1,0:T(8,128)(2,1)S(1)}) custom-call(s32[16]{0:T(128)S(1)} %get-tuple-element.70.slots, bf16[32,32,768]{2,1,0:T(8,128)(2,1)S(1)} %copy-done, bf16[32,32,768]{2,1,0:T(8,128)(2,1)S(1)} %collective-permute-done.sibling, bf16[4,32,768]{2,1,0:T(8,128)(2,1)S(1)} %collective-permute-done.6.rest_0_, ...), custom_call_target="tpu_custom_call" | custom-call | flops 65536 | bytes 1024 | tf_op jit(solution)/shard_map/attend/pallas_call | solution.py:235
  41.5 0.1 collective-permute-start.7
  41.6 1.1 %collective-permute-start.8 = (bf16[2,32,768]{2,1,0:T(8,128)(2,1)S(1)}, bf16[2,32,768]{2,1,0:T(8,128)(2,1)S(1)}, u32[]{:S(2)}, u32[]{:S(2)}) collective-permute-start(bf16[2,32,768]{2,1,0:T(8,128)(2,1)S(1)} %get-tuple-element.62), channel_id=1, source_target_pairs={{0,12},{4,8},{8,4},{12,0},{16,28},{20,24},{24,20},{28,16},{1,13},{... | collective-permute-start | bytes 294920 | tf_op jit(solution)/shard_map/ppermute | solution.py:360
  42.6 0.0 copy-done.9
  42.6 0.7 %collective-permute-done.5.rest_2_ = bf16[2,32,768]{2,1,0:T(8,128)(2,1)S(1)} collective-permute-done((bf16[2,32,768]{2,1,0:T(8,128)(2,1)S(1)}, bf16[2,32,768]{2,1,0:T(8,128)(2,1)S(1)}, u32[]{:S(2)}, u32[]{:S(2)}) %collective-permute-start.5) | collective-permute-done | bytes 98336 | tf_op jit(solution)/shard_map/ppermute | solution.py:360
  43.4 0.0 slice-start
  43.4 0.0 slice-start.1
  43.4 0.0 collective-permute-done.9.rest_0_
  43.4 2.4 %attend.7 = (bf16[2,32,768]{2,1,0:T(8,128)(2,1)S(1)}, bf16[2,32,768]{2,1,0:T(8,128)(2,1)S(1)}) custom-call(s32[16]{0:T(128)S(1)} %get-tuple-element.70.slots, bf16[32,32,768]{2,1,0:T(8,128)(2,1)S(1)} %copy-done, bf16[32,32,768]{2,1,0:T(8,128)(2,1)S(1)} %collective-permute-done.sibling, bf16[4,32,768]{2,1,0:T(8,128)(2,1)S(1)} %collective-permute-done.9.rest_0_, ...), custom_call_target="tpu_custom_call" | custom-call | flops 65536 | bytes 1024 | tf_op jit(solution)/shard_map/attend/pallas_call | solution.py:235
  45.8 2.8 %collective-permute-start.10 = (bf16[2,32,768]{2,1,0:T(8,128)(2,1)S(1)}, bf16[2,32,768]{2,1,0:T(8,128)(2,1)S(1)}, u32[]{:S(2)}, u32[]{:S(2)}) collective-permute-start(bf16[2,32,768]{2,1,0:T(8,128)(2,1)S(1)} %get-tuple-element.72), channel_id=1, source_target_pairs={{0,20},{4,16},{8,28},{12,24},{16,4},{20,0},{24,12},{28,8},{1,21},{... | collective-permute-start | bytes 294920 | tf_op jit(solution)/shard_map/ppermute | solution.py:360
  48.6 0.0 copy-start.5
  48.7 0.0 copy-start.6
  48.7 2.0 %collective-permute-start.11 = (bf16[2,32,768]{2,1,0:T(8,128)(2,1)S(1)}, bf16[2,32,768]{2,1,0:T(8,128)(2,1)S(1)}, u32[]{:S(2)}, u32[]{:S(2)}) collective-permute-start(bf16[2,32,768]{2,1,0:T(8,128)(2,1)S(1)} %get-tuple-element.73), channel_id=1, source_target_pairs={{0,8},{4,12},{8,0},{12,4},{16,24},{20,28},{24,16},{28,20},{1,9},{5... | collective-permute-start | bytes 294920 | tf_op jit(solution)/shard_map/ppermute | solution.py:360
  50.6 0.0 collective-permute-done.7.rest_0_
  50.6 0.0 collective-permute-done.8.rest_1_
  50.6 0.0 slice-done.2
  50.6 0.0 slice-done.3
  50.6 0.0 slice-done
  50.6 0.0 slice-done.1
  50.7 3.0 %feed_first.1.earlier = bf16[8,32,768]{2,1,0:T(8,128)(2,1)S(1)} custom-call(f32[1,768]{1,0:T(1,128)S(1)} %reshape.12.gain, bf16[768,3072]{1,0:T(8,128)(2,1)S(1)} %bitcast.8, bf16[3072,768]{1,0:T(8,128)(2,1)S(1)} %bitcast.10, bf16[2,32,768]{2,1,0:T(8,128)(2,1)S(1)} %collective-permute-done.2.rest_0_, bf16[2,32,768]{2,1,0:T(8,128)(2,1)S(1)} %collective-permute-done.3.rest_1_, ...), custom_call_target="tpu_custom_call" | custom-call | flops 2415919104 | bytes 9437184 | tf_op jit(solution)/shard_map/feed_first/pallas_call | solution.py:303
  53.7 0.0 collective-permute-done.10.rest_2_
  53.7 0.4 collective-permute-done.11.rest_3_
  54.2 0.0 copy-done.5
  54.2 0.0 copy-done.6
  54.2 4.5 %feed_last.1 = (bf16[16,32,768]{2,1,0:T(8,128)(2,1)}, f32[2,16]{1,0:T(2,128)}) custom-call(s32[16]{0:T(128)S(1)} %copy-done.6, f32[1,768]{1,0:T(1,128)S(1)} %reshape.12.gain, bf16[2,768]{1,0:T(2,128)(2,1)S(1)} %bitcast.12, bf16[768,3072]{1,0:T(8,128)(2,1)S(1)} %bitcast.8, bf16[3072,768]{1,0:T(8,128)(2,1)S(1)} %bitcast.10, ...), custom_call_target="tpu_custom_call" | custom-call | flops 2415919104 | bytes 9437184 | tf_op jit(solution)/shard_map/feed_last/pallas_call | solution.py:318
  (4 shorter events, 0.0 us)
Async XLA Ops:
  0.6 16.4 %collective-permute-start = (bf16[32,32,768]{2,1,0:T(8,128)(2,1)}, bf16[32,32,768]{2,1,0:T(8,128)(2,1)S(1)}, u32[]{:S(2)}, u32[]{:S(2)}) collective-permute-start(bf16[32,32,768]{2,1,0:T(8,128)(2,1)} %own.7), channel_id=1, source_target_pairs={{0,1},{1,0},{2,3},{3,2},{4,5},{5,4},{6,7},{7,6},{8,9},{9,8},{10,11... | collective-permute-start | bytes 4718600 | tf_op jit(solution)/shard_map/ppermute | solution.py:360
  2.9 17.6 %copy-start.7 = (bf16[8,197,768]{2,0,1:T(8,128)(2,1)S(1)}, bf16[8,197,768]{2,0,1:T(8,128)(2,1)}, u32[]{:S(2)}) copy-start(bf16[8,197,768]{2,0,1:T(8,128)(2,1)} %param.19) | copy-start | bytes 7262212
  19.9 1.3 %copy-start.3 = (bf16[768,768]{1,0:T(8,128)(2,1)S(1)}, bf16[768,768]{1,0:T(8,128)(2,1)}, u32[]{:S(2)}) copy-start(bf16[768,768]{1,0:T(8,128)(2,1)} %weight.1) | copy-start | bytes 3538948
  19.9 8.0 %collective-permute-start.1 = (bf16[4,32,768]{2,1,0:T(8,128)(2,1)S(1)}, bf16[4,32,768]{2,1,0:T(8,128)(2,1)S(1)}, u32[]{:S(2)}, u32[]{:S(2)}) collective-permute-start(bf16[4,32,768]{2,1,0:T(8,128)(2,1)S(1)} %get-tuple-element.42), channel_id=1, source_target_pairs={{0,2},{1,3},{2,0},{3,1},{4,6},{5,7},{6,4},{7,5},{8,10},{9,11},{10,... | collective-permute-start | bytes 589832 | tf_op jit(solution)/shard_map/ppermute | solution.py:360
  21.2 3.8 %copy-start.4 = (bf16[768,768]{1,0:T(8,128)(2,1)S(1)}, bf16[768,768]{1,0:T(8,128)(2,1)}, u32[]{:S(2)}) copy-start(bf16[768,768]{1,0:T(8,128)(2,1)} %weight.2) | copy-start | bytes 3538948
  23.5 4.4 %copy-start.8 = (f32[768]{0:T(1024)S(1)}, f32[768]{0:T(1024)}, u32[]{:S(2)}) copy-start(f32[768]{0:T(1024)} %param.25) | copy-start | bytes 9220
  23.5 4.4 %copy-start = (bf16[32,32,768]{2,1,0:T(8,128)(2,1)S(1)}, bf16[32,32,768]{2,1,0:T(8,128)(2,1)}, u32[]{:S(2)}) copy-start(bf16[32,32,768]{2,1,0:T(8,128)(2,1)} %own.7) | copy-start | bytes 4718596
  23.5 4.4 %copy-start.1 = (bf16[768,768]{1,0:T(8,128)(2,1)S(1)}, bf16[768,768]{1,0:T(8,128)(2,1)}, u32[]{:S(2)}) copy-start(bf16[768,768]{1,0:T(8,128)(2,1)} %rest_3_.7) | copy-start | bytes 3538948
  23.5 4.4 %copy-start.2 = (bf16[768,768]{1,0:T(8,128)(2,1)S(1)}, bf16[768,768]{1,0:T(8,128)(2,1)}, u32[]{:S(2)}) copy-start(bf16[768,768]{1,0:T(8,128)(2,1)} %rest_4_.7) | copy-start | bytes 3538948
  23.5 9.1 %collective-permute-start.4 = (bf16[4,32,768]{2,1,0:T(8,128)(2,1)S(1)}, bf16[4,32,768]{2,1,0:T(8,128)(2,1)S(1)}, u32[]{:S(2)}, u32[]{:S(2)}) collective-permute-start(bf16[4,32,768]{2,1,0:T(8,128)(2,1)S(1)} %get-tuple-element.55), channel_id=1, source_target_pairs={{0,2},{1,3},{2,0},{3,1},{4,6},{5,7},{6,4},{7,5},{8,10},{9,11},{10,... | collective-permute-start | bytes 589832 | tf_op jit(solution)/shard_map/ppermute | solution.py:360
  27.1 12.1 %collective-permute-start.6 = (bf16[4,32,768]{2,1,0:T(8,128)(2,1)S(1)}, bf16[4,32,768]{2,1,0:T(8,128)(2,1)S(1)}, u32[]{:S(2)}, u32[]{:S(2)}) collective-permute-start(bf16[4,32,768]{2,1,0:T(8,128)(2,1)S(1)} %get-tuple-element.60), channel_id=1, source_target_pairs={{0,2},{1,3},{2,0},{3,1},{4,6},{5,7},{6,4},{7,5},{8,10},{9,11},{10,... | collective-permute-start | bytes 589832 | tf_op jit(solution)/shard_map/ppermute | solution.py:360
  30.2 9.0 %collective-permute-start.2 = (bf16[2,32,768]{2,1,0:T(8,128)(2,1)S(1)}, bf16[2,32,768]{2,1,0:T(8,128)(2,1)S(1)}, u32[]{:S(2)}, u32[]{:S(2)}) collective-permute-start(bf16[2,32,768]{2,1,0:T(8,128)(2,1)S(1)} %get-tuple-element.50), channel_id=1, source_target_pairs={{0,24},{4,28},{8,16},{12,20},{16,8},{20,12},{24,0},{28,4},{1,25},{... | collective-permute-start | bytes 294920 | tf_op jit(solution)/shard_map/ppermute | solution.py:360
  30.8 8.4 %collective-permute-start.3 = (bf16[2,32,768]{2,1,0:T(8,128)(2,1)S(1)}, bf16[2,32,768]{2,1,0:T(8,128)(2,1)S(1)}, u32[]{:S(2)}, u32[]{:S(2)}) collective-permute-start(bf16[2,32,768]{2,1,0:T(8,128)(2,1)S(1)} %get-tuple-element.51), channel_id=1, source_target_pairs={{0,4},{4,0},{8,12},{12,8},{16,20},{20,16},{24,28},{28,24},{1,5},{5... | collective-permute-start | bytes 294920 | tf_op jit(solution)/shard_map/ppermute | solution.py:360
  31.3 12.0 %collective-permute-start.9 = (bf16[4,32,768]{2,1,0:T(8,128)(2,1)S(1)}, bf16[4,32,768]{2,1,0:T(8,128)(2,1)S(1)}, u32[]{:S(2)}, u32[]{:S(2)}) collective-permute-start(bf16[4,32,768]{2,1,0:T(8,128)(2,1)S(1)} %get-tuple-element.71), channel_id=1, source_target_pairs={{0,2},{1,3},{2,0},{3,1},{4,6},{5,7},{6,4},{7,5},{8,10},{9,11},{10,... | collective-permute-start | bytes 589832 | tf_op jit(solution)/shard_map/ppermute | solution.py:360
  32.7 18.0 %slice-start.2 = ((s8[4718592]{0:T(1024)(128)(4,1)}), s8[4194304]{0:T(1024)(128)(4,1)S(1)}, s32[]{:S(2)}) async-start(s8[4718592]{0:T(1024)(128)(4,1)} %bitcast.9), calls=%async_computation.3 | async-start | bytes 8388608
  34.9 7.7 %copy-start.9 = (f32[768]{0:T(1024)S(1)}, f32[768]{0:T(1024)}, u32[]{:S(2)}) copy-start(f32[768]{0:T(1024)} %param.28) | copy-start | bytes 9220
  34.9 15.7 %slice-start.3 = ((s8[4718592]{0:T(1024)(128)(4,1)}), s8[524288]{0:T(1024)(128)(4,1)S(1)}, s32[]{:S(2)}) async-start(s8[4718592]{0:T(1024)(128)(4,1)} %bitcast.9), calls=%async_computation.4 | async-start | bytes 1048576
  35.0 8.4 %collective-permute-start.5 = (bf16[2,32,768]{2,1,0:T(8,128)(2,1)S(1)}, bf16[2,32,768]{2,1,0:T(8,128)(2,1)S(1)}, u32[]{:S(2)}, u32[]{:S(2)}) collective-permute-start(bf16[2,32,768]{2,1,0:T(8,128)(2,1)S(1)} %get-tuple-element.56), channel_id=1, source_target_pairs={{0,28},{4,24},{8,20},{12,16},{16,12},{20,8},{24,4},{28,0},{1,29},{... | collective-permute-start | bytes 294920 | tf_op jit(solution)/shard_map/ppermute | solution.py:360
  41.5 9.1 %collective-permute-start.7 = (bf16[2,32,768]{2,1,0:T(8,128)(2,1)S(1)}, bf16[2,32,768]{2,1,0:T(8,128)(2,1)S(1)}, u32[]{:S(2)}, u32[]{:S(2)}) collective-permute-start(bf16[2,32,768]{2,1,0:T(8,128)(2,1)S(1)} %get-tuple-element.61), channel_id=1, source_target_pairs={{0,16},{4,20},{8,24},{12,28},{16,0},{20,4},{24,8},{28,12},{1,17},{... | collective-permute-start | bytes 294920 | tf_op jit(solution)/shard_map/ppermute | solution.py:360
  41.6 9.1 %collective-permute-start.8 = (bf16[2,32,768]{2,1,0:T(8,128)(2,1)S(1)}, bf16[2,32,768]{2,1,0:T(8,128)(2,1)S(1)}, u32[]{:S(2)}, u32[]{:S(2)}) collective-permute-start(bf16[2,32,768]{2,1,0:T(8,128)(2,1)S(1)} %get-tuple-element.62), channel_id=1, source_target_pairs={{0,12},{4,8},{8,4},{12,0},{16,28},{20,24},{24,20},{28,16},{1,13},{... | collective-permute-start | bytes 294920 | tf_op jit(solution)/shard_map/ppermute | solution.py:360
  43.4 7.3 %slice-start = ((s8[4718592]{0:T(1024)(128)(4,1)}), s8[4194304]{0:T(1024)(128)(4,1)S(1)}, s32[]{:S(2)}) async-start(s8[4718592]{0:T(1024)(128)(4,1)} %bitcast.7), calls=%async_computation.1 | async-start | bytes 8388608
  43.4 7.3 %slice-start.1 = ((s8[4718592]{0:T(1024)(128)(4,1)}), s8[524288]{0:T(1024)(128)(4,1)S(1)}, s32[]{:S(2)}) async-start(s8[4718592]{0:T(1024)(128)(4,1)} %bitcast.7), calls=%async_computation.2 | async-start | bytes 1048576
  45.8 7.9 %collective-permute-start.10 = (bf16[2,32,768]{2,1,0:T(8,128)(2,1)S(1)}, bf16[2,32,768]{2,1,0:T(8,128)(2,1)S(1)}, u32[]{:S(2)}, u32[]{:S(2)}) collective-permute-start(bf16[2,32,768]{2,1,0:T(8,128)(2,1)S(1)} %get-tuple-element.72), channel_id=1, source_target_pairs={{0,20},{4,16},{8,28},{12,24},{16,4},{20,0},{24,12},{28,8},{1,21},{... | collective-permute-start | bytes 294920 | tf_op jit(solution)/shard_map/ppermute | solution.py:360
  48.6 5.5 %copy-start.5 = (bf16[768,2]{0,1:T(2,128)(2,1)S(1)}, bf16[768,2]{0,1:T(2,128)(2,1)}, u32[]{:S(2)}) copy-start(bf16[768,2]{0,1:T(2,128)(2,1)} %param.29) | copy-start | bytes 9220
  48.7 5.5 %copy-start.6 = (s32[16]{0:T(128)S(1)}, s32[16]{0:T(128)}, u32[]{:S(2)}) copy-start(s32[16]{0:T(128)} %get-tuple-element.39.place) | copy-start | bytes 196
  48.7 5.5 %collective-permute-start.11 = (bf16[2,32,768]{2,1,0:T(8,128)(2,1)S(1)}, bf16[2,32,768]{2,1,0:T(8,128)(2,1)S(1)}, u32[]{:S(2)}, u32[]{:S(2)}) collective-permute-start(bf16[2,32,768]{2,1,0:T(8,128)(2,1)S(1)} %get-tuple-element.73), channel_id=1, source_target_pairs={{0,8},{4,12},{8,0},{12,4},{16,24},{20,28},{24,16},{28,20},{1,9},{5... | collective-permute-start | bytes 294920 | tf_op jit(solution)/shard_map/ppermute | solution.py:360
